TPU v7x, 128 devices: a whole 4x4x4 slice. The times are simulated.
128 devices in a mesh: patch: 8 (over y, core), bulk: 16 (over z, x).
Axes of the slice: x: 4, y: 4, z: 4, core: 2. Of those that a mesh axis runs over, the one named last changes fastest.
Arguments:
- positions: float32 [3, 2097152], P(None, ('patch', 'bulk')), may hold values from -4 to 4
- masses: float32 [2097152], P(('patch', 'bulk')), may hold values from 0.004 to 0.04
- smoothing: float32 [2097152], P(('patch', 'bulk')), may hold values from 0.8 to 1.6
- energy: float32 [2097152], P(('patch', 'bulk')), may hold values from 0.3 to 3
- level_ids: int32 [16384], P(('patch', 'bulk')), may hold values from 0 to 2
- send_list: int32 [128, 20, 8], P(('patch', 'bulk')), may hold values from 0 to 127
- pair_list: int32 [128, 2, 672], P(('patch', 'bulk')), may hold values from 0 to 287, as said below
- pair_count: int32 [128], P(('patch', 'bulk')), may hold values from 416 to 672, as said below
Outputs:
- density: float32 [2097152], P(('patch', 'bulk'))
- accel: float32 [3, 2097152], P(None, ('patch', 'bulk'))
Inputs may be any that keep to these rules, and one draw needn't show every extreme that they name: `send_list`: each entry names one of the sending device's own blocks. `pair_list`: row 0 names own blocks, row 1 names blocks of the extended set, never the pair's own block a itself by the same index; the first 160 pairs of each device join extended block 128 + k, for k in order, with some own block. `pair_count`: some device has all slots live.
All inputs are finite; a program needn't handle non-finite values.
Results may differ from a plain program's by a relative error of at most 0.0003.
Values sent between devices are 32-bit elements; how exact they have to be, the bound alone decides.
A program may use at most 64 MiB of HBM per device.

v0:
```python
import math

import jax
import jax.numpy as jnp
from jax import lax
from jax.sharding import PartitionSpec as P

NORM = 21.0 / (2.0 * math.pi)
GAMMA_LESS = 2.0 / 3.0
SHRINK = 0.8


def from_behind(block, axis, distance):
    devices = range(lax.axis_size(axis))
    route = [((i - distance) % len(devices), i) for i in devices]
    return lax.ppermute(block, axis, route)


def neighbour_steps():
    return [
        (step_patch, step_bulk)
        for step_patch in (-1, 0, 1)
        for step_bulk in range(-3, 4)
        if (step_patch, step_bulk) != (0, 0)
    ]


def kernel_terms(xa, xb, ha, hb):
    dx = xa[:, :, None] - xb[:, None, :]
    dist = jnp.sqrt(jnp.sum(dx * dx, axis=0))
    hij = 0.5 * (ha[:, None] + hb[None, :])
    qval = dist / hij
    tail = jnp.maximum(1.0 - qval, 0.0)
    inverse = 1.0 / hij
    weight = NORM * inverse**3 * tail**4 * (1.0 + 4.0 * qval)
    slope = -20.0 * NORM * inverse**5 * tail**3
    return (dx, weight, slope)


def density_pair(rec_a, rec_b):
    dx, weight, slope = kernel_terms(rec_a[0:3], rec_b[0:3], rec_a[4], rec_b[4])
    return (
        jnp.sum(weight * rec_b[3][None, :], axis=1),
        jnp.sum(weight * rec_a[3][:, None], axis=0),
    )


def force_pair(rec_a, rec_b, press_a, press_b):
    dx, weight, slope = kernel_terms(rec_a[0:3], rec_b[0:3], rec_a[4], rec_b[4])
    coef = slope * (press_a[:, None] + press_b[None, :])
    to_a = -jnp.sum((coef * rec_b[3][None, :])[None] * dx, axis=2)
    to_b = jnp.sum((coef * rec_a[3][:, None])[None] * dx, axis=1)
    return (to_a, to_b)


def self_density(rec):
    return density_pair(rec, rec)[0]


def self_force(rec, press):
    return force_pair(rec, rec, press, press)[0]


def per_device(positions, masses, smoothing, energy, level_ids, send_list, pair_list, pair_count):
    nblocks = level_ids.shape[0]
    width = masses.shape[0] // nblocks
    smooth = smoothing.reshape(nblocks, width) * SHRINK ** level_ids.astype(jnp.float32)[:, None]
    record = jnp.concatenate(
        [
            positions.reshape(3, nblocks, width),
            masses.reshape(1, nblocks, width),
            smooth[None],
            energy.reshape(1, nblocks, width),
        ],
        0,
    )
    targets = send_list[0]
    peers, slots = targets.shape
    ghosts = peers * slots
    ext_count = nblocks + ghosts
    flat_targets = targets.reshape(ghosts)
    columns = lax.axis_size("bulk")
    steps = neighbour_steps()
    offsets = [pair_step[0] * columns + pair_step[1] for pair_step in steps]
    payloads = [record[:, targets[which]] for which in range(peers)]
    arrived = jnp.concatenate(
        [from_behind(payloads[which], ("patch", "bulk"), offsets[which]) for which in range(peers)],
        1,
    )
    extended = jnp.concatenate([record, arrived], 1)
    first = pair_list[0, 0]
    second = pair_list[0, 1]
    npair = first.shape[0]
    live = (jnp.arange(npair, dtype=jnp.int32) < pair_count[0]).astype(jnp.float32)
    group_size = math.gcd(npair, 32)
    groups = npair // group_size
    first_groups = first.reshape(groups, group_size)
    second_groups = second.reshape(groups, group_size)

    def dens_group(indices):
        rows_a = jnp.moveaxis(extended[:, indices[0]], 1, 0)
        rows_b = jnp.moveaxis(extended[:, indices[1]], 1, 0)
        return jax.vmap(density_pair)(rows_a, rows_b)

    to_a, to_b = lax.map(dens_group, (first_groups, second_groups))
    to_a = to_a.reshape(npair, width)
    to_b = to_b.reshape(npair, width)
    dens_ext = jax.ops.segment_sum(to_a * live[:, None], first, ext_count) + jax.ops.segment_sum(
        to_b * live[:, None], second, ext_count
    )
    own_dens = jax.vmap(self_density)(jnp.moveaxis(record, 1, 0))
    ghost_parts = dens_ext[nblocks:].reshape(peers, slots, width)
    returned = jnp.stack(
        [
            from_behind(ghost_parts[which], ("patch", "bulk"), -offsets[which])
            for which in range(peers)
        ],
        0,
    )
    density = (
        own_dens
        + dens_ext[:nblocks]
        + jax.ops.segment_sum(returned.reshape(ghosts, width), flat_targets, nblocks)
    )
    press = GAMMA_LESS * energy.reshape(nblocks, width) / density
    fuller = jnp.concatenate([record, density[None]], 0)
    again = jnp.concatenate(
        [
            from_behind(fuller[:, targets[which]], ("patch", "bulk"), offsets[which])
            for which in range(peers)
        ],
        1,
    )
    second_ext = jnp.concatenate([record, again[:6]], 1)
    ext_dens = jnp.concatenate([density, again[6]], 0)
    ghost_press = GAMMA_LESS * second_ext[5, nblocks:] / ext_dens[nblocks:]
    ext_press = jnp.concatenate([press, ghost_press], 0)

    def force_group(indices):
        rows_a = jnp.moveaxis(second_ext[:, indices[0]], 1, 0)
        rows_b = jnp.moveaxis(second_ext[:, indices[1]], 1, 0)
        return jax.vmap(force_pair)(rows_a, rows_b, ext_press[indices[0]], ext_press[indices[1]])

    acc_a, acc_b = lax.map(force_group, (first_groups, second_groups))
    acc_a = acc_a.reshape(npair, 3, width)
    acc_b = acc_b.reshape(npair, 3, width)
    acc_ext = jax.ops.segment_sum(
        acc_a * live[:, None, None], first, ext_count
    ) + jax.ops.segment_sum(acc_b * live[:, None, None], second, ext_count)
    own_acc = jax.vmap(self_force)(jnp.moveaxis(record, 1, 0), press)
    ghost_accs = acc_ext[nblocks:].reshape(peers, slots, 3, width)
    returned_acc = jnp.stack(
        [
            from_behind(ghost_accs[which], ("patch", "bulk"), -offsets[which])
            for which in range(peers)
        ],
        0,
    )
    accel = (
        own_acc
        + acc_ext[:nblocks]
        + jax.ops.segment_sum(returned_acc.reshape(ghosts, 3, width), flat_targets, nblocks)
    )
    return (density.reshape(nblocks * width), jnp.moveaxis(accel, 1, 0).reshape(3, nblocks * width))


def solution(mesh):
    placed = (
        P(None, ("patch", "bulk")),
        P(("patch", "bulk")),
        P(("patch", "bulk")),
        P(("patch", "bulk")),
        P(("patch", "bulk")),
        P(("patch", "bulk"), None, None),
        P(("patch", "bulk"), None, None),
        P(("patch", "bulk")),
    )
    return jax.shard_map(
        per_device,
        mesh=mesh,
        in_specs=placed,
        out_specs=(P(("patch", "bulk")), P(None, ("patch", "bulk"))),
        check_vma=False,
    )
```

profile of v0, /device:TPU:1, one launch (start us, length us, event | category | flops | bytes accessed | tf_op | source)
XLA Modules:
  0.0 940.7 jit_solution(7125472671325626181)
XLA Ops:
  7.6 8.0 collective-permute-start
  18.5 7.2 collective-permute-start.1
  31.6 11.5 %fusion.16 = f32[128,128,128]{2,1,0:T(8,128)} fusion(f32[128,3,128]{2,1,0:T(4,128)S(1)} %slice.551), kind=kLoop, calls=%fused_computation.96 | loop fusion | flops 16777216 | bytes 8585216 | tf_op jit(solution)/shard_map/vmap()/reduce_sum | solution.py:30
  47.3 10.5 %fusion.27 = f32[128,128]{1,0:T(8,128)} fusion(f32[128,128]{1,0:T(8,128)S(1)} %bitcast.333, f32[128,128]{1,0:T(8,128)S(1)} %bitcast.318, f32[128,128,128]{2,1,0:T(8,128)} %fusion.16), kind=kLoop, calls=%fused_computation.111 | loop fusion | flops 35635200 | bytes 8585216 | tf_op jit(solution)/shard_map/vmap()/reduce_sum | solution.py:43
  88.2 3.7 collective-permute-start.8
  95.6 4.1 collective-permute-start.13
  110.9 6.5 collective-permute-done.17
  118.8 166.1 %while.24 = (s32[]{:T(128)}, f32[21,32,128]{2,1,0:T(8,128)}, f32[21,32,128]{2,1,0:T(8,128)}, s32[21,32]{1,0:T(8,128)}, f32[6,288,128]{2,0,1:T(8,128)S(1)}, /*index=5*/s32[21,32]{1,0:T(8,128)}, s32[]{:T(128)}) while((s32[]{:T(128)}, f32[21,32,128]{2,1,0:T(8,128)}, f32[21,32,128]{2,1,0:T(8,128)}, s32[21,32]{1,0:T(8,128)}, ...), condition=%wide.region_6.7_spmd, body=%wide.region_2.6_spmd.sunk | while | flops 14149826 | bytes 5186657 | solution.py:105
  286.2 6.1 scatter_custom_fusion.1
  292.3 6.1 scatter_custom_fusion
  298.5 5.7 collective-permute-start.39
  304.7 3.9 collective-permute-start.37
  311.0 6.1 collective-permute-done.21
  317.6 7.4 collective-permute-done.22
  334.9 4.3 collective-permute-start.26
  342.0 7.2 collective-permute-done.27
  357.0 5.2 collective-permute-done.29
  369.0 4.0 collective-permute-start.32
  373.8 12.9 %collective-permute-start.33 = (f32[8,128]{1,0:T(8,128)S(1)}, f32[8,128]{1,0:T(8,128)S(1)}, u32[]{:S(2)}, u32[]{:S(2)}) collective-permute-start(f32[8,128]{1,0:T(8,128)S(1)} %get-tuple-element.172), channel_id=1, source_target_pairs={{13,0},{14,1},{15,2},{16,3},{17,4},{18,5},{19,6},{20,7},{21,8},{22... | collective-permute-start | bytes 12296 | tf_op jit(solution)/shard_map/ppermute | solution.py:16
  387.4 11.7 %collective-permute-start.34 = (f32[8,128]{1,0:T(8,128)S(1)}, f32[8,128]{1,0:T(8,128)S(1)}, u32[]{:S(2)}, u32[]{:S(2)}) collective-permute-start(f32[8,128]{1,0:T(8,128)S(1)} %get-tuple-element.171), channel_id=1, source_target_pairs={{14,0},{15,1},{16,2},{17,3},{18,4},{19,5},{20,6},{21,7},{22,8},{23... | collective-permute-start | bytes 12296 | tf_op jit(solution)/shard_map/ppermute | solution.py:16
  401.6 4.2 collective-permute-done.35
  407.5 11.8 %fusion.22 = f32[128,128,128]{2,1,0:T(8,128)} fusion(f32[128,128]{1,0:T(8,128)S(1)} %bitcast_divide_fusion, f32[128,128]{1,0:T(8,128)S(1)} %bitcast.334, f32[128,128]{1,0:T(8,128)S(1)} %bitcast.319, f32[128,128,128]{2,1,0:T(8,128)} %fusion.16), kind=kLoop, calls=%fused_computation.106 | loop fusion | flops 33554432 | bytes 16973824 | tf_op jit(solution)/shard_map/vmap()/mul | solution.py:51
  420.6 4.2 collective-permute-start.40
  424.8 16.7 %fusion.17 = f32[128,3,128]{2,1,0:T(4,128)} fusion(f32[128,128,128]{2,1,0:T(8,128)} %fusion.22, f32[128,3,128]{2,1,0:T(4,128)S(1)} %slice.551), kind=kLoop, calls=%fused_computation.97 | loop fusion | flops 18825216 | bytes 8781824 | tf_op jit(solution)/shard_map/vmap()/reduce_sum | solution.py:51
  456.3 4.5 collective-permute-start.42
  461.0 4.4 collective-permute-start.46
  468.2 4.5 collective-permute-start.49
  475.1 4.8 collective-permute-start.53
  497.4 272.5 %while.25 = (s32[]{:T(128)}, f32[21,32,3,128]{3,2,1,0:T(4,128)S(1)}, f32[21,32,3,128]{3,2,1,0:T(4,128)}, s32[21,32]{1,0:T(8,128)}, f32[6,288,128]{2,0,1:T(8,128)...) while((s32[]{:T(128)}, f32[21,32,3,128]{3,2,1,0:T(4,128)S(1)}, ...), condition=%wide.region_15.16_spmd, body=%wide.region_11.15_spmd.sunk | while | flops 20961472 | bytes 18228584 | solution.py:144
  505.8 3.9 fusion.84
  518.8 3.9 fusion.84
  531.7 3.9 fusion.84
  544.7 3.9 fusion.84
  557.7 3.9 fusion.84
  570.7 3.9 fusion.84
  583.6 3.9 fusion.84
  596.6 3.9 fusion.84
  609.6 3.9 fusion.84
  622.6 3.9 fusion.84
  635.5 3.9 fusion.84
  648.5 3.9 fusion.84
  661.5 3.9 fusion.84
  674.5 3.9 fusion.84
  687.4 3.9 fusion.84
  700.4 3.9 fusion.84
  713.4 3.9 fusion.84
  726.4 3.9 fusion.84
  739.4 3.9 fusion.84
  752.3 3.9 fusion.84
  765.3 3.9 fusion.84
  774.3 24.6 %scatter_fusion = f32[288,3,128]{2,1,0:T(4,128)S(1)} fusion(f32[288,3,128]{2,1,0:T(4,128)S(1)} %broadcast.558.clone, s32[672]{0:T(1024)S(1)} %copy-done.10, f32[672,3,128]{2,1,0:T(4,128)S(1)} %get-tuple-element.186), kind=kCustom, calls=%fused_computation.49 | custom fusion | flops 258048 | bytes 3099264 | tf_op jit(solution)/shard_map/scatter-add | solution.py:147
  799.0 24.5 %scatter_fusion.1 = f32[288,3,128]{2,1,0:T(4,128)S(1)} fusion(f32[288,3,128]{2,1,0:T(4,128)S(1)} %broadcast.558.clone.1, s32[672]{0:T(1024)S(1)} %copy-done.9, f32[672,3,128]{2,1,0:T(4,128)S(1)} %get-tuple-element.185), kind=kCustom, calls=%fused_computation.50 | custom fusion | flops 258048 | bytes 3099264 | tf_op jit(solution)/shard_map/scatter-add | solution.py:149
  824.4 5.2 collective-permute-start.79
  837.0 5.6 collective-permute-done.61
  845.4 5.3 collective-permute-done.62
  857.0 4.7 collective-permute-done.65
  861.7 4.3 collective-permute-start.66
  868.1 8.2 collective-permute-done.67
  884.2 5.4 collective-permute-done.69
  896.5 4.0 collective-permute-start.72
  901.3 12.9 %collective-permute-start.73 = (f32[8,3,128]{2,1,0:T(4,128)S(1)}, f32[8,3,128]{2,1,0:T(4,128)S(1)}, u32[]{:S(2)}, u32[]{:S(2)}) collective-permute-start(f32[8,3,128]{2,1,0:T(4,128)S(1)} %get-tuple-element.148), channel_id=1, source_target_pairs={{13,0},{14,1},{15,2},{16,3},{17,4},{18,5},{19,6},{20,7},{21,8},{22... | collective-permute-start | bytes 36872 | tf_op jit(solution)/shard_map/ppermute | solution.py:16
  915.1 11.7 %collective-permute-start.74 = (f32[8,3,128]{2,1,0:T(4,128)S(1)}, f32[8,3,128]{2,1,0:T(4,128)S(1)}, u32[]{:S(2)}, u32[]{:S(2)}) collective-permute-start(f32[8,3,128]{2,1,0:T(4,128)S(1)} %get-tuple-element.147), channel_id=1, source_target_pairs={{14,0},{15,1},{16,2},{17,3},{18,4},{19,5},{20,6},{21,7},{22,8},{23... | collective-permute-start | bytes 36872 | tf_op jit(solution)/shard_map/ppermute | solution.py:16
  929.3 4.3 collective-permute-done.75
  933.7 6.0 scatter_fusion.2
  (958 shorter events, 538.7 us)
Async XLA Ops:
  7.6 72.9 %collective-permute-start = (f32[6,8,128]{2,0,1:T(8,128)}, f32[6,8,128]{2,0,1:T(8,128)}, u32[]{:S(2)}, u32[]{:S(2)}) collective-permute-start(f32[6,8,128]{2,0,1:T(8,128)} %bitcast.28), channel_id=1, source_target_pairs={{19,0},{20,1},{21,2},{22,3},{23,4},{24,5},{25,6},{26,7},{27,8},{28... | collective-permute-start | bytes 73736 | tf_op jit(solution)/shard_map/ppermute | solution.py:16
  17.3 100.7 %collective-permute-start.19 = (f32[6,8,128]{2,0,1:T(8,128)}, f32[6,8,128]{2,0,1:T(8,128)}, u32[]{:S(2)}, u32[]{:S(2)}) collective-permute-start(f32[6,8,128]{2,0,1:T(8,128)} %bitcast.66), channel_id=1, source_target_pairs={{109,0},{110,1},{111,2},{112,3},{113,4},{114,5},{115,6},{116,7},{1... | collective-permute-start | bytes 73736 | tf_op jit(solution)/shard_map/ppermute | solution.py:16
  18.5 63.2 %collective-permute-start.1 = (f32[6,8,128]{2,0,1:T(8,128)}, f32[6,8,128]{2,0,1:T(8,128)}, u32[]{:S(2)}, u32[]{:S(2)}) collective-permute-start(f32[6,8,128]{2,0,1:T(8,128)} %bitcast.30), channel_id=1, source_target_pairs={{18,0},{19,1},{20,2},{21,3},{22,4},{23,5},{24,6},{25,7},{26,8},{27... | collective-permute-start | bytes 73736 | tf_op jit(solution)/shard_map/ppermute | solution.py:16
  26.9 56.2 %collective-permute-start.2 = (f32[6,8,128]{2,0,1:T(8,128)}, f32[6,8,128]{2,0,1:T(8,128)}, u32[]{:S(2)}, u32[]{:S(2)}) collective-permute-start(f32[6,8,128]{2,0,1:T(8,128)} %bitcast.32), channel_id=1, source_target_pairs={{17,0},{18,1},{19,2},{20,3},{21,4},{22,5},{23,6},{24,7},{25,8},{26... | collective-permute-start | bytes 73736 | tf_op jit(solution)/shard_map/ppermute | solution.py:16
  30.0 53.8 %collective-permute-start.3 = (f32[6,8,128]{2,0,1:T(8,128)}, f32[6,8,128]{2,0,1:T(8,128)}, u32[]{:S(2)}, u32[]{:S(2)}) collective-permute-start(f32[6,8,128]{2,0,1:T(8,128)} %bitcast.34), channel_id=1, source_target_pairs={{16,0},{17,1},{18,2},{19,3},{20,4},{21,5},{22,6},{23,7},{24,8},{25... | collective-permute-start | bytes 73736 | tf_op jit(solution)/shard_map/ppermute | solution.py:16
  80.5 7.7 collective-permute-start.4
  81.7 10.2 %collective-permute-start.5 = (f32[6,8,128]{2,0,1:T(8,128)}, f32[6,8,128]{2,0,1:T(8,128)S(1)}, u32[]{:S(2)}, u32[]{:S(2)}) collective-permute-start(f32[6,8,128]{2,0,1:T(8,128)} %bitcast.376), channel_id=1, source_target_pairs={{14,0},{15,1},{16,2},{17,3},{18,4},{19,5},{20,6},{21,7},{22,8},{23... | collective-permute-start | bytes 73736 | tf_op jit(solution)/shard_map/ppermute | solution.py:16
  83.1 11.2 %collective-permute-start.6 = (f32[6,8,128]{2,0,1:T(8,128)}, f32[6,8,128]{2,0,1:T(8,128)S(1)}, u32[]{:S(2)}, u32[]{:S(2)}) collective-permute-start(f32[6,8,128]{2,0,1:T(8,128)} %bitcast.375), channel_id=1, source_target_pairs={{13,0},{14,1},{15,2},{16,3},{17,4},{18,5},{19,6},{20,7},{21,8},{22... | collective-permute-start | bytes 73736 | tf_op jit(solution)/shard_map/ppermute | solution.py:16
  83.8 10.4 %collective-permute-start.7 = (f32[6,8,128]{2,0,1:T(8,128)}, f32[6,8,128]{2,0,1:T(8,128)S(1)}, u32[]{:S(2)}, u32[]{:S(2)}) collective-permute-start(f32[6,8,128]{2,0,1:T(8,128)} %bitcast.374), channel_id=1, source_target_pairs={{3,0},{4,1},{5,2},{6,3},{7,4},{8,5},{9,6},{10,7},{11,8},{12,9},{13... | collective-permute-start | bytes 73736 | tf_op jit(solution)/shard_map/ppermute | solution.py:16
  88.2 6.2 collective-permute-start.8
  94.2 7.9 collective-permute-start.10
  94.3 9.1 collective-permute-start.11
  94.4 12.1 %collective-permute-start.12 = (f32[6,8,128]{2,0,1:T(8,128)}, f32[6,8,128]{2,0,1:T(8,128)S(1)}, u32[]{:S(2)}, u32[]{:S(2)}) collective-permute-start(f32[6,8,128]{2,0,1:T(8,128)} %bitcast.369), channel_id=1, source_target_pairs={{125,0},{126,1},{127,2},{0,3},{1,4},{2,5},{3,6},{4,7},{5,8},{6,9},... | collective-permute-start | bytes 73736 | tf_op jit(solution)/shard_map/ppermute | solution.py:16
  95.6 13.5 %collective-permute-start.13 = (f32[6,8,128]{2,0,1:T(8,128)}, f32[6,8,128]{2,0,1:T(8,128)S(1)}, u32[]{:S(2)}, u32[]{:S(2)}) collective-permute-start(f32[6,8,128]{2,0,1:T(8,128)} %bitcast.368), channel_id=1, source_target_pairs={{115,0},{116,1},{117,2},{118,3},{119,4},{120,5},{121,6},{122,7},{1... | collective-permute-start | bytes 73736 | tf_op jit(solution)/shard_map/ppermute | solution.py:16
  102.1 7.0 collective-permute-start.14
  103.4 7.5 collective-permute-start.15
  109.0 8.4 collective-permute-start.17
  109.1 9.0 collective-permute-start.18
  298.4 10.2 %collective-permute-start.20 = (f32[8,128]{1,0:T(8,128)S(1)}, f32[8,128]{1,0:T(8,128)S(1)}, u32[]{:S(2)}, u32[]{:S(2)}) collective-permute-start(f32[8,128]{1,0:T(8,128)S(1)} %slice.554), channel_id=1, source_target_pairs={{109,0},{110,1},{111,2},{112,3},{113,4},{114,5},{115,6},{116,7},{1... | collective-permute-start | bytes 12296 | tf_op jit(solution)/shard_map/ppermute | solution.py:16
  298.5 107.3 %collective-permute-start.39 = (f32[8,128]{1,0:T(8,128)S(1)}, f32[8,128]{1,0:T(8,128)S(1)}, u32[]{:S(2)}, u32[]{:S(2)}) collective-permute-start(f32[8,128]{1,0:T(8,128)S(1)} %get-tuple-element.166), channel_id=1, source_target_pairs={{19,0},{20,1},{21,2},{22,3},{23,4},{24,5},{25,6},{26,7},{27,8},{28... | collective-permute-start | bytes 12296 | tf_op jit(solution)/shard_map/ppermute | solution.py:16
  304.2 101.6 %collective-permute-start.38 = (f32[8,128]{1,0:T(8,128)S(1)}, f32[8,128]{1,0:T(8,128)S(1)}, u32[]{:S(2)}, u32[]{:S(2)}) collective-permute-start(f32[8,128]{1,0:T(8,128)S(1)} %get-tuple-element.167), channel_id=1, source_target_pairs={{18,0},{19,1},{20,2},{21,3},{22,4},{23,5},{24,6},{25,7},{26,8},{27... | collective-permute-start | bytes 12296 | tf_op jit(solution)/shard_map/ppermute | solution.py:16
  304.7 101.1 %collective-permute-start.37 = (f32[8,128]{1,0:T(8,128)S(1)}, f32[8,128]{1,0:T(8,128)S(1)}, u32[]{:S(2)}, u32[]{:S(2)}) collective-permute-start(f32[8,128]{1,0:T(8,128)S(1)} %get-tuple-element.168), channel_id=1, source_target_pairs={{17,0},{18,1},{19,2},{20,3},{21,4},{22,5},{23,6},{24,7},{25,8},{26... | collective-permute-start | bytes 12296 | tf_op jit(solution)/shard_map/ppermute | solution.py:16
  308.6 97.1 %collective-permute-start.36 = (f32[8,128]{1,0:T(8,128)S(1)}, f32[8,128]{1,0:T(8,128)S(1)}, u32[]{:S(2)}, u32[]{:S(2)}) collective-permute-start(f32[8,128]{1,0:T(8,128)S(1)} %get-tuple-element.169), channel_id=1, source_target_pairs={{16,0},{17,1},{18,2},{19,3},{20,4},{21,5},{22,6},{23,7},{24,8},{25... | collective-permute-start | bytes 12296 | tf_op jit(solution)/shard_map/ppermute | solution.py:16
  308.6 8.5 collective-permute-start.21
  317.1 7.9 collective-permute-start.22
  340.0 9.2 collective-permute-start.27
  349.2 6.6 collective-permute-start.28
  355.9 6.4 collective-permute-start.29
  373.8 13.6 %collective-permute-start.33 = (f32[8,128]{1,0:T(8,128)S(1)}, f32[8,128]{1,0:T(8,128)S(1)}, u32[]{:S(2)}, u32[]{:S(2)}) collective-permute-start(f32[8,128]{1,0:T(8,128)S(1)} %get-tuple-element.172), channel_id=1, source_target_pairs={{13,0},{14,1},{15,2},{16,3},{17,4},{18,5},{19,6},{20,7},{21,8},{22... | collective-permute-start | bytes 12296 | tf_op jit(solution)/shard_map/ppermute | solution.py:16
  387.4 12.5 %collective-permute-start.34 = (f32[8,128]{1,0:T(8,128)S(1)}, f32[8,128]{1,0:T(8,128)S(1)}, u32[]{:S(2)}, u32[]{:S(2)}) collective-permute-start(f32[8,128]{1,0:T(8,128)S(1)} %get-tuple-element.171), channel_id=1, source_target_pairs={{14,0},{15,1},{16,2},{17,3},{18,4},{19,5},{20,6},{21,7},{22,8},{23... | collective-permute-start | bytes 12296 | tf_op jit(solution)/shard_map/ppermute | solution.py:16
  400.0 5.8 collective-permute-start.35
  420.6 40.3 %collective-permute-start.40 = (f32[7,8,128]{2,0,1:T(8,128)S(1)}, f32[7,8,128]{2,0,1:T(8,128)S(1)}, u32[]{:S(2)}, u32[]{:S(2)}) collective-permute-start(f32[7,8,128]{2,0,1:T(8,128)S(1)} %bitcast.359), channel_id=1, source_target_pairs={{19,0},{20,1},{21,2},{22,3},{23,4},{24,5},{25,6},{26,7},{27,8},{28... | collective-permute-start | bytes 86024 | tf_op jit(solution)/shard_map/ppermute | solution.py:16
  454.4 6.5 collective-permute-start.41
  456.3 9.1 collective-permute-start.42
  460.8 6.8 collective-permute-start.43
  460.8 7.3 collective-permute-start.44
  460.9 11.9 %collective-permute-start.45 = (f32[7,8,128]{2,0,1:T(8,128)S(1)}, f32[7,8,128]{2,0,1:T(8,128)S(1)}, u32[]{:S(2)}, u32[]{:S(2)}) collective-permute-start(f32[7,8,128]{2,0,1:T(8,128)S(1)} %bitcast.357), channel_id=1, source_target_pairs={{14,0},{15,1},{16,2},{17,3},{18,4},{19,5},{20,6},{21,7},{22,8},{23... | collective-permute-start | bytes 86024 | tf_op jit(solution)/shard_map/ppermute | solution.py:16
  461.0 12.3 %collective-permute-start.46 = (f32[7,8,128]{2,0,1:T(8,128)S(1)}, f32[7,8,128]{2,0,1:T(8,128)S(1)}, u32[]{:S(2)}, u32[]{:S(2)}) collective-permute-start(f32[7,8,128]{2,0,1:T(8,128)S(1)} %bitcast.356), channel_id=1, source_target_pairs={{13,0},{14,1},{15,2},{16,3},{17,4},{18,5},{19,6},{20,7},{21,8},{22... | collective-permute-start | bytes 86024 | tf_op jit(solution)/shard_map/ppermute | solution.py:16
  465.4 9.7 %collective-permute-start.47 = (f32[7,8,128]{2,0,1:T(8,128)S(1)}, f32[7,8,128]{2,0,1:T(8,128)S(1)}, u32[]{:S(2)}, u32[]{:S(2)}) collective-permute-start(f32[7,8,128]{2,0,1:T(8,128)S(1)} %bitcast.355), channel_id=1, source_target_pairs={{3,0},{4,1},{5,2},{6,3},{7,4},{8,5},{9,6},{10,7},{11,8},{12,9},{13... | collective-permute-start | bytes 86024 | tf_op jit(solution)/shard_map/ppermute | solution.py:16
  467.7 7.4 collective-permute-start.48
  468.2 11.7 %collective-permute-start.49 = (f32[7,8,128]{2,0,1:T(8,128)S(1)}, f32[7,8,128]{2,0,1:T(8,128)S(1)}, u32[]{:S(2)}, u32[]{:S(2)}) collective-permute-start(f32[7,8,128]{2,0,1:T(8,128)S(1)} %bitcast.353), channel_id=1, source_target_pairs={{1,0},{2,1},{3,2},{4,3},{5,4},{6,5},{7,6},{8,7},{9,8},{10,9},{11,1... | collective-permute-start | bytes 86024 | tf_op jit(solution)/shard_map/ppermute | solution.py:16
  472.7 10.3 %collective-permute-start.50 = (f32[7,8,128]{2,0,1:T(8,128)S(1)}, f32[7,8,128]{2,0,1:T(8,128)S(1)}, u32[]{:S(2)}, u32[]{:S(2)}) collective-permute-start(f32[7,8,128]{2,0,1:T(8,128)S(1)} %bitcast.352), channel_id=1, source_target_pairs={{127,0},{0,1},{1,2},{2,3},{3,4},{4,5},{5,6},{6,7},{7,8},{8,9},{9,1... | collective-permute-start | bytes 86024 | tf_op jit(solution)/shard_map/ppermute | solution.py:16
  473.3 10.5 %collective-permute-start.51 = (f32[7,8,128]{2,0,1:T(8,128)S(1)}, f32[7,8,128]{2,0,1:T(8,128)S(1)}, u32[]{:S(2)}, u32[]{:S(2)}) collective-permute-start(f32[7,8,128]{2,0,1:T(8,128)S(1)} %bitcast.351), channel_id=1, source_target_pairs={{126,0},{127,1},{0,2},{1,3},{2,4},{3,5},{4,6},{5,7},{6,8},{7,9},{8... | collective-permute-start | bytes 86024 | tf_op jit(solution)/shard_map/ppermute | solution.py:16
  475.1 11.3 %collective-permute-start.52 = (f32[7,8,128]{2,0,1:T(8,128)S(1)}, f32[7,8,128]{2,0,1:T(8,128)S(1)}, u32[]{:S(2)}, u32[]{:S(2)}) collective-permute-start(f32[7,8,128]{2,0,1:T(8,128)S(1)} %bitcast.350), channel_id=1, source_target_pairs={{125,0},{126,1},{127,2},{0,3},{1,4},{2,5},{3,6},{4,7},{5,8},{6,9},... | collective-permute-start | bytes 86024 | tf_op jit(solution)/shard_map/ppermute | solution.py:16
  475.1 11.3 %collective-permute-start.53 = (f32[7,8,128]{2,0,1:T(8,128)S(1)}, f32[7,8,128]{2,0,1:T(8,128)S(1)}, u32[]{:S(2)}, u32[]{:S(2)}) collective-permute-start(f32[7,8,128]{2,0,1:T(8,128)S(1)} %bitcast.349), channel_id=1, source_target_pairs={{115,0},{116,1},{117,2},{118,3},{119,4},{120,5},{121,6},{122,7},{1... | collective-permute-start | bytes 86024 | tf_op jit(solution)/shard_map/ppermute | solution.py:16
  479.9 9.4 collective-permute-start.54
  483.0 8.5 collective-permute-start.55
  483.8 7.7 collective-permute-start.56
  486.4 8.2 collective-permute-start.57
  486.4 9.1 collective-permute-start.58
  489.3 7.6 collective-permute-start.59
  823.8 10.5 %collective-permute-start.60 = (f32[8,3,128]{2,1,0:T(4,128)S(1)}, f32[8,3,128]{2,1,0:T(4,128)S(1)}, u32[]{:S(2)}, u32[]{:S(2)}) collective-permute-start(f32[8,3,128]{2,1,0:T(4,128)S(1)} %slice.578), channel_id=1, source_target_pairs={{109,0},{110,1},{111,2},{112,3},{113,4},{114,5},{115,6},{116,7},{1... | collective-permute-start | bytes 36872 | tf_op jit(solution)/shard_map/ppermute | solution.py:16
  824.4 109.3 %collective-permute-start.79 = (f32[8,3,128]{2,1,0:T(4,128)S(1)}, f32[8,3,128]{2,1,0:T(4,128)S(1)}, u32[]{:S(2)}, u32[]{:S(2)}) collective-permute-start(f32[8,3,128]{2,1,0:T(4,128)S(1)} %get-tuple-element.142), channel_id=1, source_target_pairs={{19,0},{20,1},{21,2},{22,3},{23,4},{24,5},{25,6},{26,7},{27,8},{28... | collective-permute-start | bytes 36872 | tf_op jit(solution)/shard_map/ppermute | solution.py:16
  829.7 104.0 %collective-permute-start.78 = (f32[8,3,128]{2,1,0:T(4,128)S(1)}, f32[8,3,128]{2,1,0:T(4,128)S(1)}, u32[]{:S(2)}, u32[]{:S(2)}) collective-permute-start(f32[8,3,128]{2,1,0:T(4,128)S(1)} %get-tuple-element.143), channel_id=1, source_target_pairs={{18,0},{19,1},{20,2},{21,3},{22,4},{23,5},{24,6},{25,7},{26,8},{27... | collective-permute-start | bytes 36872 | tf_op jit(solution)/shard_map/ppermute | solution.py:16
  832.2 101.5 %collective-permute-start.77 = (f32[8,3,128]{2,1,0:T(4,128)S(1)}, f32[8,3,128]{2,1,0:T(4,128)S(1)}, u32[]{:S(2)}, u32[]{:S(2)}) collective-permute-start(f32[8,3,128]{2,1,0:T(4,128)S(1)} %get-tuple-element.144), channel_id=1, source_target_pairs={{17,0},{18,1},{19,2},{20,3},{21,4},{22,5},{23,6},{24,7},{25,8},{26... | collective-permute-start | bytes 36872 | tf_op jit(solution)/shard_map/ppermute | solution.py:16
  832.7 100.9 %collective-permute-start.76 = (f32[8,3,128]{2,1,0:T(4,128)S(1)}, f32[8,3,128]{2,1,0:T(4,128)S(1)}, u32[]{:S(2)}, u32[]{:S(2)}) collective-permute-start(f32[8,3,128]{2,1,0:T(4,128)S(1)} %get-tuple-element.145), channel_id=1, source_target_pairs={{16,0},{17,1},{18,2},{19,3},{20,4},{21,5},{22,6},{23,7},{24,8},{25... | collective-permute-start | bytes 36872 | tf_op jit(solution)/shard_map/ppermute | solution.py:16
  834.3 8.3 collective-permute-start.61
  842.6 8.0 collective-permute-start.62
  866.9 9.4 collective-permute-start.67
  876.3 6.8 collective-permute-start.68
  883.1 6.5 collective-permute-start.69
  901.3 13.8 %collective-permute-start.73 = (f32[8,3,128]{2,1,0:T(4,128)S(1)}, f32[8,3,128]{2,1,0:T(4,128)S(1)}, u32[]{:S(2)}, u32[]{:S(2)}) collective-permute-start(f32[8,3,128]{2,1,0:T(4,128)S(1)} %get-tuple-element.148), channel_id=1, source_target_pairs={{13,0},{14,1},{15,2},{16,3},{17,4},{18,5},{19,6},{20,7},{21,8},{22... | collective-permute-start | bytes 36872 | tf_op jit(solution)/shard_map/ppermute | solution.py:16
  915.1 12.6 %collective-permute-start.74 = (f32[8,3,128]{2,1,0:T(4,128)S(1)}, f32[8,3,128]{2,1,0:T(4,128)S(1)}, u32[]{:S(2)}, u32[]{:S(2)}) collective-permute-start(f32[8,3,128]{2,1,0:T(4,128)S(1)} %get-tuple-element.147), channel_id=1, source_target_pairs={{14,0},{15,1},{16,2},{17,3},{18,4},{19,5},{20,6},{21,7},{22,8},{23... | collective-permute-start | bytes 36872 | tf_op jit(solution)/shard_map/ppermute | solution.py:16
  927.7 5.9 collective-permute-start.75
  (34 other events, 828.7 us)
where the time goes:
time: 956 us; the launch traced here: 941 us
  other arithmetic  478 us (50%)
  starting transfers between devices  204 us (21%)
  local copies, waits for them, and re-layouts  142 us (15%)
  waiting for transfers between devices  111 us (12%)
    ppermute x80, starting transfers between devices, from_behind(): return lax.ppermute(block, axis, route)  204 us
    ppermute x80, waiting for transfers between devices, from_behind(): return lax.ppermute(block, axis, route)  111 us
    reduce_sum x43, other arithmetic, kernel_terms(): dist = jnp.sqrt(jnp.sum(dx * dx, axis=0))  98.1 us
    reduce_sum x21, other arithmetic, force_pair(): to_b = jnp.sum((coef * rec_a[3][:, None])[None] * dx, axis=1)  82.4 us
    reduce_sum x21, other arithmetic, density_pair(): jnp.sum(weight * rec_a[3][:, None], axis=0)  53 us
    mul x22, other arithmetic, force_pair(): to_a = -jnp.sum((coef * rec_b[3][None, :])[None] * dx, axis=2)  50.6 us
    gather x20, local copies, waits for them, and re-layouts, per_device(): payloads = [record[:, targets[which]] for which in range(peers)]  25.1 us
    scatter-add x1, other arithmetic, per_device(): jax.ops.segment_sum(acc_a * live[:, None, None], first, ext_count)  24.6 us
  transfers between devices with their start and end apart: 80, of which 37 were waited for; matrix products, arithmetic and copies ran while one was open for 9% of the time, Pallas kernels for 0%

commit v1 on v0

v1 whole, which is shorter than its diff:
```python
import functools
import math

import jax
import jax.numpy as jnp
from jax import lax
from jax.experimental import pallas as pl
from jax.experimental.pallas import tpu as pltpu
from jax.sharding import PartitionSpec as P

SHRINK = 0.8
NORM = 21.0 / (2.0 * math.pi)
bf16=jnp.bfloat16; f32=jnp.float32
CH8=[(0,0),(0,1),(1,0),(1,1),(0,2),(2,0),(1,2),(2,1)]
E=288

def split3(v):
    a=v.astype(bf16).astype(f32); r=v-a
    b=r.astype(bf16).astype(f32)
    return a,b,r-b
def hilo(v):
    hi=v.astype(bf16)
    return hi,(v-hi.astype(f32)).astype(bf16)

def tile_math(r2,hs):
    r2=jnp.maximum(r2,1e-30)
    s=pl.reciprocal(hs,approx=True)
    d=r2*lax.rsqrt(r2)
    q=d*s
    t=jnp.maximum(1.0-q,0.0)
    st=s*t
    c=st*st*st
    S=c*(s*s)
    W=c*(t*(q+0.25))
    return W,S

def k2(opt, G, U, pairs, count, own_ref, gh_ref, dens_ref, s_ref, C, CA, AF, BF, MM, GB, WB, acc):
    step=pl.program_id(0)
    NP=pairs.shape[1]; TOT=NP+128
    def ab(k):
        kk=jnp.maximum(k-128,0)
        a=jnp.where(k<128,k,pairs[0,kk]); b=jnp.where(k<128,k,pairs[1,kk])
        return a,b
    def targets(k):
        a,b=ab(k)
        live=k<128+count[0]
        return a,b,jnp.where(live,a,E),jnp.where(live&(k>=128),b,E)
    def first_stage(k,j):
        a,b=ab(k)
        GB[j]=jnp.dot(AF[a],BF[b],preferred_element_type=f32)
    def last_stage(k,j):
        a,b,ta,tb=targets(k)
        pa=lax.dot_general(MM[b],jnp.concatenate([WB[j,0],WB[j,1]],1),(((1,),(1,)),((),())),preferred_element_type=f32)
        pb=jnp.dot(MM[a],jnp.concatenate([WB[j,0],WB[j,1]],0),preferred_element_type=f32)
        if opt.get('only')=='a': return [(ta,pa)]
        if opt.get('only')=='b': return [(tb,pb)]
        if opt.get('only')=='m':
            return [(ta,jnp.dot(jnp.concatenate([WB[j,0],WB[j,1]],1),AF[b,:,:].reshape(128,64) if 0 else jnp.concatenate([MM[b,:,:128].astype(f32).T.astype(bf16)]*2,0),preferred_element_type=f32)[:16].reshape(16,16)),(tb,pb)]
        return [(ta,pa),(tb,pb)]
    def add(res):
        for i,r in res:
            acc[i]+=r[:8]+r[8:]
    @pl.when(step==0)
    def _():
        one=jnp.ones((E,128),f32); zero=jnp.zeros((E,128),f32)
        C[3*E:4*E]=one; C[10*E:11*E]=one
        for i in (5,6,7,8,11,12,17,18,19,20): C[i*E:(i+1)*E]=zero
        CA[4*128:5*128]=one[:128]
        for i in (6,7): CA[i*128:(i+1)*128]=zero[:128]
        x,y,z,m,h=[own_ref[c] for c in range(5)]
        n=x*x+y*y+z*z; hh=0.5*h
        for i,v in ((0,x),(1,y),(2,z),(4,n),(9,hh),(13,m),(14,m*x),(15,m*y),(16,m*z)):
            C[i*E:i*E+128]=v
        for i,v in ((0,-2*x),(1,-2*y),(2,-2*z),(3,n),(5,hh)):
            CA[i*128:(i+1)*128]=v
        for k in range(20):
            x,y,z,m,h=[gh_ref[k,c] for c in range(5)]
            n=x*x+y*y+z*z; hh=0.5*h
            for i,v in ((0,x),(1,y),(2,z),(4,n),(9,hh),(13,m),(14,m*x),(15,m*y),(16,m*z)):
                o=i*E+128+k*8
                C[o:o+8]=v
        acc[...]=jnp.zeros_like(acc)
        WB[...]=jnp.zeros_like(WB)
        def blk(i,_):
            for j in range(4):
                b=i*4+j
                for w,c in ((0,0),(5,128)):
                    p=split3(C[pl.ds(w*E+b,8,stride=E),:])
                    f=jnp.concatenate([p[q] for _,q in CH8],0).astype(bf16)
                    BF[b,:,c:c+128]=f
                mv=C[pl.ds(13*E+b,8,stride=E),:]
                hi=mv.astype(bf16).astype(f32)
                mm=jnp.concatenate([hi,mv-hi],0).astype(bf16)
                MM[b,:,:128]=mm; MM[b,:,128:]=mm
            return 0
        lax.fori_loop(0,E//4,blk,0)
        def blka(i,_):
            for j in range(4):
                b=i*4+j
                p=split3(CA[pl.ds(b,8,stride=128),:])
                f=jnp.concatenate([p[q] for q,_ in CH8],0)
                if opt.get('bt'):
                    AF[b]=f.astype(bf16).T
                else:
                    AF[b]=f.T.astype(bf16)
            return 0
        lax.fori_loop(0,32,blka,0)
        for j in range(U): first_stage(j,j)
    def body(u,_):
        k0=step*G+u*U
        res=[]
        for j in range(U):
            if not opt.get('no3'): res+=last_stage(jnp.maximum(k0-U+j,0),j)
        for j in range(U):
            for r in range(0,0 if opt.get('no2') else 128,opt.get('rows',32)):
                rows=opt.get('rows',32)
                W,S=tile_math(GB[j,r:r+rows,:128],GB[j,r:r+rows,128:])
                Shi,Slo=hilo(S)
                s_ref[u*U+j,r:r+rows]=Shi; s_ref[u*U+j,128+r:128+r+rows]=Slo
                Whi,Wlo=hilo(W)
                WB[j,0,r:r+rows]=Whi; WB[j,1,r:r+rows]=Wlo
            if not opt.get('no1'): first_stage(jnp.minimum(k0+U+j,TOT-1),j)
        add(res)
        return 0
    lax.fori_loop(0,0 if opt.get('no') else G//U,body,0)
    @pl.when(step==pl.num_programs(0)-1)
    def _():
        res=[]
        for j in range(U): res+=last_stage(TOT-U+j,j)
        add(res)
        for i in range(E//8):
            dens_ref[i*8:i*8+8]=acc[i*8:i*8+8,0,:]*(4*NORM)

def run_k2(pairs,count,own,gh,opt,G=16,U=2):
    NP=pairs.shape[1]
    n=(NP+128)//G
    return pl.pallas_call(functools.partial(k2,opt,G,U),
      grid_spec=pltpu.PrefetchScalarGridSpec(num_scalar_prefetch=2,grid=(n,),
        in_specs=[pl.BlockSpec(memory_space=pltpu.VMEM)]*2,
        out_specs=[pl.BlockSpec(memory_space=pltpu.VMEM),pl.BlockSpec((G,256,128),lambda i,*_:(0 if opt.get('nodma') else i,0,0))],
        scratch_shapes=[pltpu.VMEM((21*E,128),f32),pltpu.VMEM((8*128,128),f32),
          pltpu.VMEM((128,128,64),bf16),pltpu.VMEM((E,64,256),bf16),pltpu.VMEM((E,16,256),bf16),
          pltpu.VMEM((U,128,256),f32),pltpu.VMEM((U,2,128,128),bf16),pltpu.VMEM((E+1,8,128),f32)]),
      out_shape=[jax.ShapeDtypeStruct((E,128),f32),jax.ShapeDtypeStruct((NP+128,256,128),bf16)],
      compiler_params=pltpu.CompilerParams(vmem_limit_bytes=60*2**20),
      name="k2")(pairs,count,own,gh)

def k4(opt, G, U, pairs, count, own_ref, gh_ref, press_ref, gpress_ref, s_ref, acc_o, acc_g, C, MM, acc, accA):
    step=pl.program_id(0)
    NP=pairs.shape[1]; TOT=NP+128
    def targets(k):
        kk=jnp.maximum(k-128,0)
        a=jnp.where(k<128,k,pairs[0,kk]); b=jnp.where(k<128,k,pairs[1,kk])
        live=k<128+count[0]
        return a,b,jnp.where(live,a,128 if opt.get('astream') else E),jnp.where(live&(k>=128),b,E)
    @pl.when(step==0)
    def _():
        x,y,z,m=[own_ref[c] for c in range(4)]
        p=press_ref[...]; pm=p*m
        for i,v in enumerate((m,m*x,m*y,m*z,pm,pm*x,pm*y,pm*z)): C[i*E:i*E+128]=v
        for k in range(20):
            x,y,z,m=[gh_ref[k,c] for c in range(4)]
            p=gpress_ref[k*8:k*8+8]; pm=p*m
            o=128+k*8
            for i,v in enumerate((m,m*x,m*y,m*z,pm,pm*x,pm*y,pm*z)): C[i*E+o:i*E+o+8]=v
        acc[...]=jnp.zeros_like(acc)
        if opt.get('astream'): accA[...]=jnp.zeros_like(accA)
        def blk(i,_):
            for j in range(4):
                b=i*4+j
                mv=C[pl.ds(b,8,stride=E),:]
                hi=mv.astype(bf16).astype(f32)
                mm=jnp.concatenate([hi,mv-hi],0).astype(bf16)
                MM[b,:,:128]=mm; MM[b,:,128:]=mm
            return 0
        lax.fori_loop(0,E//4,blk,0)
    def body(u,_):
        resa=[];resb=[]
        for j in range(U):
            k=step*G+u*U+j
            a,b,ta,tb=targets(k)
            hi=s_ref[u*U+j,:128]; lo=s_ref[u*U+j,128:]
            if not opt.get('nob'):
                resb.append((tb,jnp.dot(MM[a],s_ref[u*U+j],preferred_element_type=f32)))
            if not opt.get('noa'):
                cat=jnp.concatenate([hi,lo],1)
                if opt.get('astream'):
                    resa.append((ta,lax.dot_general(cat,MM[b],(((1,),(1,)),((),())),preferred_element_type=f32)))
                else:
                    resb.append((ta,lax.dot_general(MM[b],cat,(((1,),(1,)),((),())),preferred_element_type=f32)))
        for i,r in resb: acc[i]+=r[:8]+r[8:]
        for i,r in resa: accA[i]+=r
        return 0
    lax.fori_loop(0,G//U,body,0)
    @pl.when(step==pl.num_programs(0)-1)
    def _():
        if opt.get('astream'):
            def fin(i,_):
                t=jnp.concatenate([accA[i],jnp.zeros((128,112),f32)],1).T
                acc[i]+=t[:8]+t[8:16]
                return 0
            lax.fori_loop(0,128,fin,0)
        def final(x,y,z,p,A):
            m0=p*A[0]+A[4]
            return [p*A[c+1]+A[c+5]-v*m0 for c,v in enumerate((x,y,z))]
        K=-20.0*NORM
        for i in range(16):
            r=slice(i*8,i*8+8)
            x,y,z=[own_ref[c,r] for c in range(3)]
            A=[acc[r,c,:] for c in range(8)]
            o=final(x,y,z,press_ref[r],A)
            for c in range(3): acc_o[c,r]=o[c]*K
        for i in range(20):
            x,y,z=[gh_ref[i,c] for c in range(3)]
            A=[acc[128+i*8:136+i*8,c,:] for c in range(8)]
            o=final(x,y,z,gpress_ref[i*8:i*8+8],A)
            for c in range(3): acc_g[i,c]=o[c]*K

def run_k4(pairs,count,own,gh,press,gpress,S,opt,G=16,U=2):
    NP=pairs.shape[1]
    n=(NP+128)//G
    V=pl.BlockSpec(memory_space=pltpu.VMEM)
    return pl.pallas_call(functools.partial(k4,opt,G,U),
      grid_spec=pltpu.PrefetchScalarGridSpec(num_scalar_prefetch=2,grid=(n,),
        in_specs=[V]*4+[pl.BlockSpec((G,256,128),lambda i,*_:(0 if opt.get('nodma') else i,0,0))],
        out_specs=[V,V],
        scratch_shapes=[pltpu.VMEM((8*E,128),f32),pltpu.VMEM((E,16,256),bf16),pltpu.VMEM((E+1,8,128),f32),pltpu.VMEM((129 if opt.get('astream') else 1,128,16),f32)]),
      out_shape=[jax.ShapeDtypeStruct((3,128,128),f32),jax.ShapeDtypeStruct((20,3,8,128),f32)],
      compiler_params=pltpu.CompilerParams(vmem_limit_bytes=60*2**20),
      name="k4")(pairs,count,own,gh,press,gpress,S)


MESH = pl.DeviceIdType.MESH
NB = 128
NEIGH = 20
G8 = 8


def neighbour_steps():
    return [
        (step_patch, step_bulk)
        for step_patch in (-1, 0, 1)
        for step_bulk in range(-3, 4)
        if (step_patch, step_bulk) != (0, 0)
    ]


def place(offset):
    rows, columns = lax.axis_size("patch"), lax.axis_size("bulk")
    count = rows * columns
    me = lax.axis_index("patch") * columns + lax.axis_index("bulk")
    other = lax.rem(me + (offset + count), count)
    return (lax.div(other, columns), lax.rem(other, columns))


def offsets():
    columns = lax.axis_size("bulk")
    return [u * columns + v for u, v in neighbour_steps()]


def meet():
    barrier = pltpu.get_barrier_semaphore()
    for o in offsets():
        pl.semaphore_signal(barrier, inc=1, device_id=place(o), device_id_type=MESH)
    pl.semaphore_wait(barrier, NEIGH)


def start_all(src, dst, send_sem, recv_sem, sign):
    copies = []
    for n, o in enumerate(offsets()):
        copy = pltpu.make_async_remote_copy(
            src_ref=src.at[n], dst_ref=dst.at[n], send_sem=send_sem.at[n], recv_sem=recv_sem.at[n],
            device_id=place(sign * o), device_id_type=MESH)
        copy.start()
        copies.append(copy)
    return copies


def split_dot(hot, v):
    a = v.astype(bf16)
    r = v - a.astype(f32)
    b = r.astype(bf16)
    c = (r - b.astype(f32)).astype(bf16)
    dot = functools.partial(jnp.dot, preferred_element_type=f32)
    return dot(hot, a) + (dot(hot, b) + dot(hot, c))


def one_hot(which_ref):
    rows = lax.broadcasted_iota(jnp.int32, (NB, NEIGH * G8), 0)
    return (rows == which_ref[...]).astype(f32).astype(bf16)


def forward_kernel(send_list, rec, out, buf, send_sem, recv_sem):
    meet()

    def gather(n, _):
        for g in range(G8):
            t = send_list[n * G8 + g]
            for c in range(5):
                buf[n, c, g:g + 1, :] = rec[c, pl.ds(t, 1), :]
        return 0

    lax.fori_loop(0, NEIGH, gather, 0)
    for copy in start_all(buf, out, send_sem, recv_sem, 1):
        copy.wait()


def density_kernel(send_list, which, part, gpart, energy, dens_o, press_o, gpress_o, ret, buf, s1, r1, s2, r2):
    meet()
    for copy in start_all(gpart, ret, s1, r1, -1):
        copy.wait()
    hot = one_hot(which)
    dens = part[...] + split_dot(hot, ret[...].reshape(NEIGH * G8, 128))
    dens_o[...] = dens
    press_o[...] = (2.0 / 3.0) * energy[...] / dens

    def gather(n, _):
        for g in range(G8):
            t = send_list[n * G8 + g]
            buf[n, g:g + 1, :] = press_o[pl.ds(t, 1), :]
        return 0

    lax.fori_loop(0, NEIGH, gather, 0)
    for copy in start_all(buf, gpress_o, s2, r2, 1):
        copy.wait()


def force_kernel(which, part, gpart, acc_o, ret, s1, r1):
    meet()
    for copy in start_all(gpart, ret, s1, r1, -1):
        copy.wait()
    hot = one_hot(which)
    for c in range(3):
        acc_o[c] = part[c] + split_dot(hot, ret[:, c].reshape(NEIGH * G8, 128))


def per_device(positions, masses, smoothing, energy, level_ids, send_list, pair_list, pair_count):
    V = pl.BlockSpec(memory_space=pltpu.VMEM)
    S = pl.BlockSpec(memory_space=pltpu.SMEM)
    D = pltpu.SemaphoreType.DMA((NEIGH,))
    sds = jax.ShapeDtypeStruct
    pos = positions.reshape(3, NB, 128)
    mass = masses.reshape(NB, 128)
    en = energy.reshape(NB, 128)
    level = level_ids[:, None]
    scale = jnp.where(level == 0, 1.0, jnp.where(level == 1, SHRINK, SHRINK * SHRINK))
    h = smoothing.reshape(NB, 128) * scale.astype(f32)
    rec = jnp.concatenate([pos, mass[None], h[None]], 0)
    flat = send_list.reshape(NEIGH * G8)
    which = send_list.reshape(1, NEIGH * G8)
    pairs = pair_list[0]
    gh = pl.pallas_call(
        forward_kernel, out_shape=sds((NEIGH, 5, G8, 128), f32), in_specs=[S, V], out_specs=V,
        scratch_shapes=[pltpu.VMEM((NEIGH, 5, G8, 128), f32), D, D],
        compiler_params=pltpu.CompilerParams(collective_id=0, has_side_effects=True), name="forward")(flat, rec)
    dens, tiles = run_k2(pairs, pair_count, rec, gh, {}, G=32, U=8)
    density, press, gpress = pl.pallas_call(
        density_kernel,
        out_shape=[sds((NB, 128), f32), sds((NB, 128), f32), sds((NEIGH, G8, 128), f32)],
        in_specs=[S, V, V, V, V], out_specs=[V, V, V],
        scratch_shapes=[pltpu.VMEM((NEIGH, G8, 128), f32), pltpu.VMEM((NEIGH, G8, 128), f32), D, D, D, D],
        compiler_params=pltpu.CompilerParams(collective_id=1, has_side_effects=True), name="density")(
            flat, which, dens[:NB], dens[NB:].reshape(NEIGH, G8, 128), en)
    acc, gacc = run_k4(pairs, pair_count, rec, gh, press, gpress.reshape(NEIGH * G8, 128), tiles, {}, G=16, U=16)
    accel = pl.pallas_call(
        force_kernel, out_shape=sds((3, NB, 128), f32), in_specs=[V, V, V], out_specs=V,
        scratch_shapes=[pltpu.VMEM((NEIGH, 3, G8, 128), f32), D, D],
        compiler_params=pltpu.CompilerParams(collective_id=2, has_side_effects=True), name="force")(which, acc, gacc)
    return density.reshape(NB * 128), accel.reshape(3, NB * 128)


def solution(mesh):
    both = ("patch", "bulk")
    placed = (P(None, both), P(both), P(both), P(both), P(both), P(both, None, None), P(both, None, None), P(both))
    return jax.shard_map(per_device, mesh=mesh, in_specs=placed, out_specs=(P(both), P(None, both)), check_vma=False)
```

time: 956 us -> 195 us (0.20); the launches traced: 941 us -> 194 us
  other arithmetic: 478 us -> 3.18 us
  starting transfers between devices: 204 us -> 0 us
  Pallas kernels: 0 us -> 181 us
  local copies, waits for them, and re-layouts: 142 us -> 8.44 us
  waiting for transfers between devices: 111 us -> 0 us
    reduce_sum x87 -> x0, other arithmetic: 261 us -> none  [the longest x43 98.1 us: kernel_terms(): dist = jnp.sqrt(jnp.sum(dx * dx, axis=0))]
    ppermute x80 -> x0, starting transfers between devices: 204 us -> none  [from_behind(): return lax.ppermute(block, axis, route)]
    pallas_call x0 -> x5, Pallas kernels: none -> 181 us  [the longest x1 79.6 us: run_k2(): pl.pallas_call(functools.partial(k2, opt, G, U), grid_spec=pltpu.Prefetch...]
    gather x166 -> x0, local copies, waits for them, and re-layouts: 112 us -> none  [the longest x20 25.1 us: per_device(): payloads = [record[:, targets[which]] for which in range(peers)]]
    ppermute x80 -> x0, waiting for transfers between devices: 111 us -> none  [from_behind(): return lax.ppermute(block, axis, route)]
    scatter-add x6 -> x0, other arithmetic: 68.8 us -> none  [the longest x1 24.6 us: per_device(): jax.ops.segment_sum(acc_a * live[:, None, None], first, ext_count)]
    mul x46 -> x1, other arithmetic: 69.1 us -> 0.92 us  [per_device(): h = smoothing.reshape(NB, 128) * scale.astype(f32)]
    select_n x104 -> x1, other arithmetic: 57.4 us -> 0.66 us  [per_device(): jnp.where(level == 0, 1.0, jnp.where(level == 1, SHRINK, SHRINK * SHRINK))]
  transfers between devices with their start and end apart: 80 -> 0, of which waited for: 37 -> 0; matrix products, arithmetic and copies ran while one was open for 9% -> 0% of each run, Pallas kernels for 0% -> 0%
where the time goes in v1:
time: 195 us; the launch traced here: 194 us
  Pallas kernels  181 us (93%)
  local copies, waits for them, and re-layouts  8.44 us (4%)
  other arithmetic  3.18 us (2%)
    pallas_call x1, Pallas kernels, run_k2(): pl.pallas_call(functools.partial(k2, opt, G, U), grid_spec=pltpu.Prefetch...  79.6 us
    pallas_call x1, Pallas kernels, run_k4(): pl.pallas_call(functools.partial(k4, opt, G, U), grid_spec=pltpu.Prefetch...  51.1 us
    pallas_call x1, Pallas kernels, per_device(): pl.pallas_call(forward_kernel, out_shape=sds((NEIGH, 5, G8, 128), f32), i...  19.6 us
    pallas_call x1, Pallas kernels, per_device(): pl.pallas_call(density_kernel, out_shape=[sds((NB, 128), f32), sds((NB, 1...  18.4 us
    pallas_call x1, Pallas kernels, per_device(): pl.pallas_call(force_kernel, out_shape=sds((3, NB, 128), f32), in_specs=[...  12.4 us
    unnamed x6, local copies, waits for them, and re-layouts  4.14 us

profile of v1, /device:TPU:1, one launch (start us, length us, event | category | flops | bytes accessed | tf_op | source)
XLA Modules:
  0.0 193.9 jit_solution(2032524146364547820)
XLA Ops:
  0.6 0.8 copy.11
  1.4 0.6 reshape.63.send_list
  2.0 0.7 reshape.64.which
  3.4 0.7 compare_select_fusion.1
  4.0 0.9 bitcast_multiply_fusion
  4.9 1.0 copy.18
  5.9 1.6 pad_maximum_fusion.rec.own_ref
  7.5 19.6 %forward.1.gh_ref = f32[20,5,8,128]{3,2,1,0:T(8,128)} custom-call(s32[160]{0:T(256)} %reshape.63.send_list, f32[5,128,128]{2,1,0:T(8,128)} %pad_maximum_fusion.rec.own_ref), custom_call_target="tpu_custom_call" | custom-call | tf_op jit(solution)/shard_map/forward/pallas_call | solution.py:352
  27.1 79.6 %k2.1 = (f32[288,128]{1,0:T(8,128)}, bf16[800,256,128]{2,1,0:T(8,128)(2,1)}) custom-call(s32[2,672]{1,0:T(2,128)} %bitcast.25, s32[1]{0:T(128)S(6)} %copy.20.count, f32[5,128,128]{2,1,0:T(8,128)} %pad_maximum_fusion.rec.own_ref, f32[20,5,8,128]{3,2,1,0:T(8,128)} %forward.1.gh_ref), custom_call_target="tpu_custom_call" | custom-call | tf_op jit(solution)/shard_map/k2/pallas_call | solution.py:137
  106.6 1.5 slice.6.part
  108.1 1.5 slice_bitcast_fusion.gpart
  109.6 18.4 %density.1 = (f32[128,128]{1,0:T(8,128)}, f32[128,128]{1,0:T(8,128)}, f32[20,8,128]{2,1,0:T(8,128)}) custom-call(s32[160]{0:T(256)} %reshape.63.send_list, s32[1,160]{1,0:T(1,128)} %reshape.64.which, f32[128,128]{1,0:T(8,128)} %slice.6.part, f32[20,8,128]{2,1,0:T(8,128)} %slice_bitcast_fusion.gpart, f32[128,128]{1,0:T(8,128)} %bitcast.23), custom_call_target="tpu_custom_call" | custom-call | tf_op jit(solution)/shard_map/density/pallas_call | solution.py:357
  128.0 0.0 copy-start
  128.0 51.1 %k4.1 = (f32[3,128,128]{2,1,0:T(8,128)}, f32[20,3,8,128]{3,2,1,0:T(8,128)}) custom-call(s32[2,672]{1,0:T(2,128)} %bitcast.26, s32[1]{0:T(128)S(6)} %copy.20.count, f32[5,128,128]{2,1,0:T(8,128)} %pad_maximum_fusion.rec.own_ref, f32[20,5,8,128]{3,2,1,0:T(8,128)} %forward.1.gh_ref, f32[128,128]{1,0:T(8,128)} %get-tuple-element.11.press_ref, ...), custom_call_target="tpu_custom_call" | custom-call | tf_op jit(solution)/shard_map/k4/pallas_call | solution.py:223
  179.1 12.4 %force.1 = f32[3,128,128]{2,1,0:T(8,128)} custom-call(s32[1,160]{1,0:T(1,128)} %reshape.64.which, f32[3,128,128]{2,1,0:T(8,128)} %get-tuple-element.14.part, f32[20,3,8,128]{3,2,1,0:T(8,128)} %get-tuple-element.15.gpart), custom_call_target="tpu_custom_call" | custom-call | tf_op jit(solution)/shard_map/force/pallas_call | solution.py:365
  191.5 1.8 copy.17
  193.3 0.0 copy-done
  193.3 0.6 copy.21
Async XLA Ops:
  128.0 65.3 %copy-start = (f32[128,128]{1,0:T(8,128)S(1)}, f32[128,128]{1,0:T(8,128)}, u32[]{:S(2)}) copy-start(f32[128,128]{1,0:T(8,128)} %get-tuple-element.10) | copy-start | bytes 196612

commit v2 on v0

v2 whole, which is shorter than its diff:
```python
import functools
import math

import jax
import jax.numpy as jnp
from jax import lax
from jax.experimental import pallas as pl
from jax.experimental.pallas import tpu as pltpu
from jax.sharding import PartitionSpec as P

MESH = pl.DeviceIdType.MESH
f32 = jnp.float32
bf16 = jnp.bfloat16
NORM = 21.0 / (2.0 * math.pi)
GAMMA_LESS = 2.0 / 3.0
SHRINK = 0.8
NB = 128
W128 = 128
NEIGH = 20
SLOTS = 8
GHOSTS = NEIGH * SLOTS
EXT = NB + GHOSTS
CHUNKS = [(0, 0), (0, 1), (1, 0), (1, 1), (0, 2), (2, 0), (1, 2), (2, 1)]
UNITS_STEP = 32
UNROLL = 16
FORCE_STEP = 80
FORCE_UNROLL = 16


def neighbour_steps():
    return [
        (step_patch, step_bulk)
        for step_patch in (-1, 0, 1)
        for step_bulk in range(-3, 4)
        if (step_patch, step_bulk) != (0, 0)
    ]


def place(offset):
    rows, columns = lax.axis_size("patch"), lax.axis_size("bulk")
    count = rows * columns
    me = lax.axis_index("patch") * columns + lax.axis_index("bulk")
    other = lax.rem(me + (offset + count), count)
    return (lax.div(other, columns), lax.rem(other, columns))


def offsets():
    columns = lax.axis_size("bulk")
    return [u * columns + v for u, v in neighbour_steps()]


def meet():
    barrier = pltpu.get_barrier_semaphore()
    for o in offsets():
        pl.semaphore_signal(barrier, inc=1, device_id=place(o), device_id_type=MESH)
    pl.semaphore_wait(barrier, NEIGH)


def start_all(src, dst, send_sem, recv_sem, sign):
    copies = []
    for n, o in enumerate(offsets()):
        copy = pltpu.make_async_remote_copy(
            src_ref=src.at[n], dst_ref=dst.at[n], send_sem=send_sem.at[n], recv_sem=recv_sem.at[n],
            device_id=place(sign * o), device_id_type=MESH)
        copy.start()
        copies.append(copy)
    return copies


def split3(v):
    a = v.astype(bf16).astype(f32)
    r = v - a
    b = r.astype(bf16).astype(f32)
    return a, b, r - b


def hilo(v):
    hi = v.astype(bf16)
    return hi, (v - hi.astype(f32)).astype(bf16)


def split_dot(hot, v):
    a, b, c = [p.astype(bf16) for p in split3(v)]
    dot = functools.partial(jnp.dot, preferred_element_type=f32)
    return dot(hot, a) + (dot(hot, b) + dot(hot, c))


def one_hot(which_ref):
    rows = lax.broadcasted_iota(jnp.int32, (NB, GHOSTS), 0)
    return (rows == which_ref[...]).astype(f32).astype(bf16)


def inverse_cube_root(m):
    k = jnp.exp(jnp.log(m) * (-1.0 / 3.0))
    return k * (4.0 - m * (k * k * k)) * (1.0 / 3.0)


def forward_kernel(send_list, pairs, count, pos, mass, smooth, out, idx, buf, send_sem, recv_sem):
    def gather(n, _):
        for g in range(SLOTS):
            t = send_list[0, n, g]
            for c in range(3):
                buf[n, c, g:g + 1, :] = pos[c, pl.ds(t, 1), :]
            buf[n, 3, g:g + 1, :] = mass[pl.ds(t, 1), :]
            buf[n, 4, g:g + 1, :] = smooth[pl.ds(t, 1), :]
        return 0

    meet()
    lax.fori_loop(0, NEIGH, gather, 0)
    copies = start_all(buf, out, send_sem, recv_sem, 1)
    total = NB + pairs.shape[2]
    lane = lax.broadcasted_iota(jnp.int32, (1, total - NB), 1)
    live = lane < count[0]
    own = lax.broadcasted_iota(jnp.int32, (1, NB), 1)
    idx[...] = jnp.zeros_like(idx)
    for r in range(4):
        idx[r:r + 1, :NB] = own if r < 3 else jnp.full((1, NB), EXT, jnp.int32)
    first = pairs[0, 0:1, :]
    second = pairs[0, 1:2, :]
    idx[0:1, NB:total] = first
    idx[1:2, NB:total] = second
    idx[2:3, NB:total] = jnp.where(live, first, NB)
    idx[3:4, NB:total] = jnp.where(live, second, EXT)
    for copy in copies:
        copy.wait()


def tile_math(r2, hs):
    r2 = jnp.maximum(r2, 1e-30)
    s = pl.reciprocal(hs, approx=True)
    q = r2 * lax.rsqrt(r2) * s
    t = jnp.maximum(1.0 - q, 0.0)
    st = s * t
    c = st * st * st
    return c * (t * (q + 0.25)), c * (s * s)


def density_pairs(idx, pos, mass, smooth, ghost, dens_o, dens_g, tiles, C, CA, AF, BF, GB, acc_a, acc_b):
    step = pl.program_id(0)

    def first_stage(k, j):
        GB[j] = jnp.dot(AF[idx[0, k]], BF[idx[1, k]], preferred_element_type=f32)

    @pl.when(step == 0)
    def _():
        zero = jnp.zeros((EXT, W128), f32)
        for i in (5, 6, 7, 8, 9, 12):
            C[i * EXT:(i + 1) * EXT] = zero
        CA[7 * NB:8 * NB] = zero[:NB]

        def columns(x, y, z, m, h):
            k = inverse_cube_root(m)
            k2 = k * k
            return x * k2, y * k2, z * k2, k2, (x * x + y * y + z * z) * k2, (0.5 * h) * k, k

        def fill(at, rows, v):
            for i, c in ((0, 0), (1, 1), (2, 2), (3, 3), (4, 4), (10, 5), (11, 6)):
                C[i * EXT + at:i * EXT + at + rows] = v[c]

        v = columns(pos[0], pos[1], pos[2], mass[...], smooth[...])
        fill(0, NB, v)
        for i, w in enumerate((-2.0 * v[0], -2.0 * v[1], -2.0 * v[2], v[4], v[3])):
            CA[i * NB:(i + 1) * NB] = w
        CA[5 * NB:6 * NB] = v[6]
        CA[6 * NB:7 * NB] = v[5]
        for n in range(NEIGH):
            fill(NB + n * SLOTS, SLOTS, columns(*[ghost[n, c] for c in range(5)]))
        acc_b[...] = jnp.zeros_like(acc_b)

        def right_side(i, _):
            for j in range(4):
                b = i * 4 + j
                for w, c in ((0, 0), (5, W128)):
                    p = split3(C[pl.ds(w * EXT + b, 8, stride=EXT), :])
                    BF[b, :, c:c + W128] = jnp.concatenate([p[q] for _, q in CHUNKS], 0).astype(bf16)
            return 0

        lax.fori_loop(0, EXT // 4, right_side, 0)

        def left_side(i, _):
            for j in range(8):
                b = i * 8 + j
                p = split3(CA[pl.ds(b, 8, stride=NB), :])
                AF[b] = jnp.concatenate([p[q] for q, _ in CHUNKS], 0).T.astype(bf16)
                acc_a[b] = jnp.zeros((W128, W128), f32)
            return 0

        lax.fori_loop(0, NB // 8, left_side, 0)
        for j in range(UNROLL):
            first_stage(j, j)

    def body(u, _):
        k0 = step * UNITS_STEP + u * UNROLL
        sums = []
        for j in range(UNROLL):
            ta = idx[2, k0 + j]
            part = jnp.zeros((8, W128), f32)
            for r in range(0, W128, 8):
                W, S = tile_math(GB[j, r:r + 8, :W128], GB[j, r:r + 8, W128:])
                tiles[u * UNROLL + j, r:r + 8] = S
                part = part + W
                acc_a[ta, r:r + 8] += W
            first_stage(k0 + UNROLL + j, j)
            sums.append((idx[3, k0 + j], part))
        for tb, part in sums:
            acc_b[pl.ds(pl.multiple_of(tb * 8, 8), 8), :] += part
        return 0

    lax.fori_loop(0, UNITS_STEP // UNROLL, body, 0)

    @pl.when(step == pl.num_programs(0) - 1)
    def _():
        ones = jnp.ones((16, 2 * W128), bf16)

        def fold(i, _):
            rows = []
            for j in range(4):
                hi, lo = hilo(acc_a[i * 4 + j])
                rows.append(lax.dot_general(ones, jnp.concatenate([hi, lo], 1), (((1,), (1,)), ((), ())),
                                            preferred_element_type=f32))
            for j in range(4):
                dens_o[pl.ds(i * 4 + j, 1), :] = rows[j][:1]
            return 0

        lax.fori_loop(0, NB // 4, fold, 0)
        for i in range(EXT // 8):
            v = acc_b[pl.ds(i * 64, 8, stride=8), :]
            for s in range(1, 8):
                v = v + acc_b[pl.ds(i * 64 + s, 8, stride=8), :]
            if i < NB // 8:
                r = slice(i * 8, i * 8 + 8)
                dens_o[r] = (dens_o[r] + v) * (4.0 * NORM) / mass[r]
            else:
                n = i - NB // 8
                dens_g[n] = v * (4.0 * NORM) / ghost[n, 3]


def density_kernel(send_list, which, part, gpart, energy, dens_o, press_o, gpress_o, ret, buf, s1, r1, s2, r2):
    meet()
    copies = start_all(gpart, ret, s1, r1, -1)
    hot = one_hot(which)
    for copy in copies:
        copy.wait()
    dens = part[...] + split_dot(hot, ret[...].reshape(GHOSTS, W128))
    dens_o[...] = dens
    press_o[...] = GAMMA_LESS * energy[...] / dens

    def gather(n, _):
        for g in range(SLOTS):
            buf[n, g:g + 1, :] = press_o[pl.ds(send_list[0, n, g], 1), :]
        return 0

    lax.fori_loop(0, NEIGH, gather, 0)
    for copy in start_all(buf, gpress_o, s2, r2, 1):
        copy.wait()


def force_pairs(idx, pos, mass, ghost, press, gpress, tiles, acc_o, acc_g, C, MM, acc):
    step = pl.program_id(0)

    @pl.when(step == 0)
    def _():
        def fill(at, rows, x, y, z, m, p):
            k = inverse_cube_root(m)
            w = k * k
            pw = p * w
            for i, v in enumerate((w, w * x, w * y, w * z, pw, pw * x, pw * y, pw * z)):
                C[i * EXT + at:i * EXT + at + rows] = v

        fill(0, NB, pos[0], pos[1], pos[2], mass[...], press[...])
        for n in range(NEIGH):
            fill(NB + n * SLOTS, SLOTS, *[ghost[n, c] for c in range(4)], gpress[n])
        acc[...] = jnp.zeros_like(acc)

        def columns(i, _):
            for j in range(4):
                b = i * 4 + j
                v = C[pl.ds(b, 8, stride=EXT), :]
                hi = v.astype(bf16).astype(f32)
                mm = jnp.concatenate([hi, v - hi], 0).astype(bf16)
                MM[b, :, :W128] = mm
                MM[b, :, W128:] = mm
            return 0

        lax.fori_loop(0, EXT // 4, columns, 0)

    def body(u, _):
        sums = []
        for j in range(FORCE_UNROLL):
            k = step * FORCE_STEP + u * FORCE_UNROLL + j
            hi, lo = hilo(tiles[u * FORCE_UNROLL + j])
            to_b = jnp.dot(MM[idx[0, k]], jnp.concatenate([hi, lo], 0), preferred_element_type=f32)
            to_a = lax.dot_general(MM[idx[1, k]], jnp.concatenate([hi, lo], 1), (((1,), (1,)), ((), ())),
                                   preferred_element_type=f32)
            sums.append((idx[2, k], to_a))
            sums.append((idx[3, k], to_b))
        for n, (i, v) in enumerate(sums):
            if n % 2 == 0:
                i = jnp.where(i == NB, EXT, i)
            acc[i] += v[:8] + v[8:]
        return 0

    lax.fori_loop(0, FORCE_STEP // FORCE_UNROLL, body, 0)

    @pl.when(step == pl.num_programs(0) - 1)
    def _():
        def final(p, m, spot, A):
            k = inverse_cube_root(m)
            k2 = k * k
            scale = (-20.0 * NORM) * (k2 * k2 * k)
            own = p * A[0] + A[4]
            return [(p * A[c + 1] + A[c + 5] - v * own) * scale for c, v in enumerate(spot)]

        for i in range(EXT // 8):
            r = slice(i * 8, i * 8 + 8)
            A = [acc[r, c, :] for c in range(8)]
            if i < NB // 8:
                for c, v in enumerate(final(press[r], mass[r], [pos[c, r] for c in range(3)], A)):
                    acc_o[c, r] = v
            else:
                n = i - NB // 8
                for c, v in enumerate(final(gpress[n], ghost[n, 3], [ghost[n, c] for c in range(3)], A)):
                    acc_g[n, c] = v


def force_kernel(which, part, gpart, acc_o, ret, s1, r1):
    meet()
    copies = start_all(gpart, ret, s1, r1, -1)
    hot = one_hot(which)
    for copy in copies:
        copy.wait()
    for c in range(3):
        acc_o[c] = part[c] + split_dot(hot, ret[:, c].reshape(GHOSTS, W128))


V = pl.BlockSpec(memory_space=pltpu.VMEM)
SM = pl.BlockSpec(memory_space=pltpu.SMEM)
sds = jax.ShapeDtypeStruct


def exchange_params(number):
    return pltpu.CompilerParams(collective_id=number, has_side_effects=True)


def run_density(idx, pos, mass, smooth, ghost, units):
    return pl.pallas_call(
        density_pairs,
        grid_spec=pltpu.PrefetchScalarGridSpec(
            num_scalar_prefetch=1, grid=(units // UNITS_STEP,), in_specs=[V] * 4,
            out_specs=[V, V, pl.BlockSpec((UNITS_STEP, W128, W128), lambda i, *_: (i, 0, 0))],
            scratch_shapes=[
                pltpu.VMEM((13 * EXT, W128), f32), pltpu.VMEM((8 * NB, W128), f32),
                pltpu.VMEM((NB, W128, 64), bf16), pltpu.VMEM((EXT, 64, 2 * W128), bf16),
                pltpu.VMEM((UNROLL, W128, 2 * W128), f32), pltpu.VMEM((NB + 1, W128, W128), f32),
                pltpu.VMEM(((EXT + 1) * 8, W128), f32)]),
        out_shape=[sds((NB, W128), f32), sds((NEIGH, SLOTS, W128), f32), sds((units, W128, W128), f32)],
        compiler_params=pltpu.CompilerParams(vmem_limit_bytes=60 * 2**20),
        name="density_pairs")(idx, pos, mass, smooth, ghost)


def run_force(idx, pos, mass, ghost, press, gpress, tiles):
    return pl.pallas_call(
        force_pairs,
        grid_spec=pltpu.PrefetchScalarGridSpec(
            num_scalar_prefetch=1, grid=(tiles.shape[0] // FORCE_STEP,),
            in_specs=[V] * 5 + [pl.BlockSpec((FORCE_STEP, W128, W128), lambda i, *_: (i, 0, 0))],
            out_specs=[V, V],
            scratch_shapes=[
                pltpu.VMEM((8 * EXT, W128), f32), pltpu.VMEM((EXT, 16, 2 * W128), bf16),
                pltpu.VMEM((EXT + 1, 8, W128), f32)]),
        out_shape=[sds((3, NB, W128), f32), sds((NEIGH, 3, SLOTS, W128), f32)],
        compiler_params=pltpu.CompilerParams(vmem_limit_bytes=60 * 2**20),
        name="force_pairs")(idx, pos, mass, ghost, press, gpress, tiles)


def per_device(positions, masses, smoothing, energy, level_ids, send_list, pair_list, pair_count):
    D = pltpu.SemaphoreType.DMA((NEIGH,))
    units = NB + pair_list.shape[2]
    pos = positions.reshape(3, NB, W128)
    mass = masses.reshape(NB, W128)
    level = level_ids[:, None]
    scale = jnp.where(level == 0, 1.0, jnp.where(level == 1, SHRINK, SHRINK * SHRINK)).astype(f32)
    smooth = smoothing.reshape(NB, W128) * scale
    which = send_list.reshape(1, GHOSTS)
    ghost, idx = pl.pallas_call(
        forward_kernel,
        out_shape=[sds((NEIGH, 5, SLOTS, W128), f32), sds((4, units + 2 * W128 - units % W128), jnp.int32)],
        in_specs=[SM, V, SM, V, V, V], out_specs=[V, V],
        scratch_shapes=[pltpu.VMEM((NEIGH, 5, SLOTS, W128), f32), D, D],
        compiler_params=exchange_params(0), name="forward")(send_list, pair_list, pair_count, pos, mass, smooth)
    dens, gdens, tiles = run_density(idx, pos, mass, smooth, ghost, units)
    density, press, gpress = pl.pallas_call(
        density_kernel,
        out_shape=[sds((NB, W128), f32), sds((NB, W128), f32), sds((NEIGH, SLOTS, W128), f32)],
        in_specs=[SM, V, V, V, V], out_specs=[V, V, V],
        scratch_shapes=[pltpu.VMEM((NEIGH, SLOTS, W128), f32), pltpu.VMEM((NEIGH, SLOTS, W128), f32), D, D, D, D],
        compiler_params=exchange_params(1), name="density")(
            send_list, which, dens, gdens, energy.reshape(NB, W128))
    acc, gacc = run_force(idx, pos, mass, ghost, press, gpress, tiles)
    accel = pl.pallas_call(
        force_kernel, out_shape=sds((3, NB, W128), f32), in_specs=[V, V, V], out_specs=V,
        scratch_shapes=[pltpu.VMEM((NEIGH, 3, SLOTS, W128), f32), D, D],
        compiler_params=exchange_params(2), name="force")(which, acc, gacc)
    return density.reshape(NB * W128), accel.reshape(3, NB * W128)


def solution(mesh):
    both = ("patch", "bulk")
    placed = (P(None, both), P(both), P(both), P(both), P(both), P(both, None, None), P(both, None, None), P(both))
    return jax.shard_map(per_device, mesh=mesh, in_specs=placed, out_specs=(P(both), P(None, both)), check_vma=False)
```

time: 956 us -> 149 us (0.16); the launches traced: 941 us -> 148 us
  other arithmetic: 478 us -> 2.21 us
  starting transfers between devices: 204 us -> 0 us
  Pallas kernels: 0 us -> 139 us
  local copies, waits for them, and re-layouts: 142 us -> 5.5 us
  waiting for transfers between devices: 111 us -> 0 us
    reduce_sum x87 -> x0, other arithmetic: 261 us -> none  [the longest x43 98.1 us: kernel_terms(): dist = jnp.sqrt(jnp.sum(dx * dx, axis=0))]
    ppermute x80 -> x0, starting transfers between devices: 204 us -> none  [from_behind(): return lax.ppermute(block, axis, route)]
    pallas_call x0 -> x5, Pallas kernels: none -> 139 us  [the longest x1 53.8 us: run_density(): pl.pallas_call(density_pairs, grid_spec=pltpu.PrefetchScalarGridSpec(num_...]
    gather x166 -> x0, local copies, waits for them, and re-layouts: 112 us -> none  [the longest x20 25.1 us: per_device(): payloads = [record[:, targets[which]] for which in range(peers)]]
    ppermute x80 -> x0, waiting for transfers between devices: 111 us -> none  [from_behind(): return lax.ppermute(block, axis, route)]
    scatter-add x6 -> x0, other arithmetic: 68.8 us -> none  [the longest x1 24.6 us: per_device(): jax.ops.segment_sum(acc_a * live[:, None, None], first, ext_count)]
    mul x46 -> x1, other arithmetic: 69.1 us -> 1.55 us  [per_device(): smooth = smoothing.reshape(NB, W128) * scale]
    select_n x104 -> x1, other arithmetic: 57.4 us -> 0.66 us  [per_device(): jnp.where(level == 0, 1.0, jnp.where(level == 1, SHRINK, SHRINK * SHRINK))]
  transfers between devices with their start and end apart: 80 -> 0, of which waited for: 37 -> 0; matrix products, arithmetic and copies ran while one was open for 9% -> 0% of each run, Pallas kernels for 0% -> 0%
where the time goes in v2:
time: 149 us; the launch traced here: 148 us
  Pallas kernels  139 us (93%)
  local copies, waits for them, and re-layouts  5.5 us (4%)
  other arithmetic  2.21 us (1%)
    pallas_call x1, Pallas kernels, run_density(): pl.pallas_call(density_pairs, grid_spec=pltpu.PrefetchScalarGridSpec(num_...  53.8 us
    pallas_call x1, Pallas kernels, run_force(): pl.pallas_call(force_pairs, grid_spec=pltpu.PrefetchScalarGridSpec(num_sc...  35.3 us
    pallas_call x1, Pallas kernels, per_device(): pl.pallas_call(forward_kernel, out_shape=[sds((NEIGH, 5, SLOTS, W128), f3...  19.6 us
    pallas_call x1, Pallas kernels, per_device(): pl.pallas_call(density_kernel, out_shape=[sds((NB, W128), f32), sds((NB,...  18.4 us
    pallas_call x1, Pallas kernels, per_device(): pl.pallas_call(force_kernel, out_shape=sds((3, NB, W128), f32), in_specs=...  12.3 us
    unnamed x8, local copies, waits for them, and re-layouts  4.84 us

profile of v2, /device:TPU:1, one launch (start us, length us, event | category | flops | bytes accessed | tf_op | source)
XLA Modules:
  0.0 148.5 jit_solution(8993347447311671014)
XLA Ops:
  0.6 0.8 copy.15.send_list
  1.4 0.0 copy-start
  1.4 0.7 reshape.30.which
  2.7 1.7 %copy.21 = f32[1,3,128,128]{3,2,1,0:T(8,128)} copy(f32[1,3,128,128]{3,1,2,0:T(4,128)} %bitcast.20) | data formatting | bytes 393216
  4.4 0.7 compare_select_fusion.1
  5.0 1.6 %bitcast_multiply_fusion.smooth = f32[128,128]{1,0:T(8,128)} fusion(f32[16384]{0:T(1024)} %param.10, f32[128]{0:T(128)S(1)} %compare_select_fusion.1), kind=kLoop, calls=%fused_computation.2 | loop fusion | flops 16384 | bytes 131584 | tf_op jit(solution)/shard_map/mul | solution.py:383
  6.6 0.0 copy-done
  6.6 19.6 %forward.1 = (f32[20,5,8,128]{3,2,1,0:T(8,128)}, s32[4,1024]{1,0:T(4,128)}) custom-call(s32[1,20,8]{2,1,0:T(8,128)} %copy-done, s32[1,2,672]{2,1,0:T(2,128)} %pairs.1, s32[1]{0:T(128)S(6)} %copy.23.count, f32[3,128,128]{2,1,0:T(8,128)} %bitcast.13, f32[128,128]{1,0:T(8,128)} %bitcast.17, f32[128,128]{1,0:T(8,128)} %bitcast_multiply_fusion.smooth), custom_call_target="tpu_custom_call" | custom-call | tf_op jit(solution)/shard_map/forward/pallas_call | solution.py:385
  26.2 53.8 %density_pairs.1 = (f32[128,128]{1,0:T(8,128)}, f32[20,8,128]{2,1,0:T(8,128)}, f32[800,128,128]{2,1,0:T(8,128)}) custom-call(s32[4,1024]{1,0:T(4,128)} %get-tuple-element.12.idx, f32[3,128,128]{2,1,0:T(8,128)} %bitcast.14, f32[128,128]{1,0:T(8,128)} %bitcast.18, f32[128,128]{1,0:T(8,128)} %bitcast_multiply_fusion.smooth, ...), custom_call_target="tpu_custom_call" | custom-call | tf_op jit(solution)/shard_map/density_pairs/pallas_call | solution.py:346
  80.0 18.4 %density.1 = (f32[128,128]{1,0:T(8,128)}, f32[128,128]{1,0:T(8,128)}, f32[20,8,128]{2,1,0:T(8,128)}) custom-call(s32[1,20,8]{2,1,0:T(8,128)} %copy-done, s32[1,160]{1,0:T(1,128)} %reshape.30.which, f32[128,128]{1,0:T(8,128)} %get-tuple-element.14.part, f32[20,8,128]{2,1,0:T(8,128)} %get-tuple-element.15.gpart, f32[128,128]{1,0:T(8,128)} %bitcast.22), custom_call_target="tpu_custom_call" | custom-call | tf_op jit(solution)/shard_map/density/pallas_call | solution.py:392
  98.5 0.0 copy-start.1
  98.5 35.3 %force_pairs.1 = (f32[3,128,128]{2,1,0:T(8,128)}, f32[20,3,8,128]{3,2,1,0:T(8,128)}) custom-call(s32[4,1024]{1,0:T(4,128)} %get-tuple-element.12.idx, f32[3,128,128]{2,1,0:T(8,128)} %bitcast.15, f32[128,128]{1,0:T(8,128)} %bitcast.19, f32[20,5,8,128]{3,2,1,0:T(8,128)} %get-tuple-element.13.ghost, f32[128,128]{1,0:T(8,128)} %get-tuple-element.17.press, ...), custom_call_target="tpu_custom_call" | custom-call | tf_op jit(solution)/shard_map/force_pairs/pallas_call | solution.py:362
  133.8 12.3 %force.1 = f32[3,128,128]{2,1,0:T(8,128)} custom-call(s32[1,160]{1,0:T(1,128)} %reshape.30.which, f32[3,128,128]{2,1,0:T(8,128)} %get-tuple-element.20.part, f32[20,3,8,128]{3,2,1,0:T(8,128)} %get-tuple-element.21.gpart), custom_call_target="tpu_custom_call" | custom-call | tf_op jit(solution)/shard_map/force/pallas_call | solution.py:400
  146.1 1.8 %copy.20 = f32[1,3,128,128]{3,1,2,0:T(4,128)} copy(f32[1,3,128,128]{3,2,1,0:T(8,128)} %bitcast.16) | data formatting | bytes 393216
  147.9 0.0 copy-done.1
  147.9 0.6 copy.24
Async XLA Ops:
  1.4 5.2 %copy-start = (s32[1,20,8]{2,1,0:T(8,128)}, s32[1,20,8]{2,1,0:T(8,128)S(1)}, u32[]{:S(2)}) copy-start(s32[1,20,8]{2,1,0:T(8,128)S(1)} %copy.15.send_list) | copy-start | bytes 1924
  98.5 49.4 %copy-start.1 = (f32[128,128]{1,0:T(8,128)S(1)}, f32[128,128]{1,0:T(8,128)}, u32[]{:S(2)}) copy-start(f32[128,128]{1,0:T(8,128)} %get-tuple-element.16) | copy-start | bytes 196612

commit v3 on v2

--- a/solution.py
+++ b/solution.py
@@ -23,8 +23,10 @@
 CHUNKS = [(0, 0), (0, 1), (1, 0), (1, 1), (0, 2), (2, 0), (1, 2), (2, 1)]
 UNITS_STEP = 32
 UNROLL = 16
-FORCE_STEP = 80
-FORCE_UNROLL = 16
+FORCE_STEP = 84
+FORCE_UNROLL = 14
+SELF = 8
+VMEM = 63 * 2**20
 
 
 def neighbour_steps():
@@ -85,44 +87,9 @@
     return dot(hot, a) + (dot(hot, b) + dot(hot, c))
 
 
-def one_hot(which_ref):
-    rows = lax.broadcasted_iota(jnp.int32, (NB, GHOSTS), 0)
-    return (rows == which_ref[...]).astype(f32).astype(bf16)
-
-
 def inverse_cube_root(m):
     k = jnp.exp(jnp.log(m) * (-1.0 / 3.0))
     return k * (4.0 - m * (k * k * k)) * (1.0 / 3.0)
-
-
-def forward_kernel(send_list, pairs, count, pos, mass, smooth, out, idx, buf, send_sem, recv_sem):
-    def gather(n, _):
-        for g in range(SLOTS):
-            t = send_list[0, n, g]
-            for c in range(3):
-                buf[n, c, g:g + 1, :] = pos[c, pl.ds(t, 1), :]
-            buf[n, 3, g:g + 1, :] = mass[pl.ds(t, 1), :]
-            buf[n, 4, g:g + 1, :] = smooth[pl.ds(t, 1), :]
-        return 0
-
-    meet()
-    lax.fori_loop(0, NEIGH, gather, 0)
-    copies = start_all(buf, out, send_sem, recv_sem, 1)
-    total = NB + pairs.shape[2]
-    lane = lax.broadcasted_iota(jnp.int32, (1, total - NB), 1)
-    live = lane < count[0]
-    own = lax.broadcasted_iota(jnp.int32, (1, NB), 1)
-    idx[...] = jnp.zeros_like(idx)
-    for r in range(4):
-        idx[r:r + 1, :NB] = own if r < 3 else jnp.full((1, NB), EXT, jnp.int32)
-    first = pairs[0, 0:1, :]
-    second = pairs[0, 1:2, :]
-    idx[0:1, NB:total] = first
-    idx[1:2, NB:total] = second
-    idx[2:3, NB:total] = jnp.where(live, first, NB)
-    idx[3:4, NB:total] = jnp.where(live, second, EXT)
-    for copy in copies:
-        copy.wait()
 
 
 def tile_math(r2, hs):
@@ -135,7 +102,116 @@
     return c * (t * (q + 0.25)), c * (s * s)
 
 
-def density_pairs(idx, pos, mass, smooth, ghost, dens_o, dens_g, tiles, C, CA, AF, BF, GB, acc_a, acc_b):
+def scaled_columns(x, y, z, m, h):
+    k = inverse_cube_root(m)
+    k2 = k * k
+    return x * k2, y * k2, z * k2, k2, (x * x + y * y + z * z) * k2, (0.5 * h) * k, k
+
+
+def fill_right(C, total, at, rows, v):
+    for i, c in ((0, 0), (1, 1), (2, 2), (3, 3), (4, 4), (10, 5), (11, 6)):
+        C[i * total + at:i * total + at + rows] = v[c]
+
+
+def clear_right(C, total):
+    zero = jnp.zeros((total, W128), f32)
+    for i in (5, 6, 7, 8, 9, 12):
+        C[i * total:(i + 1) * total] = zero
+
+
+def fill_left(CA, v):
+    for i, w in enumerate((-2.0 * v[0], -2.0 * v[1], -2.0 * v[2], v[4], v[3], v[6], v[5], jnp.zeros_like(v[0]))):
+        CA[i * NB:(i + 1) * NB] = w
+
+
+def right_features(C, total, b, BF, at):
+    for w, c in ((0, 0), (5, W128)):
+        p = split3(C[pl.ds(w * total + b, 8, stride=total), :])
+        BF[at, :, c:c + W128] = jnp.concatenate([p[q] for _, q in CHUNKS], 0).astype(bf16)
+
+
+def left_features(CA, b, AF, at):
+    p = split3(CA[pl.ds(b, 8, stride=NB), :])
+    AF[at] = jnp.concatenate([p[q] for q, _ in CHUNKS], 0).T.astype(bf16)
+
+
+def forward_kernel(send_list, count, pairs, pos, mass, smoothing, level, ghost_o, idx, hot_o, pos_o, smooth_o, self_o, tiles_o,
+                   buf, hot, C, CA, AF, BF, GB, tiles, send_sem, recv_sem, tile_sem):
+    lev = level[...]
+    scale = jnp.where(lev == 0, 1.0, jnp.where(lev == 1, SHRINK, SHRINK * SHRINK)).astype(f32)
+    smooth_o[...] = smoothing[...] * jnp.broadcast_to(scale, (NB, W128)).T
+    for c in range(3):
+        pos_o[c] = pos[:, c, :]
+    lane = lax.broadcasted_iota(jnp.int32, (1, NB), 1)
+
+    def gather(n, _):
+        for g in range(SLOTS):
+            t = send_list[0, n, g]
+            for c in range(3):
+                buf[n, c, g:g + 1, :] = pos_o[c, pl.ds(t, 1), :]
+            buf[n, 3, g:g + 1, :] = mass[pl.ds(t, 1), :]
+            buf[n, 4, g:g + 1, :] = smooth_o[pl.ds(t, 1), :]
+            hot[pl.ds(n * SLOTS + g, 1), :] = jnp.where(lane == t, 1.0, 0.0)
+        return 0
+
+    hot[GHOSTS:] = jnp.zeros((2 * W128 - GHOSTS, W128), f32)
+    lax.fori_loop(0, NEIGH, gather, 0)
+    meet()
+    copies = start_all(buf, ghost_o, send_sem, recv_sem, 1)
+    count_pairs = pairs.shape[2]
+    live = lax.broadcasted_iota(jnp.int32, (1, count_pairs), 1) < count[0]
+    idx[...] = jnp.zeros_like(idx)
+    first = pairs[0, 0:1, :]
+    second = pairs[0, 1:2, :]
+    idx[0:1, :count_pairs] = first
+    idx[1:2, :count_pairs] = second
+    idx[2:3, :count_pairs] = jnp.where(live, first, NB)
+    idx[3:4, :count_pairs] = jnp.where(live, second, EXT)
+    for i in range(2):
+        hot_o[:, i * W128:(i + 1) * W128] = hot[i * W128:(i + 1) * W128].T.astype(bf16)
+    v = scaled_columns(pos_o[0], pos_o[1], pos_o[2], mass[...], smooth_o[...])
+    clear_right(C, NB)
+    fill_right(C, NB, 0, NB, v)
+    fill_left(CA, v)
+
+    def features(g):
+        for j in range(SELF):
+            right_features(C, NB, g * SELF + j, BF, j)
+            left_features(CA, g * SELF + j, AF, j)
+
+    def products():
+        for j in range(SELF):
+            GB[j] = jnp.dot(AF[j], BF[j], preferred_element_type=f32)
+
+    features(0)
+    products()
+    features(1)
+
+    def body(g, _):
+        for j in range(SELF):
+            part = jnp.zeros((8, W128), f32)
+            for r in range(0, W128, 8):
+                W, S = tile_math(GB[j, r:r + 8, :W128], GB[j, r:r + 8, W128:])
+                tiles[g * SELF + j, r:r + 8] = S
+                part = part + W
+            self_o[pl.ds(g * SELF + j, 1), :] = jnp.sum(part, axis=0, keepdims=True)
+        pltpu.make_async_copy(tiles.at[pl.ds(g * SELF, SELF)], tiles_o.at[pl.ds(g * SELF, SELF)], tile_sem.at[g]).start()
+        products()
+        features(jnp.minimum(g + 2, NB // SELF - 1))
+        return 0
+
+    lax.fori_loop(0, NB // SELF, body, 0)
+
+    def landed(g, _):
+        pltpu.make_async_copy(tiles.at[pl.ds(g * SELF, SELF)], tiles_o.at[pl.ds(g * SELF, SELF)], tile_sem.at[g]).wait()
+        return 0
+
+    lax.fori_loop(0, NB // SELF, landed, 0)
+    for copy in copies:
+        copy.wait()
+
+
+def density_pairs(idx, pos, mass, smooth, ghost, self_sum, dens_o, dens_g, tiles, C, CA, AF, BF, GB, acc_a, acc_b):
     step = pl.program_id(0)
 
     def first_stage(k, j):
@@ -143,36 +219,17 @@
 
     @pl.when(step == 0)
     def _():
-        zero = jnp.zeros((EXT, W128), f32)
-        for i in (5, 6, 7, 8, 9, 12):
-            C[i * EXT:(i + 1) * EXT] = zero
-        CA[7 * NB:8 * NB] = zero[:NB]
-
-        def columns(x, y, z, m, h):
-            k = inverse_cube_root(m)
-            k2 = k * k
-            return x * k2, y * k2, z * k2, k2, (x * x + y * y + z * z) * k2, (0.5 * h) * k, k
-
-        def fill(at, rows, v):
-            for i, c in ((0, 0), (1, 1), (2, 2), (3, 3), (4, 4), (10, 5), (11, 6)):
-                C[i * EXT + at:i * EXT + at + rows] = v[c]
-
-        v = columns(pos[0], pos[1], pos[2], mass[...], smooth[...])
-        fill(0, NB, v)
-        for i, w in enumerate((-2.0 * v[0], -2.0 * v[1], -2.0 * v[2], v[4], v[3])):
-            CA[i * NB:(i + 1) * NB] = w
-        CA[5 * NB:6 * NB] = v[6]
-        CA[6 * NB:7 * NB] = v[5]
+        v = scaled_columns(pos[0], pos[1], pos[2], mass[...], smooth[...])
+        clear_right(C, EXT)
+        fill_right(C, EXT, 0, NB, v)
+        fill_left(CA, v)
         for n in range(NEIGH):
-            fill(NB + n * SLOTS, SLOTS, columns(*[ghost[n, c] for c in range(5)]))
+            fill_right(C, EXT, NB + n * SLOTS, SLOTS, scaled_columns(*[ghost[n, c] for c in range(5)]))
         acc_b[...] = jnp.zeros_like(acc_b)
 
         def right_side(i, _):
             for j in range(4):
-                b = i * 4 + j
-                for w, c in ((0, 0), (5, W128)):
-                    p = split3(C[pl.ds(w * EXT + b, 8, stride=EXT), :])
-                    BF[b, :, c:c + W128] = jnp.concatenate([p[q] for _, q in CHUNKS], 0).astype(bf16)
+                right_features(C, EXT, i * 4 + j, BF, i * 4 + j)
             return 0
 
         lax.fori_loop(0, EXT // 4, right_side, 0)
@@ -180,8 +237,7 @@
         def left_side(i, _):
             for j in range(8):
                 b = i * 8 + j
-                p = split3(CA[pl.ds(b, 8, stride=NB), :])
-                AF[b] = jnp.concatenate([p[q] for q, _ in CHUNKS], 0).T.astype(bf16)
+                left_features(CA, b, AF, b)
                 acc_a[b] = jnp.zeros((W128, W128), f32)
             return 0
 
@@ -229,19 +285,18 @@
                 v = v + acc_b[pl.ds(i * 64 + s, 8, stride=8), :]
             if i < NB // 8:
                 r = slice(i * 8, i * 8 + 8)
-                dens_o[r] = (dens_o[r] + v) * (4.0 * NORM) / mass[r]
+                dens_o[r] = (dens_o[r] + (v + self_sum[r])) * (4.0 * NORM) / mass[r]
             else:
                 n = i - NB // 8
                 dens_g[n] = v * (4.0 * NORM) / ghost[n, 3]
 
 
-def density_kernel(send_list, which, part, gpart, energy, dens_o, press_o, gpress_o, ret, buf, s1, r1, s2, r2):
+def density_kernel(send_list, hot, part, gpart, energy, dens_o, press_o, gpress_o, ret, buf, s1, r1, s2, r2):
     meet()
     copies = start_all(gpart, ret, s1, r1, -1)
-    hot = one_hot(which)
     for copy in copies:
         copy.wait()
-    dens = part[...] + split_dot(hot, ret[...].reshape(GHOSTS, W128))
+    dens = part[...] + split_dot(hot[:, :GHOSTS], ret[...].reshape(GHOSTS, W128))
     dens_o[...] = dens
     press_o[...] = GAMMA_LESS * energy[...] / dens
 
@@ -255,7 +310,7 @@
         copy.wait()
 
 
-def force_pairs(idx, pos, mass, ghost, press, gpress, tiles, acc_o, acc_g, C, MM, acc):
+def force_pairs(idx, pos, mass, ghost, press, gpress, tiles, own_tiles, acc_o, acc_g, C, MM, acc):
     step = pl.program_id(0)
 
     @pl.when(step == 0)
@@ -300,6 +355,17 @@
             acc[i] += v[:8] + v[8:]
         return 0
 
+    def own_body(u, _):
+        sums = []
+        for j in range(SELF):
+            a = step * own_tiles.shape[0] + u * SELF + j
+            hi, lo = hilo(own_tiles[u * SELF + j])
+            sums.append((a, jnp.dot(MM[a], jnp.concatenate([hi, lo], 0), preferred_element_type=f32)))
+        for a, v in sums:
+            acc[a] += v[:8] + v[8:]
+        return 0
+
+    lax.fori_loop(0, own_tiles.shape[0] // SELF, own_body, 0)
     lax.fori_loop(0, FORCE_STEP // FORCE_UNROLL, body, 0)
 
     @pl.when(step == pl.num_programs(0) - 1)
@@ -323,14 +389,13 @@
                     acc_g[n, c] = v
 
 
-def force_kernel(which, part, gpart, acc_o, ret, s1, r1):
+def force_kernel(hot, part, gpart, acc_o, ret, s1, r1):
     meet()
     copies = start_all(gpart, ret, s1, r1, -1)
-    hot = one_hot(which)
     for copy in copies:
         copy.wait()
     for c in range(3):
-        acc_o[c] = part[c] + split_dot(hot, ret[:, c].reshape(GHOSTS, W128))
+        acc_o[:, c, :] = part[c] + split_dot(hot[:, :GHOSTS], ret[:, c].reshape(GHOSTS, W128))
 
 
 V = pl.BlockSpec(memory_space=pltpu.VMEM)
@@ -339,69 +404,79 @@
 
 
 def exchange_params(number):
-    return pltpu.CompilerParams(collective_id=number, has_side_effects=True)
-
-
-def run_density(idx, pos, mass, smooth, ghost, units):
+    return pltpu.CompilerParams(collective_id=number, has_side_effects=True, vmem_limit_bytes=VMEM)
+
+
+def run_forward(send_list, pair_count, pair_list, pos, mass, smoothing, level):
+    D = pltpu.SemaphoreType.DMA((NEIGH,))
+    slots = pair_list.shape[2] + 2 * W128 - pair_list.shape[2] % W128
+    vm = pltpu.VMEM
+    return pl.pallas_call(
+        forward_kernel,
+        out_shape=[
+            sds((NEIGH, 5, SLOTS, W128), f32), sds((4, slots), jnp.int32), sds((NB, 2 * W128), bf16),
+            sds((3, NB, W128), f32), sds((NB, W128), f32), sds((NB, W128), f32), sds((NB, W128, W128), f32)],
+        in_specs=[SM, SM, V, V, V, V, V], out_specs=[V] * 6 + [pl.BlockSpec(memory_space=pl.ANY)],
+        scratch_shapes=[
+            vm((NEIGH, 5, SLOTS, W128), f32), vm((2 * W128, W128), f32), vm((13 * NB, W128), f32), vm((8 * NB, W128), f32),
+            vm((SELF, W128, 64), bf16), vm((SELF, 64, 2 * W128), bf16), vm((SELF, W128, 2 * W128), f32),
+            vm((NB, W128, W128), f32), D, D, pltpu.SemaphoreType.DMA((NB // SELF,))],
+        compiler_params=pltpu.CompilerParams(collective_id=0, has_side_effects=True, vmem_limit_bytes=VMEM),
+        name="forward")(send_list, pair_count, pair_list, pos, mass, smoothing, level)
+
+
+def run_density(idx, pos, mass, smooth, ghost, self_sum, pairs):
+    vm = pltpu.VMEM
     return pl.pallas_call(
         density_pairs,
         grid_spec=pltpu.PrefetchScalarGridSpec(
-            num_scalar_prefetch=1, grid=(units // UNITS_STEP,), in_specs=[V] * 4,
+            num_scalar_prefetch=1, grid=(pairs // UNITS_STEP,), in_specs=[V] * 5,
             out_specs=[V, V, pl.BlockSpec((UNITS_STEP, W128, W128), lambda i, *_: (i, 0, 0))],
             scratch_shapes=[
-                pltpu.VMEM((13 * EXT, W128), f32), pltpu.VMEM((8 * NB, W128), f32),
-                pltpu.VMEM((NB, W128, 64), bf16), pltpu.VMEM((EXT, 64, 2 * W128), bf16),
-                pltpu.VMEM((UNROLL, W128, 2 * W128), f32), pltpu.VMEM((NB + 1, W128, W128), f32),
-                pltpu.VMEM(((EXT + 1) * 8, W128), f32)]),
-        out_shape=[sds((NB, W128), f32), sds((NEIGH, SLOTS, W128), f32), sds((units, W128, W128), f32)],
-        compiler_params=pltpu.CompilerParams(vmem_limit_bytes=60 * 2**20),
-        name="density_pairs")(idx, pos, mass, smooth, ghost)
-
-
-def run_force(idx, pos, mass, ghost, press, gpress, tiles):
+                vm((13 * EXT, W128), f32), vm((8 * NB, W128), f32), vm((NB, W128, 64), bf16), vm((EXT, 64, 2 * W128), bf16),
+                vm((UNROLL, W128, 2 * W128), f32), vm((NB + 1, W128, W128), f32), vm(((EXT + 1) * 8, W128), f32)]),
+        out_shape=[sds((NB, W128), f32), sds((NEIGH, SLOTS, W128), f32), sds((pairs, W128, W128), f32)],
+        compiler_params=pltpu.CompilerParams(vmem_limit_bytes=VMEM),
+        name="density_pairs")(idx, pos, mass, smooth, ghost, self_sum)
+
+
+def run_force(idx, pos, mass, ghost, press, gpress, tiles, own_tiles):
+    steps = tiles.shape[0] // FORCE_STEP
+    vm = pltpu.VMEM
     return pl.pallas_call(
         force_pairs,
         grid_spec=pltpu.PrefetchScalarGridSpec(
-            num_scalar_prefetch=1, grid=(tiles.shape[0] // FORCE_STEP,),
-            in_specs=[V] * 5 + [pl.BlockSpec((FORCE_STEP, W128, W128), lambda i, *_: (i, 0, 0))],
+            num_scalar_prefetch=1, grid=(steps,),
+            in_specs=[V] * 5 + [pl.BlockSpec((FORCE_STEP, W128, W128), lambda i, *_: (i, 0, 0)),
+                                pl.BlockSpec((NB // steps, W128, W128), lambda i, *_: (i, 0, 0))],
             out_specs=[V, V],
-            scratch_shapes=[
-                pltpu.VMEM((8 * EXT, W128), f32), pltpu.VMEM((EXT, 16, 2 * W128), bf16),
-                pltpu.VMEM((EXT + 1, 8, W128), f32)]),
+            scratch_shapes=[vm((8 * EXT, W128), f32), vm((EXT, 16, 2 * W128), bf16), vm((EXT + 1, 8, W128), f32)]),
         out_shape=[sds((3, NB, W128), f32), sds((NEIGH, 3, SLOTS, W128), f32)],
-        compiler_params=pltpu.CompilerParams(vmem_limit_bytes=60 * 2**20),
-        name="force_pairs")(idx, pos, mass, ghost, press, gpress, tiles)
+        compiler_params=pltpu.CompilerParams(vmem_limit_bytes=VMEM),
+        name="force_pairs")(idx, pos, mass, ghost, press, gpress, tiles, own_tiles)
 
 
 def per_device(positions, masses, smoothing, energy, level_ids, send_list, pair_list, pair_count):
     D = pltpu.SemaphoreType.DMA((NEIGH,))
-    units = NB + pair_list.shape[2]
-    pos = positions.reshape(3, NB, W128)
+    vm = pltpu.VMEM
     mass = masses.reshape(NB, W128)
-    level = level_ids[:, None]
-    scale = jnp.where(level == 0, 1.0, jnp.where(level == 1, SHRINK, SHRINK * SHRINK)).astype(f32)
-    smooth = smoothing.reshape(NB, W128) * scale
-    which = send_list.reshape(1, GHOSTS)
-    ghost, idx = pl.pallas_call(
-        forward_kernel,
-        out_shape=[sds((NEIGH, 5, SLOTS, W128), f32), sds((4, units + 2 * W128 - units % W128), jnp.int32)],
-        in_specs=[SM, V, SM, V, V, V], out_specs=[V, V],
-        scratch_shapes=[pltpu.VMEM((NEIGH, 5, SLOTS, W128), f32), D, D],
-        compiler_params=exchange_params(0), name="forward")(send_list, pair_list, pair_count, pos, mass, smooth)
-    dens, gdens, tiles = run_density(idx, pos, mass, smooth, ghost, units)
+    ghost, idx, hot, pos, smooth, self_sum, own_tiles = run_forward(
+        send_list, pair_count, pair_list, positions.reshape(3, NB, W128).transpose(1, 0, 2), mass,
+        smoothing.reshape(NB, W128), level_ids.reshape(1, NB))
+    dens, gdens, tiles = run_density(idx, pos, mass, smooth, ghost, self_sum, pair_list.shape[2])
     density, press, gpress = pl.pallas_call(
         density_kernel,
         out_shape=[sds((NB, W128), f32), sds((NB, W128), f32), sds((NEIGH, SLOTS, W128), f32)],
         in_specs=[SM, V, V, V, V], out_specs=[V, V, V],
-        scratch_shapes=[pltpu.VMEM((NEIGH, SLOTS, W128), f32), pltpu.VMEM((NEIGH, SLOTS, W128), f32), D, D, D, D],
+        scratch_shapes=[vm((NEIGH, SLOTS, W128), f32), vm((NEIGH, SLOTS, W128), f32), D, D, D, D],
         compiler_params=exchange_params(1), name="density")(
-            send_list, which, dens, gdens, energy.reshape(NB, W128))
-    acc, gacc = run_force(idx, pos, mass, ghost, press, gpress, tiles)
+            send_list, hot, dens, gdens, energy.reshape(NB, W128))
+    acc, gacc = run_force(idx, pos, mass, ghost, press, gpress, tiles, own_tiles)
     accel = pl.pallas_call(
-        force_kernel, out_shape=sds((3, NB, W128), f32), in_specs=[V, V, V], out_specs=V,
-        scratch_shapes=[pltpu.VMEM((NEIGH, 3, SLOTS, W128), f32), D, D],
-        compiler_params=exchange_params(2), name="force")(which, acc, gacc)
-    return density.reshape(NB * W128), accel.reshape(3, NB * W128)
+        force_kernel, out_shape=sds((NB, 3, W128), f32), in_specs=[V, V, V], out_specs=V,
+        scratch_shapes=[vm((NEIGH, 3, SLOTS, W128), f32), D, D],
+        compiler_params=exchange_params(2), name="force")(hot, acc, gacc)
+    return density.reshape(NB * W128), accel.transpose(1, 0, 2).reshape(3, NB * W128)
 
 
 def solution(mesh):

time: 149 us -> 139 us (0.933)
  Pallas kernels: 139 us -> 134 us
  other arithmetic: 2.21 us -> 0 us
  local copies, waits for them, and re-layouts: 5.5 us -> 3.7 us
    pallas_call x1, Pallas kernels: 53.8 us -> 47.8 us  [run_density(): pl.pallas_call(density_pairs, grid_spec=pltpu.PrefetchScalarGridSpec(num_...]
    pallas_call x2, Pallas kernels: 31.9 us -> 34.3 us  [the longest x1 21.8 us: run_forward(): pl.pallas_call(forward_kernel, out_shape=[sds((NEIGH, 5, SLOTS, W128), f3...]
    pallas_call x1, Pallas kernels: 18.4 us -> 16.7 us  [per_device(): pl.pallas_call(density_kernel, out_shape=[sds((NB, W128), f32), sds((NB,...]
    mul x1 -> x0, other arithmetic: 1.55 us -> none  [per_device(): smooth = smoothing.reshape(NB, W128) * scale]
    unnamed x8 -> x5, local copies, waits for them, and re-layouts: 4.84 us -> 3.7 us
where the time goes in v3:
time: 139 us
  Pallas kernels  134 us (96%)
  local copies, waits for them, and re-layouts  3.7 us (3%)
    pallas_call x1, Pallas kernels, run_density(): pl.pallas_call(density_pairs, grid_spec=pltpu.PrefetchScalarGridSpec(num_...  47.8 us
    pallas_call x1, Pallas kernels, run_force(): pl.pallas_call(force_pairs, grid_spec=pltpu.PrefetchScalarGridSpec(num_sc...  35 us
    pallas_call x1, Pallas kernels, run_forward(): pl.pallas_call(forward_kernel, out_shape=[sds((NEIGH, 5, SLOTS, W128), f3...  21.8 us
    pallas_call x1, Pallas kernels, per_device(): pl.pallas_call(density_kernel, out_shape=[sds((NB, W128), f32), sds((NB,...  16.7 us
    pallas_call x1, Pallas kernels, per_device(): pl.pallas_call(force_kernel, out_shape=sds((NB, 3, W128), f32), in_specs=...  12.5 us
    unnamed x5, local copies, waits for them, and re-layouts  3.7 us

profile of v3, /device:TPU:1, one launch (start us, length us, event | category | flops | bytes accessed | tf_op | source)
XLA Modules:
  0.0 138.8 jit_solution(15490303448910275561)
XLA Ops:
  0.6 1.4 copy.11.send_list
  2.6 21.8 %forward.1 = (f32[20,5,8,128]{3,2,1,0:T(8,128)}, s32[4,896]{1,0:T(4,128)}, bf16[128,256]{1,0:T(8,128)(2,1)}, f32[3,128,128]{2,1,0:T(8,128)}, f32[128,128]{1,0:T(...) custom-call(s32[1,20,8]{2,1,0:T(8,128)} %copy.11.send_list, s32[1]{0:T(128)S(6)} %copy.14.count, ...), custom_call_target="tpu_custom_call" | custom-call | tf_op jit(solution)/shard_map/forward/pallas_call | solution.py:414
  24.5 47.8 %density_pairs.1 = (f32[128,128]{1,0:T(8,128)}, f32[20,8,128]{2,1,0:T(8,128)}, f32[672,128,128]{2,1,0:T(8,128)}) custom-call(s32[4,896]{1,0:T(4,128)} %get-tuple-element.18.idx, f32[3,128,128]{2,1,0:T(8,128)} %get-tuple-element.19.pos, f32[128,128]{1,0:T(8,128)} %bitcast.13, f32[128,128]{1,0:T(8,128)} %get-tuple-element.20.smooth, ...), custom_call_target="tpu_custom_call" | custom-call | tf_op jit(solution)/shard_map/density_pairs/pallas_call | solution.py:430
  72.2 16.7 %density.1 = (f32[128,128]{1,0:T(8,128)}, f32[128,128]{1,0:T(8,128)}, f32[20,8,128]{2,1,0:T(8,128)}) custom-call(s32[1,20,8]{2,1,0:T(8,128)} %copy.11.send_list, bf16[128,256]{1,0:T(8,128)(2,1)} %get-tuple-element.17.hot, f32[128,128]{1,0:T(8,128)} %get-tuple-element.23.part, f32[20,8,128]{2,1,0:T(8,128)} %get-tuple-element.24.gpart, f32[128,128]{1,0:T(8,128)} %bitcast.18), custom_call_target="tpu_custom_call" | custom-call | tf_op jit(solution)/shard_map/density/pallas_call | solution.py:467
  88.9 0.0 copy-start
  88.9 35.0 %force_pairs.1 = (f32[3,128,128]{2,1,0:T(8,128)}, f32[20,3,8,128]{3,2,1,0:T(8,128)}) custom-call(s32[4,896]{1,0:T(4,128)} %get-tuple-element.18.idx, f32[3,128,128]{2,1,0:T(8,128)} %get-tuple-element.19.pos, f32[128,128]{1,0:T(8,128)} %bitcast.14, f32[20,5,8,128]{3,2,1,0:T(8,128)} %get-tuple-element.21.ghost, f32[128,128]{1,0:T(8,128)} %get-tuple-element.26.press, ...), custom_call_target="tpu_custom_call" | custom-call | tf_op jit(solution)/shard_map/force_pairs/pallas_call | solution.py:446
  123.9 12.5 %force.1 = f32[128,3,128]{2,1,0:T(4,128)} custom-call(bf16[128,256]{1,0:T(8,128)(2,1)} %get-tuple-element.17.hot, f32[3,128,128]{2,1,0:T(8,128)} %get-tuple-element.30.part, f32[20,3,8,128]{3,2,1,0:T(8,128)} %get-tuple-element.31.gpart), custom_call_target="tpu_custom_call" | custom-call | tf_op jit(solution)/shard_map/force/pallas_call | solution.py:475
  136.4 0.0 copy-done
  136.4 0.6 copy.15
  137.1 1.7 %copy.16 = f32[3,16384]{1,0:T(4,128)} copy(f32[3,16384]{1,0:T(4,128)} %bitcast.11) | data formatting | bytes 393216
Async XLA Ops:
  88.9 47.5 %copy-start = (f32[128,128]{1,0:T(8,128)S(1)}, f32[128,128]{1,0:T(8,128)}, u32[]{:S(2)}) copy-start(f32[128,128]{1,0:T(8,128)} %get-tuple-element.25) | copy-start | bytes 196612

commit v4 on v3

--- a/solution.py
+++ b/solution.py
@@ -23,8 +23,9 @@
 CHUNKS = [(0, 0), (0, 1), (1, 0), (1, 1), (0, 2), (2, 0), (1, 2), (2, 1)]
 UNITS_STEP = 32
 UNROLL = 16
-FORCE_STEP = 84
+CHUNK = 84
 FORCE_UNROLL = 14
+EARLY = 2
 SELF = 8
 VMEM = 63 * 2**20
 
@@ -161,6 +162,7 @@
     count_pairs = pairs.shape[2]
     live = lax.broadcasted_iota(jnp.int32, (1, count_pairs), 1) < count[0]
     idx[...] = jnp.zeros_like(idx)
+    idx[2:4, :] = jnp.full((2, idx.shape[1]), EXT, jnp.int32)
     first = pairs[0, 0:1, :]
     second = pairs[0, 1:2, :]
     idx[0:1, :count_pairs] = first
@@ -291,120 +293,160 @@
                 dens_g[n] = v * (4.0 * NORM) / ghost[n, 3]
 
 
-def density_kernel(send_list, hot, part, gpart, energy, dens_o, press_o, gpress_o, ret, buf, s1, r1, s2, r2):
+def back_kernel(idx, send_list, idx_v, hot, pos, mass, ghost, part, gpart, energy, tiles_h, own_h, dens_o, acc_o,
+                T, R, RS, MM, C, hot_a, hot_b, press, gpress, ret, buf, gacc, racc,
+                tile_sem, s1, r1, s2, r2, s3, r3):
+    pairs = tiles_h.shape[0]
+    chunks = pairs // CHUNK
+    tail = chunks - 2
+
+    def tile_copy(c):
+        at = pl.ds(c * CHUNK, CHUNK)
+        return pltpu.make_async_copy(tiles_h.at[at], T.at[at], tile_sem.at[c])
+
+    own_at = pl.ds(tail * CHUNK, NB)
+    own_copy = pltpu.make_async_copy(own_h, T.at[own_at], tile_sem.at[chunks])
+    own_copy.start()
+    for c in range(tail):
+        tile_copy(c).start()
     meet()
     copies = start_all(gpart, ret, s1, r1, -1)
+
+    slots = R.shape[0] // 16
+    R[pairs * 8:slots * 8] = jnp.zeros(((slots - pairs) * 8, W128), f32)
+    R[(slots + pairs) * 8:] = jnp.zeros(((slots - pairs) * 8, W128), f32)
+    for w in range(slots // W128):
+        at = slice(w * W128, (w + 1) * W128)
+        for matrix, row in ((hot_a, 2), (hot_b, 3)):
+            rows = matrix.shape[0]
+            which = idx_v[row:row + 1, at]
+            blocks = lax.broadcasted_iota(jnp.int32, (rows, W128), 0)
+            matrix[:, at] = jnp.where(blocks == which, 1.0, 0.0).astype(bf16)
+
+    def weights(at, rows, x, y, z, m, p):
+        k = inverse_cube_root(m)
+        w = k * k
+        pw = p * w
+        for i, v in enumerate((w, w * x, w * y, w * z, pw, pw * x, pw * y, pw * z)):
+            C[i * EXT + at:i * EXT + at + rows] = v
+
+    def columns(i, _):
+        for j in range(4):
+            b = i * 4 + j
+            v = C[pl.ds(b, 8, stride=EXT), :]
+            hi = v.astype(bf16).astype(f32)
+            mm = jnp.concatenate([hi, v - hi], 0).astype(bf16)
+            MM[b, :, :W128] = mm
+            MM[b, :, W128:] = mm
+        return 0
+
     for copy in copies:
         copy.wait()
     dens = part[...] + split_dot(hot[:, :GHOSTS], ret[...].reshape(GHOSTS, W128))
     dens_o[...] = dens
-    press_o[...] = GAMMA_LESS * energy[...] / dens
+    press[...] = GAMMA_LESS * energy[...] / dens
 
     def gather(n, _):
         for g in range(SLOTS):
-            buf[n, g:g + 1, :] = press_o[pl.ds(send_list[0, n, g], 1), :]
+            buf[n, g:g + 1, :] = press[pl.ds(send_list[0, n, g], 1), :]
         return 0
 
     lax.fori_loop(0, NEIGH, gather, 0)
-    for copy in start_all(buf, gpress_o, s2, r2, 1):
+    copies = start_all(buf, gpress, s2, r2, 1)
+
+    weights(0, NB, pos[0], pos[1], pos[2], mass[...], press[...])
+    lax.fori_loop(0, NB // 4, columns, 0)
+
+    def to_b(k, hi, lo):
+        return jnp.dot(MM[idx[0, k]], jnp.concatenate([hi, lo], 0), preferred_element_type=f32)
+
+    def to_a(k, hi, lo):
+        return lax.dot_general(MM[idx[1, k]], jnp.concatenate([hi, lo], 1), (((1,), (1,)), ((), ())),
+                               preferred_element_type=f32)
+
+    def put(ref, k, v):
+        ref[pl.ds(pl.multiple_of(k * 8, 8), 8), :] = v[:8] + v[8:]
+
+    def own_body(u, _):
+        out = []
+        for j in range(16):
+            a = u * 16 + j
+            hi, lo = hilo(T[tail * CHUNK + a])
+            out.append((a, jnp.dot(MM[a], jnp.concatenate([hi, lo], 0), preferred_element_type=f32)))
+        for a, v in out:
+            put(RS, a, v)
+        return 0
+
+    def pair_body(do_a, do_b, u, _):
+        out = []
+        for j in range(FORCE_UNROLL):
+            k = u * FORCE_UNROLL + j
+            hi, lo = hilo(T[k])
+            if do_b:
+                out.append((slots + k, to_b(k, hi, lo)))
+            if do_a:
+                out.append((k, to_a(k, hi, lo)))
+        for k, v in out:
+            put(R, k, v)
+        return 0
+
+    per = CHUNK // FORCE_UNROLL
+    own_copy.wait()
+    lax.fori_loop(0, NB // 16, own_body, 0)
+    for c in range(tail, chunks):
+        tile_copy(c).start()
+    for c in range(EARLY):
+        tile_copy(c).wait()
+    lax.fori_loop(0, EARLY * per, functools.partial(pair_body, False, True), 0)
+    for copy in copies:
         copy.wait()
-
-
-def force_pairs(idx, pos, mass, ghost, press, gpress, tiles, own_tiles, acc_o, acc_g, C, MM, acc):
-    step = pl.program_id(0)
-
-    @pl.when(step == 0)
-    def _():
-        def fill(at, rows, x, y, z, m, p):
-            k = inverse_cube_root(m)
-            w = k * k
-            pw = p * w
-            for i, v in enumerate((w, w * x, w * y, w * z, pw, pw * x, pw * y, pw * z)):
-                C[i * EXT + at:i * EXT + at + rows] = v
-
-        fill(0, NB, pos[0], pos[1], pos[2], mass[...], press[...])
-        for n in range(NEIGH):
-            fill(NB + n * SLOTS, SLOTS, *[ghost[n, c] for c in range(4)], gpress[n])
-        acc[...] = jnp.zeros_like(acc)
-
-        def columns(i, _):
-            for j in range(4):
-                b = i * 4 + j
-                v = C[pl.ds(b, 8, stride=EXT), :]
-                hi = v.astype(bf16).astype(f32)
-                mm = jnp.concatenate([hi, v - hi], 0).astype(bf16)
-                MM[b, :, :W128] = mm
-                MM[b, :, W128:] = mm
-            return 0
-
-        lax.fori_loop(0, EXT // 4, columns, 0)
-
-    def body(u, _):
-        sums = []
-        for j in range(FORCE_UNROLL):
-            k = step * FORCE_STEP + u * FORCE_UNROLL + j
-            hi, lo = hilo(tiles[u * FORCE_UNROLL + j])
-            to_b = jnp.dot(MM[idx[0, k]], jnp.concatenate([hi, lo], 0), preferred_element_type=f32)
-            to_a = lax.dot_general(MM[idx[1, k]], jnp.concatenate([hi, lo], 1), (((1,), (1,)), ((), ())),
-                                   preferred_element_type=f32)
-            sums.append((idx[2, k], to_a))
-            sums.append((idx[3, k], to_b))
-        for n, (i, v) in enumerate(sums):
-            if n % 2 == 0:
-                i = jnp.where(i == NB, EXT, i)
-            acc[i] += v[:8] + v[8:]
-        return 0
-
-    def own_body(u, _):
-        sums = []
-        for j in range(SELF):
-            a = step * own_tiles.shape[0] + u * SELF + j
-            hi, lo = hilo(own_tiles[u * SELF + j])
-            sums.append((a, jnp.dot(MM[a], jnp.concatenate([hi, lo], 0), preferred_element_type=f32)))
-        for a, v in sums:
-            acc[a] += v[:8] + v[8:]
-        return 0
-
-    lax.fori_loop(0, own_tiles.shape[0] // SELF, own_body, 0)
-    lax.fori_loop(0, FORCE_STEP // FORCE_UNROLL, body, 0)
-
-    @pl.when(step == pl.num_programs(0) - 1)
-    def _():
-        def final(p, m, spot, A):
-            k = inverse_cube_root(m)
-            k2 = k * k
-            scale = (-20.0 * NORM) * (k2 * k2 * k)
-            own = p * A[0] + A[4]
-            return [(p * A[c + 1] + A[c + 5] - v * own) * scale for c, v in enumerate(spot)]
-
-        for i in range(EXT // 8):
-            r = slice(i * 8, i * 8 + 8)
-            A = [acc[r, c, :] for c in range(8)]
-            if i < NB // 8:
-                for c, v in enumerate(final(press[r], mass[r], [pos[c, r] for c in range(3)], A)):
-                    acc_o[c, r] = v
-            else:
-                n = i - NB // 8
-                for c, v in enumerate(final(gpress[n], ghost[n, 3], [ghost[n, c] for c in range(3)], A)):
-                    acc_g[n, c] = v
-
-
-def force_kernel(hot, part, gpart, acc_o, ret, s1, r1):
-    meet()
-    copies = start_all(gpart, ret, s1, r1, -1)
+    for n in range(NEIGH):
+        weights(NB + n * SLOTS, SLOTS, *[ghost[n, c] for c in range(4)], gpress[n])
+    lax.fori_loop(NB // 4, EXT // 4, columns, 0)
+    lax.fori_loop(0, EARLY * per, functools.partial(pair_body, True, False), 0)
+
+    def chunk_body(c, _):
+        tile_copy(c).wait()
+        lax.fori_loop(c * per, (c + 1) * per, functools.partial(pair_body, True, True), 0)
+        return 0
+
+    lax.fori_loop(EARLY, chunks, chunk_body, 0)
+
+    dot = functools.partial(jnp.dot, preferred_element_type=f32)
+    A = []
+    for c in range(0, 8, 2):
+        total = []
+        for half, matrix in ((0, hot_a), (1, hot_b)):
+            v = [R[pl.ds(half * slots * 8 + c + i, slots, stride=8), :] for i in range(2)]
+            hi, lo = hilo(jnp.concatenate(v, 1))
+            total.append(dot(matrix[...], hi) + dot(matrix[...], lo))
+        own = total[1][:NB] + total[0]
+        for i in range(2):
+            at = slice(i * W128, (i + 1) * W128)
+            A.append((own[:, at] + RS[pl.ds(c + i, NB, stride=8), :], total[1][NB:, at]))
+    scale = -20.0 * NORM
+
+    def final(p, m, spot, A):
+        k = inverse_cube_root(m)
+        k2 = k * k
+        own = p * A[0] + A[4]
+        return [(p * A[c + 1] + A[c + 5] - v * own) * (scale * (k2 * k2 * k)) for c, v in enumerate(spot)]
+
+    for n in range(NEIGH):
+        r = slice(n * SLOTS, (n + 1) * SLOTS)
+        for c, v in enumerate(final(gpress[n], ghost[n, 3], [ghost[n, c] for c in range(3)], [x[1][r] for x in A])):
+            gacc[n, c] = v
+    copies = start_all(gacc, racc, s3, r3, -1)
+    mine = final(press[...], mass[...], [pos[c] for c in range(3)], [x[0] for x in A])
     for copy in copies:
         copy.wait()
     for c in range(3):
-        acc_o[:, c, :] = part[c] + split_dot(hot[:, :GHOSTS], ret[:, c].reshape(GHOSTS, W128))
+        acc_o[:, c, :] = mine[c] + split_dot(hot[:, :GHOSTS], racc[:, c].reshape(GHOSTS, W128))
 
 
 V = pl.BlockSpec(memory_space=pltpu.VMEM)
 SM = pl.BlockSpec(memory_space=pltpu.SMEM)
 sds = jax.ShapeDtypeStruct
-
-
-def exchange_params(number):
-    return pltpu.CompilerParams(collective_id=number, has_side_effects=True, vmem_limit_bytes=VMEM)
 
 
 def run_forward(send_list, pair_count, pair_list, pos, mass, smoothing, level):
@@ -440,42 +482,34 @@
         name="density_pairs")(idx, pos, mass, smooth, ghost, self_sum)
 
 
-def run_force(idx, pos, mass, ghost, press, gpress, tiles, own_tiles):
-    steps = tiles.shape[0] // FORCE_STEP
-    vm = pltpu.VMEM
-    return pl.pallas_call(
-        force_pairs,
-        grid_spec=pltpu.PrefetchScalarGridSpec(
-            num_scalar_prefetch=1, grid=(steps,),
-            in_specs=[V] * 5 + [pl.BlockSpec((FORCE_STEP, W128, W128), lambda i, *_: (i, 0, 0)),
-                                pl.BlockSpec((NB // steps, W128, W128), lambda i, *_: (i, 0, 0))],
-            out_specs=[V, V],
-            scratch_shapes=[vm((8 * EXT, W128), f32), vm((EXT, 16, 2 * W128), bf16), vm((EXT + 1, 8, W128), f32)]),
-        out_shape=[sds((3, NB, W128), f32), sds((NEIGH, 3, SLOTS, W128), f32)],
-        compiler_params=pltpu.CompilerParams(vmem_limit_bytes=VMEM),
-        name="force_pairs")(idx, pos, mass, ghost, press, gpress, tiles, own_tiles)
-
-
-def per_device(positions, masses, smoothing, energy, level_ids, send_list, pair_list, pair_count):
+def run_back(idx, send_list, hot, pos, mass, ghost, part, gpart, energy, tiles, own_tiles):
     D = pltpu.SemaphoreType.DMA((NEIGH,))
     vm = pltpu.VMEM
+    pairs = tiles.shape[0]
+    slots = pairs + (-pairs) % (2 * W128)
+    A = pl.BlockSpec(memory_space=pl.ANY)
+    return pl.pallas_call(
+        back_kernel,
+        out_shape=[sds((NB, W128), f32), sds((NB, 3, W128), f32)],
+        in_specs=[SM, SM] + [V] * 8 + [A, A], out_specs=[V, V],
+        scratch_shapes=[
+            vm((pairs, W128, W128), f32), vm((2 * slots * 8, W128), f32), vm((NB * 8, W128), f32),
+            vm((EXT, 16, 2 * W128), bf16), vm((8 * EXT, W128), f32), vm((NB, slots), bf16), vm((EXT, slots), bf16),
+            vm((NB, W128), f32), vm((NEIGH, SLOTS, W128), f32), vm((NEIGH, SLOTS, W128), f32), vm((NEIGH, SLOTS, W128), f32),
+            vm((NEIGH, 3, SLOTS, W128), f32), vm((NEIGH, 3, SLOTS, W128), f32),
+            pltpu.SemaphoreType.DMA((pairs // CHUNK + 1,)), D, D, D, D, D, D],
+        compiler_params=pltpu.CompilerParams(collective_id=1, has_side_effects=True, vmem_limit_bytes=VMEM),
+        name="back")(idx, send_list, idx, hot, pos, mass, ghost, part, gpart, energy, tiles, own_tiles)
+
+
+def per_device(positions, masses, smoothing, energy, level_ids, send_list, pair_list, pair_count):
     mass = masses.reshape(NB, W128)
     ghost, idx, hot, pos, smooth, self_sum, own_tiles = run_forward(
         send_list, pair_count, pair_list, positions.reshape(3, NB, W128).transpose(1, 0, 2), mass,
         smoothing.reshape(NB, W128), level_ids.reshape(1, NB))
     dens, gdens, tiles = run_density(idx, pos, mass, smooth, ghost, self_sum, pair_list.shape[2])
-    density, press, gpress = pl.pallas_call(
-        density_kernel,
-        out_shape=[sds((NB, W128), f32), sds((NB, W128), f32), sds((NEIGH, SLOTS, W128), f32)],
-        in_specs=[SM, V, V, V, V], out_specs=[V, V, V],
-        scratch_shapes=[vm((NEIGH, SLOTS, W128), f32), vm((NEIGH, SLOTS, W128), f32), D, D, D, D],
-        compiler_params=exchange_params(1), name="density")(
-            send_list, hot, dens, gdens, energy.reshape(NB, W128))
-    acc, gacc = run_force(idx, pos, mass, ghost, press, gpress, tiles, own_tiles)
-    accel = pl.pallas_call(
-        force_kernel, out_shape=sds((NB, 3, W128), f32), in_specs=[V, V, V], out_specs=V,
-        scratch_shapes=[vm((NEIGH, 3, SLOTS, W128), f32), D, D],
-        compiler_params=exchange_params(2), name="force")(hot, acc, gacc)
+    density, accel = run_back(
+        idx, send_list, hot, pos, mass, ghost, dens, gdens, energy.reshape(NB, W128), tiles, own_tiles)
     return density.reshape(NB * W128), accel.transpose(1, 0, 2).reshape(3, NB * W128)
 
 

time: 139 us -> 125 us (0.90)
  Pallas kernels: 134 us -> 119 us
    pallas_call x3 -> x1, Pallas kernels: 64.2 us -> 49.7 us  [run_back(): pl.pallas_call(back_kernel, out_shape=[sds((NB, W128), f32), sds((NB, 3,...]
    unnamed x5 -> x3, local copies, waits for them, and re-layouts: 3.7 us -> 4.53 us
where the time goes in v4:
time: 125 us
  Pallas kernels  119 us (95%)
  local copies, waits for them, and re-layouts  4.53 us (4%)
  between operations  1.29 us (1%)
    pallas_call x1, Pallas kernels, run_back(): pl.pallas_call(back_kernel, out_shape=[sds((NB, W128), f32), sds((NB, 3,...  49.7 us
    pallas_call x1, Pallas kernels, run_density(): pl.pallas_call(density_pairs, grid_spec=pltpu.PrefetchScalarGridSpec(num_...  47.8 us
    pallas_call x1, Pallas kernels, run_forward(): pl.pallas_call(forward_kernel, out_shape=[sds((NEIGH, 5, SLOTS, W128), f3...  21.7 us
    unnamed x3, local copies, waits for them, and re-layouts  4.53 us

profile of v4, /device:TPU:1, one launch (start us, length us, event | category | flops | bytes accessed | tf_op | source)
XLA Modules:
  0.0 125.0 jit_solution(17023795939296232984)
XLA Ops:
  1.3 1.4 %copy.10.send_list = s32[1,20,8]{2,1,0:T(8,128)} copy(s32[1,20,8]{1,2,0:T(8,128)} %param.13) | data formatting | bytes 1280 | tf_op args[5]
  2.6 21.7 %forward.1 = (f32[20,5,8,128]{3,2,1,0:T(8,128)}, s32[4,896]{1,0:T(4,128)}, bf16[128,256]{1,0:T(8,128)(2,1)}, f32[3,128,128]{2,1,0:T(8,128)}, f32[128,128]{1,0:T(...) custom-call(s32[1,20,8]{2,1,0:T(8,128)} %copy.10.send_list, s32[1]{0:T(128)S(6)} %copy.14.count, ...), custom_call_target="tpu_custom_call" | custom-call | tf_op jit(solution)/shard_map/forward/pallas_call | solution.py:456
  24.4 47.8 %density_pairs.1 = (f32[128,128]{1,0:T(8,128)}, f32[20,8,128]{2,1,0:T(8,128)}, f32[672,128,128]{2,1,0:T(8,128)}) custom-call(s32[4,896]{1,0:T(4,128)} %get-tuple-element.14.idx.idx_v, f32[3,128,128]{2,1,0:T(8,128)} %get-tuple-element.16.pos, f32[128,128]{1,0:T(8,128)} %bitcast.12, f32[128,128]{1,0:T(8,128)} %get-tuple-element.18.smooth, ...), custom_call_target="tpu_custom_call" | custom-call | tf_op jit(solution)/shard_map/density_pairs/pallas_call | solution.py:472
  72.2 49.7 %back.1 = (f32[128,128]{1,0:T(8,128)}, f32[128,3,128]{2,1,0:T(4,128)}) custom-call(s32[4,896]{1,0:T(4,128)} %get-tuple-element.14.idx.idx_v, s32[1,20,8]{2,1,0:T(8,128)} %copy.10.send_list, s32[4,896]{1,0:T(4,128)} %get-tuple-element.14.idx.idx_v, bf16[128,256]{1,0:T(8,128)(2,1)} %get-tuple-element.15.hot, f32[3,128,128]{2,1,0:T(8,128)} %get-tuple-element.16.pos, ...), custom_call_target="tpu_custom_call" | custom-call | tf_op jit(solution)/shard_map/back/pallas_call | solution.py:491
  121.9 1.5 %copy.15 = f32[16384]{0:T(1024)} copy(f32[16384]{0:T(1024)} %bitcast.18) | data formatting | bytes 131072
  123.3 1.7 %copy.16 = f32[3,16384]{1,0:T(4,128)} copy(f32[3,16384]{1,0:T(4,128)} %bitcast.15) | data formatting | bytes 393216

commit v5 on v4

--- a/solution.py
+++ b/solution.py
@@ -21,8 +21,7 @@
 GHOSTS = NEIGH * SLOTS
 EXT = NB + GHOSTS
 CHUNKS = [(0, 0), (0, 1), (1, 0), (1, 1), (0, 2), (2, 0), (1, 2), (2, 1)]
-UNITS_STEP = 32
-UNROLL = 16
+UNROLL = 14
 CHUNK = 84
 FORCE_UNROLL = 14
 EARLY = 2
@@ -136,11 +135,22 @@
     AF[at] = jnp.concatenate([p[q] for q, _ in CHUNKS], 0).T.astype(bf16)
 
 
-def forward_kernel(send_list, count, pairs, pos, mass, smoothing, level, ghost_o, idx, hot_o, pos_o, smooth_o, self_o, tiles_o,
-                   buf, hot, C, CA, AF, BF, GB, tiles, send_sem, recv_sem, tile_sem):
+def pair_matrices(idx_v, hot_a, hot_b):
+    for w in range(hot_a.shape[1] // W128):
+        at = slice(w * W128, (w + 1) * W128)
+        for matrix, row in ((hot_a, 2), (hot_b, 3)):
+            which = idx_v[row:row + 1, at]
+            blocks = lax.broadcasted_iota(jnp.int32, (matrix.shape[0], W128), 0)
+            matrix[:, at] = jnp.where(blocks == which, 1.0, 0.0).astype(bf16)
+
+
+def front_kernel(send_list, count, pair_ends, pairs, pos, mass, smoothing, level,
+                 ghost_o, idx, hot_o, pos_o, dens_o, gdens_o, own_o, tiles_o,
+                 smooth, self_sum, buf, hot, C, CA, AF, BF, GB, own_tiles, T, RT, PB, hot_a, hot_b,
+                 send_sem, recv_sem, own_sem, tile_sem):
     lev = level[...]
     scale = jnp.where(lev == 0, 1.0, jnp.where(lev == 1, SHRINK, SHRINK * SHRINK)).astype(f32)
-    smooth_o[...] = smoothing[...] * jnp.broadcast_to(scale, (NB, W128)).T
+    smooth[...] = smoothing[...] * jnp.broadcast_to(scale, (NB, W128)).T
     for c in range(3):
         pos_o[c] = pos[:, c, :]
     lane = lax.broadcasted_iota(jnp.int32, (1, NB), 1)
@@ -151,7 +161,7 @@
             for c in range(3):
                 buf[n, c, g:g + 1, :] = pos_o[c, pl.ds(t, 1), :]
             buf[n, 3, g:g + 1, :] = mass[pl.ds(t, 1), :]
-            buf[n, 4, g:g + 1, :] = smooth_o[pl.ds(t, 1), :]
+            buf[n, 4, g:g + 1, :] = smooth[pl.ds(t, 1), :]
             hot[pl.ds(n * SLOTS + g, 1), :] = jnp.where(lane == t, 1.0, 0.0)
         return 0
 
@@ -159,138 +169,134 @@
     lax.fori_loop(0, NEIGH, gather, 0)
     meet()
     copies = start_all(buf, ghost_o, send_sem, recv_sem, 1)
-    count_pairs = pairs.shape[2]
-    live = lax.broadcasted_iota(jnp.int32, (1, count_pairs), 1) < count[0]
+
+    npairs = pairs.shape[2]
+    live = lax.broadcasted_iota(jnp.int32, (1, npairs), 1) < count[0]
     idx[...] = jnp.zeros_like(idx)
     idx[2:4, :] = jnp.full((2, idx.shape[1]), EXT, jnp.int32)
     first = pairs[0, 0:1, :]
     second = pairs[0, 1:2, :]
-    idx[0:1, :count_pairs] = first
-    idx[1:2, :count_pairs] = second
-    idx[2:3, :count_pairs] = jnp.where(live, first, NB)
-    idx[3:4, :count_pairs] = jnp.where(live, second, EXT)
+    idx[0:1, :npairs] = first
+    idx[1:2, :npairs] = second
+    idx[2:3, :npairs] = jnp.where(live, first, NB)
+    idx[3:4, :npairs] = jnp.where(live, second, EXT)
+    pair_matrices(idx, hot_a, hot_b)
     for i in range(2):
         hot_o[:, i * W128:(i + 1) * W128] = hot[i * W128:(i + 1) * W128].T.astype(bf16)
-    v = scaled_columns(pos_o[0], pos_o[1], pos_o[2], mass[...], smooth_o[...])
-    clear_right(C, NB)
-    fill_right(C, NB, 0, NB, v)
+    PB[npairs * 8:] = jnp.zeros((PB.shape[0] - npairs * 8, W128), f32)
+    RT[...] = jnp.zeros_like(RT)
+    clear_right(C, EXT)
+    v = scaled_columns(pos_o[0], pos_o[1], pos_o[2], mass[...], smooth[...])
+    fill_right(C, EXT, 0, NB, v)
     fill_left(CA, v)
 
     def features(g):
         for j in range(SELF):
-            right_features(C, NB, g * SELF + j, BF, j)
-            left_features(CA, g * SELF + j, AF, j)
-
-    def products():
-        for j in range(SELF):
-            GB[j] = jnp.dot(AF[j], BF[j], preferred_element_type=f32)
+            b = g * SELF + j
+            right_features(C, EXT, b, BF, b)
+            left_features(CA, b, AF, b)
+
+    def product(a, b, j):
+        GB[j] = jnp.dot(AF[a], BF[b], preferred_element_type=f32)
+
+    def own_copy(g):
+        at = pl.ds(g * SELF, SELF)
+        return pltpu.make_async_copy(own_tiles.at[at], own_o.at[at], own_sem.at[g])
 
     features(0)
-    products()
+    for j in range(SELF):
+        product(j, j, j)
     features(1)
 
-    def body(g, _):
+    def own_body(g, _):
+        after = jnp.minimum(g + 1, NB // SELF - 1)
         for j in range(SELF):
             part = jnp.zeros((8, W128), f32)
             for r in range(0, W128, 8):
                 W, S = tile_math(GB[j, r:r + 8, :W128], GB[j, r:r + 8, W128:])
-                tiles[g * SELF + j, r:r + 8] = S
+                own_tiles[g * SELF + j, r:r + 8] = S
                 part = part + W
-            self_o[pl.ds(g * SELF + j, 1), :] = jnp.sum(part, axis=0, keepdims=True)
-        pltpu.make_async_copy(tiles.at[pl.ds(g * SELF, SELF)], tiles_o.at[pl.ds(g * SELF, SELF)], tile_sem.at[g]).start()
-        products()
+            self_sum[pl.ds(g * SELF + j, 1), :] = jnp.sum(part, axis=0, keepdims=True)
+        own_copy(g).start()
+        for j in range(SELF):
+            product(after * SELF + j, after * SELF + j, j)
         features(jnp.minimum(g + 2, NB // SELF - 1))
         return 0
 
-    lax.fori_loop(0, NB // SELF, body, 0)
-
-    def landed(g, _):
-        pltpu.make_async_copy(tiles.at[pl.ds(g * SELF, SELF)], tiles_o.at[pl.ds(g * SELF, SELF)], tile_sem.at[g]).wait()
-        return 0
-
-    lax.fori_loop(0, NB // SELF, landed, 0)
+    lax.fori_loop(0, NB // SELF, own_body, 0)
     for copy in copies:
         copy.wait()
 
-
-def density_pairs(idx, pos, mass, smooth, ghost, self_sum, dens_o, dens_g, tiles, C, CA, AF, BF, GB, acc_a, acc_b):
-    step = pl.program_id(0)
-
-    def first_stage(k, j):
-        GB[j] = jnp.dot(AF[idx[0, k]], BF[idx[1, k]], preferred_element_type=f32)
-
-    @pl.when(step == 0)
-    def _():
-        v = scaled_columns(pos[0], pos[1], pos[2], mass[...], smooth[...])
-        clear_right(C, EXT)
-        fill_right(C, EXT, 0, NB, v)
-        fill_left(CA, v)
-        for n in range(NEIGH):
-            fill_right(C, EXT, NB + n * SLOTS, SLOTS, scaled_columns(*[ghost[n, c] for c in range(5)]))
-        acc_b[...] = jnp.zeros_like(acc_b)
-
-        def right_side(i, _):
-            for j in range(4):
-                right_features(C, EXT, i * 4 + j, BF, i * 4 + j)
-            return 0
-
-        lax.fori_loop(0, EXT // 4, right_side, 0)
-
-        def left_side(i, _):
-            for j in range(8):
-                b = i * 8 + j
-                left_features(CA, b, AF, b)
-                acc_a[b] = jnp.zeros((W128, W128), f32)
-            return 0
-
-        lax.fori_loop(0, NB // 8, left_side, 0)
+    for n in range(NEIGH):
+        fill_right(C, EXT, NB + n * SLOTS, SLOTS, scaled_columns(*[ghost_o[n, c] for c in range(5)]))
+
+    def ghost_features(i, _):
+        for j in range(8):
+            right_features(C, EXT, i * 8 + j, BF, i * 8 + j)
+        return 0
+
+    lax.fori_loop(NB // 8, EXT // 8, ghost_features, 0)
+    for j in range(UNROLL):
+        product(pair_ends[0, 0, j], pair_ends[0, 1, j], j)
+    lanes = lax.broadcasted_iota(jnp.int32, (8, W128), 1)
+
+    def tile_copy(c):
+        return pltpu.make_async_copy(T.at[lax.rem(c, 2)], tiles_o.at[pl.ds(c * CHUNK, CHUNK)], tile_sem.at[c])
+
+    def pair_body(c, u, _):
+        k0 = c * CHUNK + u * UNROLL
+        slot = lax.rem(c, 2)
         for j in range(UNROLL):
-            first_stage(j, j)
-
-    def body(u, _):
-        k0 = step * UNITS_STEP + u * UNROLL
-        sums = []
-        for j in range(UNROLL):
-            ta = idx[2, k0 + j]
+            here = lanes == lax.rem(k0 + j, W128)
+            column = lax.div(k0 + j, W128)
             part = jnp.zeros((8, W128), f32)
             for r in range(0, W128, 8):
                 W, S = tile_math(GB[j, r:r + 8, :W128], GB[j, r:r + 8, W128:])
-                tiles[u * UNROLL + j, r:r + 8] = S
+                T[slot, u * UNROLL + j, r:r + 8] = S
                 part = part + W
-                acc_a[ta, r:r + 8] += W
-            first_stage(k0 + UNROLL + j, j)
-            sums.append((idx[3, k0 + j], part))
-        for tb, part in sums:
-            acc_b[pl.ds(pl.multiple_of(tb * 8, 8), 8), :] += part
-        return 0
-
-    lax.fori_loop(0, UNITS_STEP // UNROLL, body, 0)
-
-    @pl.when(step == pl.num_programs(0) - 1)
-    def _():
-        ones = jnp.ones((16, 2 * W128), bf16)
-
-        def fold(i, _):
-            rows = []
-            for j in range(4):
-                hi, lo = hilo(acc_a[i * 4 + j])
-                rows.append(lax.dot_general(ones, jnp.concatenate([hi, lo], 1), (((1,), (1,)), ((), ())),
-                                            preferred_element_type=f32))
-            for j in range(4):
-                dens_o[pl.ds(i * 4 + j, 1), :] = rows[j][:1]
-            return 0
-
-        lax.fori_loop(0, NB // 4, fold, 0)
-        for i in range(EXT // 8):
-            v = acc_b[pl.ds(i * 64, 8, stride=8), :]
-            for s in range(1, 8):
-                v = v + acc_b[pl.ds(i * 64 + s, 8, stride=8), :]
-            if i < NB // 8:
-                r = slice(i * 8, i * 8 + 8)
-                dens_o[r] = (dens_o[r] + (v + self_sum[r])) * (4.0 * NORM) / mass[r]
-            else:
-                n = i - NB // 8
-                dens_g[n] = v * (4.0 * NORM) / ghost[n, 3]
+                RT[column, r:r + 8] = jnp.where(here, jnp.sum(W, axis=1, keepdims=True), RT[column, r:r + 8])
+            PB[pl.ds(pl.multiple_of((k0 + j) * 8, 8), 8), :] = part
+            k = jnp.minimum(k0 + UNROLL + j, npairs - 1)
+            product(pair_ends[0, 0, k], pair_ends[0, 1, k], j)
+        return 0
+
+    chunks = npairs // CHUNK
+
+    def chunk_body(c, _):
+        @pl.when(c >= 2)
+        def _():
+            tile_copy(c - 2).wait()
+
+        lax.fori_loop(0, CHUNK // UNROLL, functools.partial(pair_body, c), 0)
+        tile_copy(c).start()
+        return 0
+
+    lax.fori_loop(0, chunks, chunk_body, 0)
+
+    dot = functools.partial(jnp.dot, preferred_element_type=f32)
+    rows = jnp.zeros((W128, NB), f32)
+    for w in range(RT.shape[0]):
+        for p in hilo(RT[w]):
+            rows = rows + lax.dot_general(p, hot_a[:, w * W128:(w + 1) * W128], (((1,), (1,)), ((), ())),
+                                          preferred_element_type=f32)
+    slots = PB.shape[0] // 8
+    part = PB[pl.ds(0, slots, stride=8), :]
+    for i in range(1, 8):
+        part = part + PB[pl.ds(i, slots, stride=8), :]
+    hi, lo = hilo(part)
+    sums = dot(hot_b[...], hi) + dot(hot_b[...], lo)
+    dens_o[...] = (sums[:NB] + rows.T + self_sum[...]) * (4.0 * NORM) / mass[...]
+    for n in range(NEIGH):
+        at = NB + n * SLOTS
+        gdens_o[n] = sums[at:at + SLOTS] * (4.0 * NORM) / ghost_o[n, 3]
+
+    def own_landed(g, _):
+        own_copy(g).wait()
+        return 0
+
+    lax.fori_loop(0, NB // SELF, own_landed, 0)
+    for c in range(chunks - 2, chunks):
+        tile_copy(c).wait()
 
 
 def back_kernel(idx, send_list, idx_v, hot, pos, mass, ghost, part, gpart, energy, tiles_h, own_h, dens_o, acc_o,
@@ -315,13 +321,7 @@
     slots = R.shape[0] // 16
     R[pairs * 8:slots * 8] = jnp.zeros(((slots - pairs) * 8, W128), f32)
     R[(slots + pairs) * 8:] = jnp.zeros(((slots - pairs) * 8, W128), f32)
-    for w in range(slots // W128):
-        at = slice(w * W128, (w + 1) * W128)
-        for matrix, row in ((hot_a, 2), (hot_b, 3)):
-            rows = matrix.shape[0]
-            which = idx_v[row:row + 1, at]
-            blocks = lax.broadcasted_iota(jnp.int32, (rows, W128), 0)
-            matrix[:, at] = jnp.where(blocks == which, 1.0, 0.0).astype(bf16)
+    pair_matrices(idx_v, hot_a, hot_b)
 
     def weights(at, rows, x, y, z, m, p):
         k = inverse_cube_root(m)
@@ -449,37 +449,27 @@
 sds = jax.ShapeDtypeStruct
 
 
-def run_forward(send_list, pair_count, pair_list, pos, mass, smoothing, level):
+def run_front(send_list, pair_count, pair_list, pos, mass, smoothing, level):
     D = pltpu.SemaphoreType.DMA((NEIGH,))
-    slots = pair_list.shape[2] + 2 * W128 - pair_list.shape[2] % W128
     vm = pltpu.VMEM
+    A = pl.BlockSpec(memory_space=pl.ANY)
+    pairs = pair_list.shape[2]
+    slots = pairs + (-pairs) % (2 * W128)
     return pl.pallas_call(
-        forward_kernel,
+        front_kernel,
         out_shape=[
             sds((NEIGH, 5, SLOTS, W128), f32), sds((4, slots), jnp.int32), sds((NB, 2 * W128), bf16),
-            sds((3, NB, W128), f32), sds((NB, W128), f32), sds((NB, W128), f32), sds((NB, W128, W128), f32)],
-        in_specs=[SM, SM, V, V, V, V, V], out_specs=[V] * 6 + [pl.BlockSpec(memory_space=pl.ANY)],
+            sds((3, NB, W128), f32), sds((NB, W128), f32), sds((NEIGH, SLOTS, W128), f32),
+            sds((NB, W128, W128), f32), sds((pairs, W128, W128), f32)],
+        in_specs=[SM, SM, SM, V, V, V, V, V], out_specs=[V] * 6 + [A, A],
         scratch_shapes=[
-            vm((NEIGH, 5, SLOTS, W128), f32), vm((2 * W128, W128), f32), vm((13 * NB, W128), f32), vm((8 * NB, W128), f32),
-            vm((SELF, W128, 64), bf16), vm((SELF, 64, 2 * W128), bf16), vm((SELF, W128, 2 * W128), f32),
-            vm((NB, W128, W128), f32), D, D, pltpu.SemaphoreType.DMA((NB // SELF,))],
+            vm((NB, W128), f32), vm((NB, W128), f32), vm((NEIGH, 5, SLOTS, W128), f32), vm((2 * W128, W128), f32),
+            vm((13 * EXT, W128), f32), vm((8 * NB, W128), f32), vm((NB, W128, 64), bf16), vm((EXT, 64, 2 * W128), bf16),
+            vm((UNROLL, W128, 2 * W128), f32), vm((NB, W128, W128), f32), vm((2, CHUNK, W128, W128), f32),
+            vm((slots // W128, W128, W128), f32), vm((slots * 8, W128), f32), vm((NB, slots), bf16), vm((EXT, slots), bf16),
+            D, D, pltpu.SemaphoreType.DMA((NB // SELF,)), pltpu.SemaphoreType.DMA((pairs // CHUNK,))],
         compiler_params=pltpu.CompilerParams(collective_id=0, has_side_effects=True, vmem_limit_bytes=VMEM),
-        name="forward")(send_list, pair_count, pair_list, pos, mass, smoothing, level)
-
-
-def run_density(idx, pos, mass, smooth, ghost, self_sum, pairs):
-    vm = pltpu.VMEM
-    return pl.pallas_call(
-        density_pairs,
-        grid_spec=pltpu.PrefetchScalarGridSpec(
-            num_scalar_prefetch=1, grid=(pairs // UNITS_STEP,), in_specs=[V] * 5,
-            out_specs=[V, V, pl.BlockSpec((UNITS_STEP, W128, W128), lambda i, *_: (i, 0, 0))],
-            scratch_shapes=[
-                vm((13 * EXT, W128), f32), vm((8 * NB, W128), f32), vm((NB, W128, 64), bf16), vm((EXT, 64, 2 * W128), bf16),
-                vm((UNROLL, W128, 2 * W128), f32), vm((NB + 1, W128, W128), f32), vm(((EXT + 1) * 8, W128), f32)]),
-        out_shape=[sds((NB, W128), f32), sds((NEIGH, SLOTS, W128), f32), sds((pairs, W128, W128), f32)],
-        compiler_params=pltpu.CompilerParams(vmem_limit_bytes=VMEM),
-        name="density_pairs")(idx, pos, mass, smooth, ghost, self_sum)
+        name="front")(send_list, pair_count, pair_list, pair_list, pos, mass, smoothing, level)
 
 
 def run_back(idx, send_list, hot, pos, mass, ghost, part, gpart, energy, tiles, own_tiles):
@@ -504,10 +494,9 @@
 
 def per_device(positions, masses, smoothing, energy, level_ids, send_list, pair_list, pair_count):
     mass = masses.reshape(NB, W128)
-    ghost, idx, hot, pos, smooth, self_sum, own_tiles = run_forward(
+    ghost, idx, hot, pos, dens, gdens, own_tiles, tiles = run_front(
         send_list, pair_count, pair_list, positions.reshape(3, NB, W128).transpose(1, 0, 2), mass,
         smoothing.reshape(NB, W128), level_ids.reshape(1, NB))
-    dens, gdens, tiles = run_density(idx, pos, mass, smooth, ghost, self_sum, pair_list.shape[2])
     density, accel = run_back(
         idx, send_list, hot, pos, mass, ghost, dens, gdens, energy.reshape(NB, W128), tiles, own_tiles)
     return density.reshape(NB * W128), accel.transpose(1, 0, 2).reshape(3, NB * W128)

time: 125 us -> 113 us (0.904)
  Pallas kernels: 119 us -> 106 us
    pallas_call x2 -> x1, Pallas kernels: 69.5 us -> 56.6 us  [run_front(): pl.pallas_call(front_kernel, out_shape=[sds((NEIGH, 5, SLOTS, W128), f32)...]
where the time goes in v5:
time: 113 us; the launch traced here: 112 us
  Pallas kernels  106 us (94%)
  local copies, waits for them, and re-layouts  4.54 us (4%)
  between operations  1.29 us (1%)
    pallas_call x1, Pallas kernels, run_front(): pl.pallas_call(front_kernel, out_shape=[sds((NEIGH, 5, SLOTS, W128), f32)...  56.6 us
    pallas_call x1, Pallas kernels, run_back(): pl.pallas_call(back_kernel, out_shape=[sds((NB, W128), f32), sds((NB, 3,...  49.8 us
    unnamed x3, local copies, waits for them, and re-layouts  4.54 us

profile of v5, /device:TPU:1, one launch (start us, length us, event | category | flops | bytes accessed | tf_op | source)
XLA Modules:
  0.0 112.3 jit_solution(18386085526766387479)
XLA Ops:
  1.3 1.4 %copy.10.send_list = s32[1,20,8]{2,1,0:T(8,128)} copy(s32[1,20,8]{1,2,0:T(8,128)} %param.13) | data formatting | bytes 1280 | tf_op args[5]
  2.6 56.6 %front.1 = (f32[20,5,8,128]{3,2,1,0:T(8,128)}, s32[4,768]{1,0:T(4,128)}, bf16[128,256]{1,0:T(8,128)(2,1)}, f32[3,128,128]{2,1,0:T(8,128)}, f32[128,128]{1,0:T(8,...) custom-call(s32[1,20,8]{2,1,0:T(8,128)} %copy.10.send_list, s32[1]{0:T(128)S(6)} %copy.14.count, ...), custom_call_target="tpu_custom_call" | custom-call | tf_op jit(solution)/shard_map/front/pallas_call | solution.py:458
  59.3 49.8 %back.1 = (f32[128,128]{1,0:T(8,128)}, f32[128,3,128]{2,1,0:T(4,128)}) custom-call(s32[4,768]{1,0:T(4,128)} %get-tuple-element.12.idx.idx_v, s32[1,20,8]{2,1,0:T(8,128)} %copy.10.send_list, s32[4,768]{1,0:T(4,128)} %get-tuple-element.12.idx.idx_v, bf16[128,256]{1,0:T(8,128)(2,1)} %get-tuple-element.13.hot, f32[3,128,128]{2,1,0:T(8,128)} %get-tuple-element.14.pos, ...), custom_call_target="tpu_custom_call" | custom-call | tf_op jit(solution)/shard_map/back/pallas_call | solution.py:481
  109.1 1.5 %copy.15 = f32[16384]{0:T(1024)} copy(f32[16384]{0:T(1024)} %bitcast.17) | data formatting | bytes 131072
  110.6 1.7 %copy.16 = f32[3,16384]{1,0:T(4,128)} copy(f32[3,16384]{1,0:T(4,128)} %bitcast.14) | data formatting | bytes 393216

commit v6 on v5

v6 whole, which is shorter than its diff:
```python
import functools
import math

import jax
import jax.numpy as jnp
from jax import lax
from jax.experimental import pallas as pl
from jax.experimental.pallas import tpu as pltpu
from jax.sharding import PartitionSpec as P

MESH = pl.DeviceIdType.MESH
f32 = jnp.float32
bf16 = jnp.bfloat16
NORM = 21.0 / (2.0 * math.pi)
GAMMA_LESS = 2.0 / 3.0
SHRINK = 0.8
NB = 128
W128 = 128
NEIGH = 20
SLOTS = 8
GHOSTS = NEIGH * SLOTS
EXT = NB + GHOSTS
CHUNKS = [(0, 0), (0, 1), (1, 0), (1, 1), (0, 2), (2, 0), (1, 2), (2, 1)]
UNROLL = 28
CHUNK = 84
FORCE_UNROLL = 28
KEEP = 5
SELF = 8
VMEM = 63 * 2**20


def neighbour_steps():
    return [
        (step_patch, step_bulk)
        for step_patch in (-1, 0, 1)
        for step_bulk in range(-3, 4)
        if (step_patch, step_bulk) != (0, 0)
    ]


def place(offset):
    rows, columns = lax.axis_size("patch"), lax.axis_size("bulk")
    count = rows * columns
    me = lax.axis_index("patch") * columns + lax.axis_index("bulk")
    other = lax.rem(me + (offset + count), count)
    return (lax.div(other, columns), lax.rem(other, columns))


def offsets():
    columns = lax.axis_size("bulk")
    return [u * columns + v for u, v in neighbour_steps()]


def meet():
    barrier = pltpu.get_barrier_semaphore()
    for o in offsets():
        pl.semaphore_signal(barrier, inc=1, device_id=place(o), device_id_type=MESH)
    pl.semaphore_wait(barrier, NEIGH)


def start_all(src, dst, send_sem, recv_sem, sign):
    copies = []
    for n, o in enumerate(offsets()):
        copy = pltpu.make_async_remote_copy(
            src_ref=src.at[n], dst_ref=dst.at[n], send_sem=send_sem.at[n], recv_sem=recv_sem.at[n],
            device_id=place(sign * o), device_id_type=MESH)
        copy.start()
        copies.append(copy)
    return copies


def split3(v):
    a = v.astype(bf16).astype(f32)
    r = v - a
    b = r.astype(bf16).astype(f32)
    return a, b, r - b


def hilo(v):
    hi = v.astype(bf16)
    return hi, (v - hi.astype(f32)).astype(bf16)


def split_dot(hot, v):
    a, b, c = [p.astype(bf16) for p in split3(v)]
    dot = functools.partial(jnp.dot, preferred_element_type=f32)
    return dot(hot, a) + (dot(hot, b) + dot(hot, c))


def inverse_cube_root(m):
    k = jnp.exp(jnp.log(m) * (-1.0 / 3.0))
    return k * (4.0 - m * (k * k * k)) * (1.0 / 3.0)


def tile_math(r2, hs):
    r2 = jnp.maximum(r2, 1e-30)
    s = pl.reciprocal(hs, approx=True)
    q = r2 * lax.rsqrt(r2) * s
    t = jnp.maximum(1.0 - q, 0.0)
    st = s * t
    c = st * st * st
    return c * (t * (q + 0.25)), c * (s * s)


def scaled_columns(x, y, z, m, h):
    k = inverse_cube_root(m)
    k2 = k * k
    return x * k2, y * k2, z * k2, k2, (x * x + y * y + z * z) * k2, (0.5 * h) * k, k


def fill_right(C, total, at, rows, v):
    for i, c in ((0, 0), (1, 1), (2, 2), (3, 3), (4, 4), (10, 5), (11, 6)):
        C[i * total + at:i * total + at + rows] = v[c]


def clear_right(C, total):
    zero = jnp.zeros((total, W128), f32)
    for i in (5, 6, 7, 8, 9, 12):
        C[i * total:(i + 1) * total] = zero


def fill_left(CA, v):
    for i, w in enumerate((-2.0 * v[0], -2.0 * v[1], -2.0 * v[2], v[4], v[3], v[6], v[5], jnp.zeros_like(v[0]))):
        CA[i * NB:(i + 1) * NB] = w


def right_features(C, total, b, BF, at):
    for w, c in ((0, 0), (5, W128)):
        p = split3(C[pl.ds(w * total + b, 8, stride=total), :])
        BF[at, :, c:c + W128] = jnp.concatenate([p[q] for _, q in CHUNKS], 0).astype(bf16)


def left_features(CA, b, AF, at):
    p = split3(CA[pl.ds(b, 8, stride=NB), :])
    AF[at] = jnp.concatenate([p[q] for q, _ in CHUNKS], 0).T.astype(bf16)


def pair_matrices(idx_v, hot_a, hot_b):
    for w in range(hot_a.shape[1] // W128):
        at = slice(w * W128, (w + 1) * W128)
        for matrix, row in ((hot_a, 2), (hot_b, 3)):
            which = idx_v[row:row + 1, at]
            blocks = lax.broadcasted_iota(jnp.int32, (matrix.shape[0], W128), 0)
            matrix[:, at] = jnp.where(blocks == which, 1.0, 0.0).astype(bf16)


def whole_kernel(send_list, count, pair_ends, pairs, pos_in, mass, smoothing, energy, level,
                 dens_o, acc_o, own_h, tiles_h,
                 ghost, idx, hot_o, pos, smooth, self_sum, gdens, buf, C, AF, BF, GB, T, RT, R, RS, MM, hot_a, hot_b,
                 gpress, ret, gacc, racc,
                 send_sem, recv_sem, own_sem, tile_sem, s1, r1, s2, r2, s3, r3):
    left = R.at[pl.ds(0, 8 * NB)]
    press, pbuf = smooth, gdens
    hot = R.at[pl.ds(8 * NB, 2 * W128)]
    right = R.at[pl.ds(R.shape[0] // 2, 13 * EXT)]
    lev = level[...]
    scale = jnp.where(lev == 0, 1.0, jnp.where(lev == 1, SHRINK, SHRINK * SHRINK)).astype(f32)
    smooth[...] = smoothing[...] * jnp.broadcast_to(scale, (NB, W128)).T
    for c in range(3):
        pos[c] = pos_in[:, c, :]
    lane = lax.broadcasted_iota(jnp.int32, (1, NB), 1)

    def gather(n, _):
        for g in range(SLOTS):
            t = send_list[0, g, n]
            for c in range(3):
                buf[n, c, g:g + 1, :] = pos[c, pl.ds(t, 1), :]
            buf[n, 3, g:g + 1, :] = mass[pl.ds(t, 1), :]
            buf[n, 4, g:g + 1, :] = smooth[pl.ds(t, 1), :]
            hot[pl.ds(n * SLOTS + g, 1), :] = jnp.where(lane == t, 1.0, 0.0)
        return 0

    hot[pl.ds(GHOSTS, 2 * W128 - GHOSTS), :] = jnp.zeros((2 * W128 - GHOSTS, W128), f32)
    lax.fori_loop(0, NEIGH, gather, 0)
    meet()
    copies = start_all(buf, ghost, send_sem, recv_sem, 1)

    npairs = pairs.shape[2]
    live = lax.broadcasted_iota(jnp.int32, (1, npairs), 1) < count[0]
    idx[...] = jnp.zeros_like(idx)
    idx[2:4, :] = jnp.full((2, idx.shape[1]), EXT, jnp.int32)
    first = pairs[0, 0:1, :]
    second = pairs[0, 1:2, :]
    idx[0:1, :npairs] = first
    idx[1:2, :npairs] = second
    idx[2:3, :npairs] = jnp.where(live, first, NB)
    idx[3:4, :npairs] = jnp.where(live, second, EXT)
    pair_matrices(idx, hot_a, hot_b)
    for i in range(2):
        hot_o[:, i * W128:(i + 1) * W128] = hot[i * W128:(i + 1) * W128].T.astype(bf16)
    slots = R.shape[0] // 16
    R[npairs * 8:slots * 8] = jnp.zeros(((slots - npairs) * 8, W128), f32)
    R[(slots + npairs) * 8:] = jnp.zeros(((slots - npairs) * 8, W128), f32)
    RT[...] = jnp.zeros_like(RT)
    clear_right(right, EXT)
    v = scaled_columns(pos[0], pos[1], pos[2], mass[...], smooth[...])
    fill_right(right, EXT, 0, NB, v)
    fill_left(left, v)

    own_first = (KEEP - 2) * CHUNK
    chunks = npairs // CHUNK

    def features(g):
        for j in range(SELF):
            b = g * SELF + j
            right_features(right, EXT, b, BF, b)
            left_features(left, b, AF, b)

    def product(a, b, j):
        GB[j] = jnp.dot(AF[a], BF[b], preferred_element_type=f32)

    def own_copy(g):
        return pltpu.make_async_copy(T.at[pl.ds(own_first + g * SELF, SELF)], own_h.at[pl.ds(g * SELF, SELF)], own_sem.at[g])

    features(0)
    for j in range(SELF):
        product(j, j, j)
    features(1)

    def own_body(g, _):
        after = jnp.minimum(g + 1, NB // SELF - 1)
        for j in range(SELF):
            part = jnp.zeros((8, W128), f32)
            for r in range(0, W128, 8):
                W, S = tile_math(GB[j, r:r + 8, :W128], GB[j, r:r + 8, W128:])
                T[own_first + g * SELF + j, r:r + 8] = S
                part = part + W
            self_sum[pl.ds(g * SELF + j, 1), :] = jnp.sum(part, axis=0, keepdims=True)
        own_copy(g).start()
        for j in range(SELF):
            product(after * SELF + j, after * SELF + j, j)
        features(jnp.minimum(g + 2, NB // SELF - 1))
        return 0

    lax.fori_loop(0, NB // SELF, own_body, 0)
    for copy in copies:
        copy.wait()

    for n in range(NEIGH):
        fill_right(right, EXT, NB + n * SLOTS, SLOTS, scaled_columns(*[ghost[n, c] for c in range(5)]))

    def ghost_features(i, _):
        for j in range(8):
            right_features(right, EXT, i * 8 + j, BF, i * 8 + j)
        return 0

    lax.fori_loop(NB // 8, EXT // 8, ghost_features, 0)
    for j in range(UNROLL):
        product(pair_ends[0, 0, j], pair_ends[0, 1, j], j)
    lanes = lax.broadcasted_iota(jnp.int32, (8, W128), 1)

    def spill_out(c):
        at = pl.ds(c * CHUNK, CHUNK)
        return pltpu.make_async_copy(T.at[at], tiles_h.at[at], tile_sem.at[c])

    def spill_back(c):
        at = pl.ds(c * CHUNK, CHUNK)
        return pltpu.make_async_copy(tiles_h.at[at], T.at[at], tile_sem.at[chunks - KEEP + c])

    def pair_body(c, u, _):
        k0 = c * CHUNK + u * UNROLL
        slot = lax.rem(c, KEEP) * CHUNK + u * UNROLL
        for j in range(UNROLL):
            here = lanes == lax.rem(k0 + j, W128)
            column = lax.div(k0 + j, W128)
            part = jnp.zeros((8, W128), f32)
            for r in range(0, W128, 8):
                W, S = tile_math(GB[j, r:r + 8, :W128], GB[j, r:r + 8, W128:])
                T[slot + j, r:r + 8] = S
                part = part + W
                RT[column, r:r + 8] = jnp.where(here, jnp.sum(W, axis=1, keepdims=True), RT[column, r:r + 8])
            R[pl.ds(pl.multiple_of((k0 + j) * 8, 8), 8), :] = part
            k = jnp.minimum(k0 + UNROLL + j, npairs - 1)
            product(pair_ends[0, 0, k], pair_ends[0, 1, k], j)
        return 0

    def own_landed(g, _):
        own_copy(g).wait()
        return 0

    def chunk_body(c, _):
        @pl.when(c == KEEP - 2)
        def _():
            lax.fori_loop(0, NB // SELF, own_landed, 0)

        @pl.when(c >= KEEP)
        def _():
            spill_out(c - KEEP).wait()

        lax.fori_loop(0, CHUNK // UNROLL, functools.partial(pair_body, c), 0)

        @pl.when(c < chunks - KEEP)
        def _():
            spill_out(c).start()

        return 0

    lax.fori_loop(0, chunks, chunk_body, 0)

    dot = functools.partial(jnp.dot, preferred_element_type=f32)
    rows = jnp.zeros((W128, NB), f32)
    for w in range(RT.shape[0]):
        for p in hilo(RT[w]):
            rows = rows + lax.dot_general(p, hot_a[:, w * W128:(w + 1) * W128], (((1,), (1,)), ((), ())),
                                          preferred_element_type=f32)
    part = R[pl.ds(0, slots, stride=8), :]
    for i in range(1, 8):
        part = part + R[pl.ds(i, slots, stride=8), :]
    hi, lo = hilo(part)
    sums = dot(hot_b[...], hi) + dot(hot_b[...], lo)
    for n in range(NEIGH):
        at = NB + n * SLOTS
        gdens[n] = sums[at:at + SLOTS] * (4.0 * NORM) / ghost[n, 3]
    copies = start_all(gdens, ret, s1, r1, -1)
    mine = (sums[:NB] + rows.T + self_sum[...]) * (4.0 * NORM) / mass[...]

    def weights(at, rows, x, y, z, m, p):
        k = inverse_cube_root(m)
        w = k * k
        pw = p * w
        for i, v in enumerate((w, w * x, w * y, w * z, pw, pw * x, pw * y, pw * z)):
            C[i * EXT + at:i * EXT + at + rows] = v

    def columns(i, _):
        for j in range(4):
            b = i * 4 + j
            v = C[pl.ds(b, 8, stride=EXT), :]
            hi = v.astype(bf16).astype(f32)
            mm = jnp.concatenate([hi, v - hi], 0).astype(bf16)
            MM[b, :, :W128] = mm
            MM[b, :, W128:] = mm
        return 0

    for copy in copies:
        copy.wait()
    dens = mine + split_dot(hot_o[:, :GHOSTS], ret[...].reshape(GHOSTS, W128))
    dens_o[...] = dens
    press[...] = GAMMA_LESS * energy[...] / dens

    def gather_press(n, _):
        for g in range(SLOTS):
            pbuf[n, g:g + 1, :] = press[pl.ds(send_list[0, g, n], 1), :]
        return 0

    lax.fori_loop(0, NEIGH, gather_press, 0)
    copies = start_all(pbuf, gpress, s2, r2, 1)

    weights(0, NB, pos[0], pos[1], pos[2], mass[...], press[...])
    lax.fori_loop(0, NB // 4, columns, 0)

    def to_b(k, hi, lo):
        return jnp.dot(MM[pair_ends[0, 0, k]], jnp.concatenate([hi, lo], 0), preferred_element_type=f32)

    def to_a(k, hi, lo):
        return lax.dot_general(MM[pair_ends[0, 1, k]], jnp.concatenate([hi, lo], 1), (((1,), (1,)), ((), ())),
                               preferred_element_type=f32)

    def put(ref, k, v):
        ref[pl.ds(pl.multiple_of(k * 8, 8), 8), :] = v[:8] + v[8:]

    def own_sums(u, _):
        out = []
        for j in range(16):
            a = u * 16 + j
            hi, lo = hilo(T[own_first + a])
            out.append((a, jnp.dot(MM[a], jnp.concatenate([hi, lo], 0), preferred_element_type=f32)))
        for a, v in out:
            put(RS, a, v)
        return 0

    def pair_sums(do_a, do_b, c, u, _):
        out = []
        for j in range(FORCE_UNROLL):
            k = c * CHUNK + u * FORCE_UNROLL + j
            hi, lo = hilo(T[lax.rem(c, KEEP) * CHUNK + u * FORCE_UNROLL + j])
            if do_b:
                out.append((slots + k, to_b(k, hi, lo)))
            if do_a:
                out.append((k, to_a(k, hi, lo)))
        for k, v in out:
            put(R, k, v)
        return 0

    def chunk_sums(do_a, do_b, c):
        lax.fori_loop(0, CHUNK // FORCE_UNROLL, functools.partial(pair_sums, do_a, do_b, c), 0)

    def early(do_a, do_b, i, _):
        chunk_sums(do_a, do_b, KEEP + i)
        return 0

    lax.fori_loop(0, chunks - KEEP, functools.partial(early, False, True), 0)
    for copy in copies:
        copy.wait()
    for n in range(NEIGH):
        weights(NB + n * SLOTS, SLOTS, *[ghost[n, c] for c in range(4)], gpress[n])
    lax.fori_loop(NB // 4, EXT // 4, columns, 0)
    lax.fori_loop(0, chunks - KEEP, functools.partial(early, True, False), 0)
    for c in range(chunks - KEEP):
        spill_back(c).start()
    own_back = pltpu.make_async_copy(own_h, T.at[pl.ds(own_first, NB)], tile_sem.at[2 * (chunks - KEEP)])

    def rest(i, _):
        c = lax.rem(chunks - KEEP + i, KEEP)

        @pl.when(i == 2)
        def _():
            own_back.start()

        @pl.when(i >= 2)
        def _():
            spill_back(c).wait()

        chunk_sums(True, True, c)
        return 0

    lax.fori_loop(0, KEEP, rest, 0)
    own_back.wait()
    lax.fori_loop(0, NB // 16, own_sums, 0)

    A = []
    for c in range(0, 8, 2):
        total = []
        for half, matrix in ((0, hot_a), (1, hot_b)):
            v = [R[pl.ds(half * slots * 8 + c + i, slots, stride=8), :] for i in range(2)]
            hi, lo = hilo(jnp.concatenate(v, 1))
            total.append(dot(matrix[...], hi) + dot(matrix[...], lo))
        own = total[1][:NB] + total[0]
        for i in range(2):
            at = slice(i * W128, (i + 1) * W128)
            A.append((own[:, at] + RS[pl.ds(c + i, NB, stride=8), :], total[1][NB:, at]))
    scale = -20.0 * NORM

    def final(p, m, spot, A):
        k = inverse_cube_root(m)
        k2 = k * k
        own = p * A[0] + A[4]
        return [(p * A[c + 1] + A[c + 5] - v * own) * (scale * (k2 * k2 * k)) for c, v in enumerate(spot)]

    for n in range(NEIGH):
        r = slice(n * SLOTS, (n + 1) * SLOTS)
        for c, v in enumerate(final(gpress[n], ghost[n, 3], [ghost[n, c] for c in range(3)], [x[1][r] for x in A])):
            gacc[n, c] = v
    copies = start_all(gacc, racc, s3, r3, -1)
    mine = final(press[...], mass[...], [pos[c] for c in range(3)], [x[0] for x in A])
    for copy in copies:
        copy.wait()
    for c in range(3):
        acc_o[:, c, :] = mine[c] + split_dot(hot_o[:, :GHOSTS], racc[:, c].reshape(GHOSTS, W128))


V = pl.BlockSpec(memory_space=pltpu.VMEM)
SM = pl.BlockSpec(memory_space=pltpu.SMEM)
sds = jax.ShapeDtypeStruct


def run_whole(send_list, pair_count, pair_list, pos, mass, smoothing, energy, level):
    D = pltpu.SemaphoreType.DMA((NEIGH,))
    vm = pltpu.VMEM
    A = pl.BlockSpec(memory_space=pl.ANY)
    pairs = pair_list.shape[2]
    slots = pairs + (-pairs) % (2 * W128)
    one = vm((NB, W128), f32)
    eight = vm((NEIGH, SLOTS, W128), f32)
    three = vm((NEIGH, 3, SLOTS, W128), f32)
    five = vm((NEIGH, 5, SLOTS, W128), f32)
    return pl.pallas_call(
        whole_kernel,
        out_shape=[sds((NB, W128), f32), sds((NB, 3, W128), f32), sds((NB, W128, W128), f32),
                   sds((pairs - KEEP * CHUNK, W128, W128), f32)],
        in_specs=[SM, SM, SM, V, V, V, V, V, V], out_specs=[V, V, A, A],
        scratch_shapes=[
            five, vm((4, slots), jnp.int32), vm((NB, 2 * W128), bf16), vm((3, NB, W128), f32), one, one, eight, five,
            vm((8 * EXT, W128), f32), vm((NB, W128, 64), bf16),
            vm((EXT, 64, 2 * W128), bf16), vm((UNROLL, W128, 2 * W128), f32), vm((KEEP * CHUNK, W128, W128), f32),
            vm((slots // W128, W128, W128), f32), vm((2 * slots * 8, W128), f32), vm((NB * 8, W128), f32),
            vm((EXT, 16, 2 * W128), bf16), vm((NB, slots), bf16), vm((EXT, slots), bf16),
            eight, eight, three, three,
            D, D, pltpu.SemaphoreType.DMA((NB // SELF,)), pltpu.SemaphoreType.DMA((2 * (pairs // CHUNK - KEEP) + 1,)), D, D, D, D, D, D],
        compiler_params=pltpu.CompilerParams(collective_id=0, has_side_effects=True, vmem_limit_bytes=VMEM),
        name="whole")(send_list, pair_count, pair_list, pair_list, pos, mass, smoothing, energy, level)


def per_device(positions, masses, smoothing, energy, level_ids, send_list, pair_list, pair_count):
    mass = masses.reshape(NB, W128)
    density, accel, _, _ = run_whole(
        send_list.transpose(0, 2, 1), pair_count, pair_list, positions.reshape(3, NB, W128).transpose(1, 0, 2), mass,
        smoothing.reshape(NB, W128), energy.reshape(NB, W128), level_ids.reshape(1, NB))
    return density.reshape(NB * W128), accel.transpose(1, 0, 2).reshape(3, NB * W128)


def solution(mesh):
    both = ("patch", "bulk")
    placed = (P(None, both), P(both), P(both), P(both), P(both), P(both, None, None), P(both, None, None), P(both))
    return jax.shard_map(per_device, mesh=mesh, in_specs=placed, out_specs=(P(both), P(None, both)), check_vma=False)
```

time: 113 us -> 100 us (0.88)
  Pallas kernels: 106 us -> 95.6 us
  local copies, waits for them, and re-layouts: 4.54 us -> 3.17 us
    pallas_call x2 -> x1, Pallas kernels: 106 us -> 95.6 us  [run_whole(): pl.pallas_call(whole_kernel, out_shape=[sds((NB, W128), f32), sds((NB, 3,...]
    unnamed x3 -> x2, local copies, waits for them, and re-layouts: 4.54 us -> 3.17 us
where the time goes in v6:
time: 100 us
  Pallas kernels  95.6 us (96%)
  local copies, waits for them, and re-layouts  3.17 us (3%)
  between operations  1.29 us (1%)
    pallas_call x1, Pallas kernels, run_whole(): pl.pallas_call(whole_kernel, out_shape=[sds((NB, W128), f32), sds((NB, 3,...  95.6 us
    unnamed x2, local copies, waits for them, and re-layouts  3.17 us

profile of v6, /device:TPU:1, one launch (start us, length us, event | category | flops | bytes accessed | tf_op | source)
XLA Modules:
  0.0 100.1 jit_solution(3945985005160452656)
XLA Ops:
  1.3 95.6 %whole.1 = (f32[128,128]{1,0:T(8,128)}, f32[128,3,128]{2,1,0:T(4,128)}, f32[128,128,128]{2,1,0:T(8,128)}, f32[252,128,128]{2,1,0:T(8,128)}) custom-call(s32[1,8,20]{2,1,0:T(8,128)} %bitcast.18, s32[1]{0:T(128)S(6)} %copy.12.count, s32[1,2,672]{2,1,0:T(2,128)} %pairs.1, s32[1,2,672]{2,1,0:T(2,128)} %pairs.1, f32[128,3,128]{2,1,0:T(4,128)} %bitcast.12, ...), custom_call_target="tpu_custom_call" | custom-call | tf_op jit(solution)/shard_map/whole/pallas_call | solution.py:466
  96.9 1.5 %copy.13 = f32[16384]{0:T(1024)} copy(f32[16384]{0:T(1024)} %bitcast.14) | data formatting | bytes 131072
  98.4 1.7 %copy.14 = f32[3,16384]{1,0:T(4,128)} copy(f32[3,16384]{1,0:T(4,128)} %bitcast.13) | data formatting | bytes 393216

commit v7 on v6

--- a/solution.py
+++ b/solution.py
@@ -23,7 +23,7 @@
 CHUNKS = [(0, 0), (0, 1), (1, 0), (1, 1), (0, 2), (2, 0), (1, 2), (2, 1)]
 UNROLL = 28
 CHUNK = 84
-FORCE_UNROLL = 28
+FORCE_UNROLL = 42
 KEEP = 5
 SELF = 8
 VMEM = 63 * 2**20
@@ -51,11 +51,11 @@
     return [u * columns + v for u, v in neighbour_steps()]
 
 
-def meet():
+def greet():
     barrier = pltpu.get_barrier_semaphore()
     for o in offsets():
         pl.semaphore_signal(barrier, inc=1, device_id=place(o), device_id_type=MESH)
-    pl.semaphore_wait(barrier, NEIGH)
+    return barrier
 
 
 def start_all(src, dst, send_sem, recv_sem, sign):
@@ -149,6 +149,7 @@
                  ghost, idx, hot_o, pos, smooth, self_sum, gdens, buf, C, AF, BF, GB, T, RT, R, RS, MM, hot_a, hot_b,
                  gpress, ret, gacc, racc,
                  send_sem, recv_sem, own_sem, tile_sem, s1, r1, s2, r2, s3, r3):
+    barrier = greet()
     left = R.at[pl.ds(0, 8 * NB)]
     press, pbuf = smooth, gdens
     hot = R.at[pl.ds(8 * NB, 2 * W128)]
@@ -172,7 +173,7 @@
 
     hot[pl.ds(GHOSTS, 2 * W128 - GHOSTS), :] = jnp.zeros((2 * W128 - GHOSTS, W128), f32)
     lax.fori_loop(0, NEIGH, gather, 0)
-    meet()
+    pl.semaphore_wait(barrier, NEIGH)
     copies = start_all(buf, ghost, send_sem, recv_sem, 1)
 
     npairs = pairs.shape[2]
@@ -298,21 +299,21 @@
     lax.fori_loop(0, chunks, chunk_body, 0)
 
     dot = functools.partial(jnp.dot, preferred_element_type=f32)
+    part = R[pl.ds(0, slots, stride=8), :]
+    for i in range(1, 8):
+        part = part + R[pl.ds(i, slots, stride=8), :]
+    hi, lo = hilo(part)
+    away = dot(hot_b[NB:], hi) + dot(hot_b[NB:], lo)
+    for n in range(NEIGH):
+        gdens[n] = away[n * SLOTS:(n + 1) * SLOTS] * (4.0 * NORM) / ghost[n, 3]
+    copies = start_all(gdens, ret, s1, r1, -1)
     rows = jnp.zeros((W128, NB), f32)
     for w in range(RT.shape[0]):
         for p in hilo(RT[w]):
             rows = rows + lax.dot_general(p, hot_a[:, w * W128:(w + 1) * W128], (((1,), (1,)), ((), ())),
                                           preferred_element_type=f32)
-    part = R[pl.ds(0, slots, stride=8), :]
-    for i in range(1, 8):
-        part = part + R[pl.ds(i, slots, stride=8), :]
-    hi, lo = hilo(part)
-    sums = dot(hot_b[...], hi) + dot(hot_b[...], lo)
-    for n in range(NEIGH):
-        at = NB + n * SLOTS
-        gdens[n] = sums[at:at + SLOTS] * (4.0 * NORM) / ghost[n, 3]
-    copies = start_all(gdens, ret, s1, r1, -1)
-    mine = (sums[:NB] + rows.T + self_sum[...]) * (4.0 * NORM) / mass[...]
+    home = dot(hot_b[:NB], hi) + dot(hot_b[:NB], lo)
+    mine = (home + rows.T + self_sum[...]) * (4.0 * NORM) / mass[...]
 
     def weights(at, rows, x, y, z, m, p):
         k = inverse_cube_root(m)
@@ -417,17 +418,18 @@
     own_back.wait()
     lax.fori_loop(0, NB // 16, own_sums, 0)
 
-    A = []
-    for c in range(0, 8, 2):
-        total = []
-        for half, matrix in ((0, hot_a), (1, hot_b)):
-            v = [R[pl.ds(half * slots * 8 + c + i, slots, stride=8), :] for i in range(2)]
-            hi, lo = hilo(jnp.concatenate(v, 1))
-            total.append(dot(matrix[...], hi) + dot(matrix[...], lo))
-        own = total[1][:NB] + total[0]
-        for i in range(2):
-            at = slice(i * W128, (i + 1) * W128)
-            A.append((own[:, at] + RS[pl.ds(c + i, NB, stride=8), :], total[1][NB:, at]))
+    def block_sums(halves):
+        A = []
+        for c in range(0, 8, 2):
+            total = None
+            for half, matrix in halves:
+                v = [R[pl.ds(half * slots * 8 + c + i, slots, stride=8), :] for i in range(2)]
+                hi, lo = hilo(jnp.concatenate(v, 1))
+                term = dot(matrix, hi) + dot(matrix, lo)
+                total = term if total is None else total + term
+            A += [total[:, :W128], total[:, W128:]]
+        return A
+
     scale = -20.0 * NORM
 
     def final(p, m, spot, A):
@@ -436,12 +438,14 @@
         own = p * A[0] + A[4]
         return [(p * A[c + 1] + A[c + 5] - v * own) * (scale * (k2 * k2 * k)) for c, v in enumerate(spot)]
 
+    A = block_sums([(1, hot_b[NB:])])
     for n in range(NEIGH):
         r = slice(n * SLOTS, (n + 1) * SLOTS)
-        for c, v in enumerate(final(gpress[n], ghost[n, 3], [ghost[n, c] for c in range(3)], [x[1][r] for x in A])):
+        for c, v in enumerate(final(gpress[n], ghost[n, 3], [ghost[n, c] for c in range(3)], [x[r] for x in A])):
             gacc[n, c] = v
     copies = start_all(gacc, racc, s3, r3, -1)
-    mine = final(press[...], mass[...], [pos[c] for c in range(3)], [x[0] for x in A])
+    A = [x + RS[pl.ds(c, NB, stride=8), :] for c, x in enumerate(block_sums([(0, hot_a[...]), (1, hot_b[:NB])]))]
+    mine = final(press[...], mass[...], [pos[c] for c in range(3)], A)
     for copy in copies:
         copy.wait()
     for c in range(3):
@@ -480,11 +484,23 @@
         name="whole")(send_list, pair_count, pair_list, pair_list, pos, mass, smoothing, energy, level)
 
 
+def leave_kernel(dens, acc, dens_o, acc_o):
+    dens_o[...] = dens[...]
+    acc_o[...] = acc[...]
+
+
+def leave(dens, acc):
+    return pl.pallas_call(
+        leave_kernel, out_shape=[sds(dens.shape, f32), sds(acc.shape, f32)], in_specs=[V, V], out_specs=[V, V],
+        compiler_params=pltpu.CompilerParams(vmem_limit_bytes=VMEM), name="leave")(dens, acc)
+
+
 def per_device(positions, masses, smoothing, energy, level_ids, send_list, pair_list, pair_count):
     mass = masses.reshape(NB, W128)
     density, accel, _, _ = run_whole(
         send_list.transpose(0, 2, 1), pair_count, pair_list, positions.reshape(3, NB, W128).transpose(1, 0, 2), mass,
         smoothing.reshape(NB, W128), energy.reshape(NB, W128), level_ids.reshape(1, NB))
+    density, accel = leave(density, accel)
     return density.reshape(NB * W128), accel.transpose(1, 0, 2).reshape(3, NB * W128)
 
 

time: 100 us -> 95.7 us (0.957)
  local copies, waits for them, and re-layouts: 3.17 us -> 0 us
  Pallas kernels: 95.6 us -> 94.2 us
    unnamed x2 -> x0, local copies, waits for them, and re-layouts: 3.17 us -> none
    pallas_call x1, Pallas kernels: 95.6 us -> 92.5 us  [run_whole(): pl.pallas_call(whole_kernel, out_shape=[sds((NB, W128), f32), sds((NB, 3,...]
    pallas_call x0 -> x1, Pallas kernels: none -> 1.76 us  [leave(): pl.pallas_call(leave_kernel, out_shape=[sds(dens.shape, f32), sds(acc.sha...]
where the time goes in v7:
time: 95.7 us; the launch traced here: 95.5 us
  Pallas kernels  94.2 us (98%)
  between operations  1.29 us (1%)
    pallas_call x1, Pallas kernels, run_whole(): pl.pallas_call(whole_kernel, out_shape=[sds((NB, W128), f32), sds((NB, 3,...  92.5 us

profile of v7, /device:TPU:1, one launch (start us, length us, event | category | flops | bytes accessed | tf_op | source)
XLA Modules:
  0.0 95.5 jit_solution(453851409047917398)
XLA Ops:
  1.3 92.5 %whole.1 = (f32[128,128]{1,0:T(8,128)}, f32[128,3,128]{2,1,0:T(4,128)}, f32[128,128,128]{2,1,0:T(8,128)}, f32[252,128,128]{2,1,0:T(8,128)}) custom-call(s32[1,8,20]{2,1,0:T(8,128)} %bitcast.16, s32[1]{0:T(128)S(6)} %copy.10.count, s32[1,2,672]{2,1,0:T(2,128)} %pairs.1, s32[1,2,672]{2,1,0:T(2,128)} %pairs.1, f32[128,3,128]{2,1,0:T(4,128)} %bitcast.12, ...), custom_call_target="tpu_custom_call" | custom-call | tf_op jit(solution)/shard_map/whole/pallas_call | solution.py:470
  93.8 1.8 %leave.1 = (f32[128,128]{1,0:T(8,128)}, f32[128,3,128]{2,1,0:T(4,128)}) custom-call(f32[128,128]{1,0:T(8,128)} %get-tuple-element.6.dens, f32[128,3,128]{2,1,0:T(4,128)} %get-tuple-element.7.acc), custom_call_target="tpu_custom_call" | custom-call | tf_op jit(solution)/shard_map/leave/pallas_call | solution.py:493

commit v8 on v7

--- a/solution.py
+++ b/solution.py
@@ -25,7 +25,7 @@
 CHUNK = 84
 FORCE_UNROLL = 42
 KEEP = 5
-SELF = 8
+SELF = 16
 VMEM = 63 * 2**20
 
 
@@ -254,9 +254,9 @@
         at = pl.ds(c * CHUNK, CHUNK)
         return pltpu.make_async_copy(T.at[at], tiles_h.at[at], tile_sem.at[c])
 
-    def spill_back(c):
-        at = pl.ds(c * CHUNK, CHUNK)
-        return pltpu.make_async_copy(tiles_h.at[at], T.at[at], tile_sem.at[chunks - KEEP + c])
+    def spill_back(c, place):
+        return pltpu.make_async_copy(tiles_h.at[pl.ds(c * CHUNK, CHUNK)], T.at[pl.ds(place * CHUNK, CHUNK)],
+                                     tile_sem.at[chunks - KEEP + c])
 
     def pair_body(c, u, _):
         k0 = c * CHUNK + u * UNROLL
@@ -369,11 +369,11 @@
             put(RS, a, v)
         return 0
 
-    def pair_sums(do_a, do_b, c, u, _):
+    def pair_sums(do_a, do_b, c, place, u, _):
         out = []
         for j in range(FORCE_UNROLL):
             k = c * CHUNK + u * FORCE_UNROLL + j
-            hi, lo = hilo(T[lax.rem(c, KEEP) * CHUNK + u * FORCE_UNROLL + j])
+            hi, lo = hilo(T[place * CHUNK + u * FORCE_UNROLL + j])
             if do_b:
                 out.append((slots + k, to_b(k, hi, lo)))
             if do_a:
@@ -382,11 +382,11 @@
             put(R, k, v)
         return 0
 
-    def chunk_sums(do_a, do_b, c):
-        lax.fori_loop(0, CHUNK // FORCE_UNROLL, functools.partial(pair_sums, do_a, do_b, c), 0)
+    def chunk_sums(do_a, do_b, c, place):
+        lax.fori_loop(0, CHUNK // FORCE_UNROLL, functools.partial(pair_sums, do_a, do_b, c, place), 0)
 
     def early(do_a, do_b, i, _):
-        chunk_sums(do_a, do_b, KEEP + i)
+        chunk_sums(do_a, do_b, KEEP + i, i)
         return 0
 
     lax.fori_loop(0, chunks - KEEP, functools.partial(early, False, True), 0)
@@ -395,28 +395,26 @@
     for n in range(NEIGH):
         weights(NB + n * SLOTS, SLOTS, *[ghost[n, c] for c in range(4)], gpress[n])
     lax.fori_loop(NB // 4, EXT // 4, columns, 0)
-    lax.fori_loop(0, chunks - KEEP, functools.partial(early, True, False), 0)
-    for c in range(chunks - KEEP):
-        spill_back(c).start()
     own_back = pltpu.make_async_copy(own_h, T.at[pl.ds(own_first, NB)], tile_sem.at[2 * (chunks - KEEP)])
 
     def rest(i, _):
         c = lax.rem(chunks - KEEP + i, KEEP)
-
-        @pl.when(i == 2)
-        def _():
-            own_back.start()
+        place = KEEP - 2 + lax.rem(i, 2)
 
         @pl.when(i >= 2)
         def _():
-            spill_back(c).wait()
-
-        chunk_sums(True, True, c)
+            spill_back(c, place).wait()
+
+        chunk_sums(True, True, c, place)
+
+        @pl.when(i + 2 < KEEP)
+        def _():
+            spill_back(lax.rem(chunks - KEEP + i + 2, KEEP), place).start()
+
         return 0
 
     lax.fori_loop(0, KEEP, rest, 0)
-    own_back.wait()
-    lax.fori_loop(0, NB // 16, own_sums, 0)
+    own_back.start()
 
     def block_sums(halves):
         A = []
@@ -444,6 +442,9 @@
         for c, v in enumerate(final(gpress[n], ghost[n, 3], [ghost[n, c] for c in range(3)], [x[r] for x in A])):
             gacc[n, c] = v
     copies = start_all(gacc, racc, s3, r3, -1)
+    lax.fori_loop(0, chunks - KEEP, functools.partial(early, True, False), 0)
+    own_back.wait()
+    lax.fori_loop(0, NB // 16, own_sums, 0)
     A = [x + RS[pl.ds(c, NB, stride=8), :] for c, x in enumerate(block_sums([(0, hot_a[...]), (1, hot_b[:NB])]))]
     mine = final(press[...], mass[...], [pos[c] for c in range(3)], A)
     for copy in copies:

time: 95.7 us -> 93.1 us (0.973)
  Pallas kernels: 94.2 us -> 91.4 us
    pallas_call x1, Pallas kernels: 92.5 us -> 89.6 us  [run_whole(): pl.pallas_call(whole_kernel, out_shape=[sds((NB, W128), f32), sds((NB, 3,...]
where the time goes in v8:
time: 93.1 us; the launch traced here: 92.6 us
  Pallas kernels  91.4 us (98%)
  between operations  1.29 us (1%)
    pallas_call x1, Pallas kernels, run_whole(): pl.pallas_call(whole_kernel, out_shape=[sds((NB, W128), f32), sds((NB, 3,...  89.6 us

profile of v8, /device:TPU:1, one launch (start us, length us, event | category | flops | bytes accessed | tf_op | source)
XLA Modules:
  0.0 92.6 jit_solution(13637464058840219296)
XLA Ops:
  1.3 89.6 %whole.1 = (f32[128,128]{1,0:T(8,128)}, f32[128,3,128]{2,1,0:T(4,128)}, f32[128,128,128]{2,1,0:T(8,128)}, f32[252,128,128]{2,1,0:T(8,128)}) custom-call(s32[1,8,20]{2,1,0:T(8,128)} %bitcast.16, s32[1]{0:T(128)S(6)} %copy.10.count, s32[1,2,672]{2,1,0:T(2,128)} %pairs.1, s32[1,2,672]{2,1,0:T(2,128)} %pairs.1, f32[128,3,128]{2,1,0:T(4,128)} %bitcast.12, ...), custom_call_target="tpu_custom_call" | custom-call | tf_op jit(solution)/shard_map/whole/pallas_call | solution.py:471
  90.9 1.8 %leave.1 = (f32[128,128]{1,0:T(8,128)}, f32[128,3,128]{2,1,0:T(4,128)}) custom-call(f32[128,128]{1,0:T(8,128)} %get-tuple-element.6.dens, f32[128,3,128]{2,1,0:T(4,128)} %get-tuple-element.7.acc), custom_call_target="tpu_custom_call" | custom-call | tf_op jit(solution)/shard_map/leave/pallas_call | solution.py:494

commit v9 on v8

--- a/solution.py
+++ b/solution.py
@@ -21,7 +21,7 @@
 GHOSTS = NEIGH * SLOTS
 EXT = NB + GHOSTS
 CHUNKS = [(0, 0), (0, 1), (1, 0), (1, 1), (0, 2), (2, 0), (1, 2), (2, 1)]
-UNROLL = 28
+UNROLL = 42
 CHUNK = 84
 FORCE_UNROLL = 42
 KEEP = 5

time: 93.1 us -> 92.4 us (level)
  no operation moved by 1% of the time
where the time goes in v9:
time: 92.4 us; the launch traced here: 91.9 us
  Pallas kernels  90.6 us (98%)
  between operations  1.29 us (1%)
    pallas_call x1, Pallas kernels, run_whole(): pl.pallas_call(whole_kernel, out_shape=[sds((NB, W128), f32), sds((NB, 3,...  88.9 us

profile of v9, /device:TPU:1, one launch (start us, length us, event | category | flops | bytes accessed | tf_op | source)
XLA Modules:
  0.0 91.9 jit_solution(4607849145344914644)
XLA Ops:
  1.3 88.9 %whole.1 = (f32[128,128]{1,0:T(8,128)}, f32[128,3,128]{2,1,0:T(4,128)}, f32[128,128,128]{2,1,0:T(8,128)}, f32[252,128,128]{2,1,0:T(8,128)}) custom-call(s32[1,8,20]{2,1,0:T(8,128)} %bitcast.16, s32[1]{0:T(128)S(6)} %copy.10.count, s32[1,2,672]{2,1,0:T(2,128)} %pairs.1, s32[1,2,672]{2,1,0:T(2,128)} %pairs.1, f32[128,3,128]{2,1,0:T(4,128)} %bitcast.12, ...), custom_call_target="tpu_custom_call" | custom-call | tf_op jit(solution)/shard_map/whole/pallas_call | solution.py:471
  90.2 1.8 %leave.1 = (f32[128,128]{1,0:T(8,128)}, f32[128,3,128]{2,1,0:T(4,128)}) custom-call(f32[128,128]{1,0:T(8,128)} %get-tuple-element.6.dens, f32[128,3,128]{2,1,0:T(4,128)} %get-tuple-element.7.acc), custom_call_target="tpu_custom_call" | custom-call | tf_op jit(solution)/shard_map/leave/pallas_call | solution.py:494
